TPU v7x, 128 devices: a whole 4x4x4 slice. The times are simulated.
128 devices in a mesh: genome: 32 (over y, x, core), cell: 4 (over z).
Axes of the slice: x: 4, y: 4, z: 4, core: 2. Of those that a mesh axis runs over, the one named last changes fastest.
Arguments:
- inputs: bfloat16 [4, 65536, 512], P('cell', 'genome'), may hold values from -6 to 6
- weight: bfloat16 [512, 512], replicated, may hold values from -0.25 to 0.25
- band_vals: bfloat16 [4, 512, 9, 128, 128], P('cell', 'genome'), may hold values from -1 to 1, as said below
- far_rows: int32 [4, 32, 32, 2], P('cell', 'genome'), may hold values from 0 to 15
- far_send: int32 [4, 32, 32, 2], P('cell', 'genome'), may hold values from 0 to 15
- far_count: int32 [4, 32, 32], P('cell', 'genome'), may hold values from 0 to 2, as said below
- far_vals: bfloat16 [4, 32, 32, 2, 128, 128], P('cell', 'genome'), may hold values from -0.25 to 0.25
- grad_out: bfloat16 [4, 65536, 512], P('cell', 'genome'), may hold values from -6 to 6
Outputs:
- output: bfloat16 [4, 65536, 512], P('cell', 'genome')
- grad_in: bfloat16 [4, 65536, 512], P('cell', 'genome')
- grad_weight: float32 [512, 512], replicated
Inputs may be any that keep to these rules, and one draw needn't show every extreme that they name: The band is symmetric: band_vals[c, i, d] is the transpose of band_vals[c, i + d - 4, 8 - d] wherever both blocks lie in the grid. `far_count`: slots used from one sender to one receiver; for each cell type some receiving device gets 2 from every sender.
All inputs are finite; a program needn't handle non-finite values.
Results may differ from a plain program's by a relative error of at most 0.007.
Values may be sent and summed in bfloat16 or wider, within the bound.
No kernel may reach another device: no remote copies, remote signals or barrier semaphores. Data moves between devices by JAX's collectives and lax.ppermute only.
A program may use at most 192 MiB of HBM per device.

v0:
```python
import math

import jax
import jax.numpy as jnp
from jax import lax
from jax.sharding import PartitionSpec as P

BLK = 128
BAND = 4


band_gain = 3.0


def padded_2(block, sides, width):
    for axis, dim in sides:
        count = lax.axis_size(axis)
        forward = [(i, i + 1) for i in range(count - 1)]
        backward = [(target, source) for source, target in forward]
        low = lax.ppermute(
            lax.slice_in_dim(block, block.shape[dim] - width, None, axis=dim), axis, forward
        )
        high = lax.ppermute(lax.slice_in_dim(block, 0, width, axis=dim), axis, backward)
        block = jnp.concatenate([low, block, high], axis=dim)
    return block


def band_sum(padded, band_vals):
    block_count = band_vals.shape[1]
    cells_here = padded.shape[0]
    blocks = padded.reshape(cells_here, -1, BLK, padded.shape[-1])
    summed = None
    for offset in range(2 * BAND + 1):
        window = blocks[:, offset : offset + block_count]
        single_term = jnp.einsum(
            "cnij,cnjf->cnif", band_vals[:, :, offset], window, preferred_element_type=jnp.float32
        )
        summed = single_term if summed is None else summed + single_term
    factor = band_gain / math.sqrt((2 * BAND + 1) * BLK)
    return (factor * summed).reshape(cells_here, block_count * BLK, -1)


def project(values, weight):
    return jnp.einsum("crf,fg->crg", values, weight, preferred_element_type=jnp.float32).astype(
        jnp.bfloat16
    )


def pick_rows(blocks, chosen):
    return blocks[chosen]


def on_device(inputs, weight, band_vals, far_rows, far_send, far_count, far_vals, grad_out):
    cells_here = inputs.shape[0]
    rows_here = inputs.shape[1]
    feature_count = inputs.shape[2]
    block_count = band_vals.shape[1]
    rim_rows = BAND * BLK
    projected = project(inputs, weight)
    padded_z = padded_2(projected, (("genome", 1),), rim_rows)
    band_part = band_sum(padded_z, band_vals)
    send_index = far_send[:, 0]
    slot_ids = jnp.arange(far_send.shape[-1], dtype=jnp.int32)
    live = slot_ids[None, None, :] < far_count[:, 0][:, :, None]
    zero_value = jnp.zeros((), jnp.bfloat16)
    blocks = projected.reshape(cells_here, block_count, BLK, feature_count)
    chosen = jax.vmap(pick_rows)(blocks, send_index)
    arrived = lax.all_to_all(
        jnp.where(live[..., None, None], chosen, zero_value),
        "genome",
        split_axis=1,
        concat_axis=1,
        tiled=True,
    )
    loop_vals = far_vals[:, 0]
    loop_terms = jnp.einsum(
        "cpsij,cpsjf->cpsif", loop_vals, arrived, preferred_element_type=jnp.float32
    )
    block_ids = jnp.arange(block_count, dtype=jnp.int32)
    target_index = far_rows[:, 0]
    target_hot = (target_index[..., None] == block_ids).astype(jnp.float32)
    far_part = jnp.einsum(
        "cpsn,cpsif->cnif", target_hot, loop_terms, precision=lax.Precision.HIGHEST
    )
    preact = band_part + far_part.reshape(cells_here, rows_here, feature_count)
    sigma = jax.nn.sigmoid(preact)
    output = (preact * sigma).astype(jnp.bfloat16)
    slope = sigma * (1.0 + preact * (1.0 - sigma))
    grads = (grad_out.astype(jnp.float32) * slope).astype(jnp.bfloat16)
    padded_g = padded_2(grads, (("genome", 1),), rim_rows)
    back_band = band_sum(padded_g, band_vals)
    grad_blocks = grads.reshape(cells_here, block_count, BLK, feature_count)
    target_grads = jax.vmap(pick_rows)(grad_blocks, target_index)
    returned = jnp.einsum(
        "cpsji,cpsjf->cpsif", loop_vals, target_grads, preferred_element_type=jnp.float32
    ).astype(jnp.bfloat16)
    came_back = lax.all_to_all(returned, "genome", split_axis=1, concat_axis=1, tiled=True)
    masked = jnp.where(live[..., None, None], came_back, zero_value)
    source_hot = (send_index[..., None] == block_ids).astype(jnp.bfloat16)
    back_far = jnp.einsum(
        "cpsn,cpsif->cnif", source_hot, masked, preferred_element_type=jnp.float32
    )
    grad_z = (back_band + back_far.reshape(cells_here, rows_here, feature_count)).astype(
        jnp.bfloat16
    )
    grad_in = jnp.einsum("crg,fg->crf", grad_z, weight, preferred_element_type=jnp.float32).astype(
        jnp.bfloat16
    )
    local_weight = jnp.einsum("crf,crg->fg", inputs, grad_z, preferred_element_type=jnp.float32)
    grad_weight = lax.psum(local_weight, ("genome", "cell"))
    return (output, grad_in, grad_weight)


def solution(mesh):
    return jax.shard_map(
        on_device,
        mesh=mesh,
        in_specs=(
            P("cell", "genome", None),
            P(),
            P("cell", "genome", None, None, None),
            P("cell", "genome", None, None),
            P("cell", "genome", None, None),
            P("cell", "genome", None),
            P("cell", "genome", None, None, None, None),
            P("cell", "genome", None),
        ),
        out_specs=(P("cell", "genome", None), P("cell", "genome", None), P()),
        check_vma=False,
    )
```

profile of v0, /device:TPU:1, one launch (start us, length us, event | category | flops | bytes accessed | tf_op | source)
XLA Modules:
  0.0 609.4 jit_solution(17560293576824832732)
XLA Ops:
  8.2 4.3 convolution_convert_fusion.1
  12.5 7.2 %gather_fusion = bf16[64,128,512]{2,1,0:T(8,128)(2,1)} fusion(bf16[1,16,128,512]{3,2,1,0:T(8,128)(2,1)} %bitcast.243, s32[64]{0:T(128)S(1)} %reshape.459), kind=kCustom, calls=%fused_computation | custom fusion | bytes 16777728 | tf_op jit(solution)/shard_map/vmap()/gather | solution.py:50
  19.7 11.3 %copy.83 = bf16[64,128,512]{1,2,0:T(8,128)(2,1)} copy(bf16[64,128,512]{2,1,0:T(8,128)(2,1)} %gather_fusion) | data formatting | bytes 16777216 | tf_op jit(solution)/shard_map/vmap()/gather | solution.py:50
  31.1 7.3 %broadcast_select_fusion = bf16[1,32,2,128,512]{3,4,2,0,1:T(8,128)(2,1)} fusion(bf16[1,32,2,128,512]{3,4,2,0,1:T(8,128)(2,1)} %bitcast.246, pred[32,2]{1,0:T(8,128)(4,1)S(1)} %iota_compare_fusion.1), kind=kLoop, calls=%fused_computation.6 | loop fusion | flops 4194304 | bytes 16777280 | tf_op jit(solution)/shard_map/jit(_where)/select_n | solution.py:69
  38.4 8.8 %all-to-all-start = ((bf16[1,32,2,128,512]{3,4,2,0,1:T(8,128)(2,1)}), bf16[1,32,2,128,512]{3,4,2,0,1:T(8,128)(2,1)}, u32[]{:S(2)}, u32[]{:S(2)}) async-start(bf16[1,32,2,128,512]{3,4,2,0,1:T(8,128)(2,1)} %broadcast_select_fusion), calls=%async_computation | async-start | bytes 16777216 | tf_op jit(solution)/shard_map/all_to_all | solution.py:68
  51.7 3.5 collective-permute-start
  55.5 96.8 %collective-permute-done.1 = bf16[1,512,512]{2,1,0:T(8,128)(2,1)S(1)} collective-permute-done((bf16[1,512,512]{2,1,0:T(8,128)(2,1)}, bf16[1,512,512]{2,1,0:T(8,128)(2,1)S(1)}, u32[]{:S(2)}, u32[]{:S(2)}) %collective-permute-start.1) | collective-permute-done | bytes 524320 | tf_op jit(solution)/shard_map/ppermute | solution.py:23
  154.1 4.1 fusion.19
  158.2 2.8 fusion.20
  169.0 2.7 fusion.24
  171.7 2.7 fusion.26
  177.1 11.5 %convolution_bitcast_fusion = f32[32,2,128,512]{2,3,1,0:T(8,128)} fusion(bf16[1,32,2,128,512]{3,4,2,0,1:T(8,128)(2,1)} %all-to-all-done, bf16[1,1,32,2,128,128]{5,4,3,2,1,0:T(8,128)(2,1)S(1)} %copy-done), kind=kOutput, calls=%fused_computation.2 | convolution fusion | flops 1073741824 | bytes 27262976 | tf_op jit(solution)/shard_map/cpsij,cpsjf->cpsif/dot_general | solution.py:76
  188.5 20.0 %copy.84 = f32[32,2,128,512]{3,0,1,2:T(8,128)} copy(f32[32,2,128,512]{2,3,1,0:T(8,128)} %convolution_bitcast_fusion) | data formatting | bytes 33554432 | tf_op jit(solution)/shard_map/cpsij,cpsjf->cpsif/dot_general | solution.py:76
  208.5 12.0 %convolution_bitcast_fusion.1 = f32[16,128,512]{2,0,1:T(8,128)} fusion(f32[32,2,128,512]{3,0,1,2:T(8,128)} %copy.84, s32[32,2]{0,1:T(2,128)S(1)} %bitcast.256), kind=kOutput, calls=%fused_computation.26 | convolution fusion | flops 805307392 | bytes 20971776 | tf_op jit(solution)/shard_map/cpsn,cpsif->cnif/dot_general | solution.py:82
  220.5 16.6 %bitcast_add_fusion.1 = f32[16,128,512]{2,1,0:T(8,128)} fusion(f32[16,128,512]{2,0,1:T(8,128)} %convolution_bitcast_fusion.1, f32[16,512,128]{1,2,0:T(8,128)} %fusion.19, f32[16,512,128]{1,2,0:T(8,128)} %fusion.20, f32[16,512,128]{1,2,0:T(8,128)} %fusion.21, f32[16,512,128]{1,2,0:T(8,128)} %fusion.22, f32[16,512,128]{1,2,0:T(8,128)} %fusion.23, ...), kind=kOutput, calls=%fused_computation.20 | convolution fusion | flops 278921216 | bytes 44564480 | tf_op jit(solution)/shard_map/cnij,cnjf->cnif/dot_general | solution.py:35
  237.1 4.8 fusion.9
  241.8 7.2 %gather_fusion.1 = bf16[64,128,512]{2,1,0:T(8,128)(2,1)} fusion(bf16[1,16,128,512]{3,2,1,0:T(8,128)(2,1)} %bitcast.242, s32[64]{0:T(128)S(1)} %reshape.467), kind=kCustom, calls=%fused_computation.1 | custom fusion | bytes 16777728 | tf_op jit(solution)/shard_map/vmap()/gather | solution.py:50
  249.0 9.0 %convert_bitcast_fusion = bf16[1,32,2,128,512]{3,4,2,0,1:T(8,128)(2,1)} fusion(bf16[32,2,128,512]{3,2,1,0:T(8,128)(2,1)} %bitcast.247, bf16[1,1,32,2,128,128]{5,4,3,2,1,0:T(8,128)(2,1)S(1)} %copy-done), kind=kOutput, calls=%fused_computation.5 | convolution fusion | flops 1077936128 | bytes 18874368 | tf_op jit(solution)/shard_map/cpsji,cpsjf->cpsif/dot_general | solution.py:94
  258.1 10.0 %all-to-all-start.1 = ((bf16[1,32,2,128,512]{3,4,2,0,1:T(8,128)(2,1)}), bf16[1,32,2,128,512]{3,4,2,0,1:T(8,128)(2,1)}, u32[]{:S(2)}, u32[]{:S(2)}) async-start(bf16[1,32,2,128,512]{3,4,2,0,1:T(8,128)(2,1)} %convert_bitcast_fusion), calls=%async_computation.1 | async-start | bytes 16777216 | tf_op jit(solution)/shard_map/all_to_all | solution.py:97
  271.7 3.3 collective-permute-start.2
  275.0 98.2 %collective-permute-done.3 = bf16[1,512,512]{2,1,0:T(8,128)(2,1)S(1)} collective-permute-done((bf16[1,512,512]{2,1,0:T(8,128)(2,1)S(1)}, bf16[1,512,512]{2,1,0:T(8,128)(2,1)S(1)}, u32[]{:S(2)}, u32[]{:S(2)}) %collective-permute-start.3) | collective-permute-done | bytes 524320 | tf_op jit(solution)/shard_map/ppermute | solution.py:23
  375.1 4.3 fusion.11
  379.4 3.8 fusion.12
  388.5 2.8 fusion.15
  391.3 2.7 fusion.16
  399.2 7.2 %select_bitcast_fusion = bf16[32,2,128,512]{2,3,1,0:T(8,128)(2,1)} fusion(bf16[1,32,2,128,512]{3,4,2,0,1:T(8,128)(2,1)} %all-to-all-done.1, pred[32,2]{1,0:T(8,128)(4,1)S(1)} %iota_compare_fusion.1), kind=kLoop, calls=%fused_computation.4 | loop fusion | flops 4194304 | bytes 16777280 | tf_op jit(solution)/shard_map/reshape.86
  406.5 14.7 %copy.92 = bf16[32,2,128,512]{3,0,1,2:T(8,128)(2,1)} copy(bf16[32,2,128,512]{2,3,1,0:T(8,128)(2,1)} %select_bitcast_fusion) | data formatting | bytes 16777216 | tf_op jit(solution)/shard_map/reshape.86
  421.2 6.8 %convolution_bitcast_fusion.2 = f32[16,128,512]{2,0,1:T(8,128)} fusion(bf16[32,2,128,512]{3,0,1,2:T(8,128)(2,1)} %copy.92, s32[32,2]{0,1:T(2,128)S(1)} %bitcast.255), kind=kOutput, calls=%fused_computation.27 | convolution fusion | flops 134218752 | bytes 12583168 | tf_op jit(solution)/shard_map/cpsn,cpsif->cnif/dot_general | solution.py:100
  428.0 15.5 %fusion.1 = bf16[16,128,512]{2,1,0:T(8,128)(2,1)} fusion(f32[16,128,512]{2,0,1:T(8,128)} %convolution_bitcast_fusion.2, f32[16,512,128]{1,2,0:T(8,128)} %fusion.11, f32[16,512,128]{1,2,0:T(8,128)} %fusion.12, f32[16,512,128]{1,2,0:T(8,128)} %fusion.13, f32[16,512,128]{1,2,0:T(8,128)} %fusion.14, f32[16,512,128]{1,2,0:T(8,128)} %fusion.15, ...), kind=kOutput, calls=%fused_computation.8 | convolution fusion | flops 279969792 | bytes 42467328 | tf_op jit(solution)/shard_map/cnij,cnjf->cnif/dot_general | solution.py:35
  443.5 4.5 fusion.32
  448.0 4.2 fusion.10
  452.2 147.8 %all-reduce.2.cloned.1.call-done = f32[512,512]{0,1:T(8,128)} async-done(((f32[512,512]{0,1:T(8,128)}), f32[512,512]{0,1:T(8,128)}) %all-reduce.2.cloned.1.call-update) | async-done | bytes 1048592 | tf_op jit(solution)/shard_map/psum | solution.py:110
  (62 shorter events, 36.8 us)
Async XLA Ops:
  7.2 169.9 %copy-start = (bf16[1,1,32,2,128,128]{5,4,3,2,1,0:T(8,128)(2,1)S(1)}, bf16[1,1,32,2,128,128]{5,4,3,2,1,0:T(8,128)(2,1)}, u32[]{:S(2)}) copy-start(bf16[1,1,32,2,128,128]{5,4,3,2,1,0:T(8,128)(2,1)} %param.14) | copy-start | bytes 6291460
  19.7 11.3 %copy-start.8 = (s32[1,1,32]{2,1,0:T(1,128)S(1)}, s32[1,1,32]{2,1,0:T(1,128)}, u32[]{:S(2)}) copy-start(s32[1,1,32]{2,1,0:T(1,128)} %param.13) | copy-start | bytes 388
  38.4 16.9 %copy-start.7 = (s32[1,1,32,2]{2,3,1,0:T(2,128)S(1)}, s32[1,1,32,2]{2,3,1,0:T(2,128)}, u32[]{:S(2)}) copy-start(s32[1,1,32,2]{2,3,1,0:T(2,128)} %param.11) | copy-start | bytes 772
  38.4 138.7 %all-to-all-start = ((bf16[1,32,2,128,512]{3,4,2,0,1:T(8,128)(2,1)}), bf16[1,32,2,128,512]{3,4,2,0,1:T(8,128)(2,1)}, u32[]{:S(2)}, u32[]{:S(2)}) async-start(bf16[1,32,2,128,512]{3,4,2,0,1:T(8,128)(2,1)} %broadcast_select_fusion), calls=%async_computation | async-start | bytes 16777216 | tf_op jit(solution)/shard_map/all_to_all | solution.py:68
  47.2 111.1 %slice-start = ((s8[4718592]{0:T(1024)(128)(4,1)}), s8[524288]{0:T(1024)(128)(4,1)S(1)}, s32[]{:S(2)}) async-start(s8[4718592]{0:T(1024)(128)(4,1)} %bitcast.248), calls=%async_computation.3 | async-start | bytes 1048576
  49.5 102.8 %collective-permute-start.1 = (bf16[1,512,512]{2,1,0:T(8,128)(2,1)}, bf16[1,512,512]{2,1,0:T(8,128)(2,1)S(1)}, u32[]{:S(2)}, u32[]{:S(2)}) collective-permute-start(bf16[1,512,512]{2,1,0:T(8,128)(2,1)} %get-tuple-element.20), channel_id=1, source_target_pairs={{4,0},{8,4},{12,8},{16,12},{20,16},{24,20},{28,24},{32,28},{36,32}... | collective-permute-start | bytes 1572872 | tf_op jit(solution)/shard_map/ppermute | solution.py:23
  51.7 100.6 %collective-permute-start = (bf16[1,512,512]{2,1,0:T(8,128)(2,1)}, bf16[1,512,512]{2,1,0:T(8,128)(2,1)}, u32[]{:S(2)}, u32[]{:S(2)}) collective-permute-start(bf16[1,512,512]{2,1,0:T(8,128)(2,1)} %get-tuple-element.19), channel_id=1, source_target_pairs={{0,4},{4,8},{8,12},{12,16},{16,20},{20,24},{24,28},{28,32},{32,36}... | collective-permute-start | bytes 1572872 | tf_op jit(solution)/shard_map/ppermute | solution.py:20
  55.5 102.8 %slice-start.1 = ((s8[4718592]{0:T(1024)(128)(4,1)}), s8[4194304]{0:T(1024)(128)(4,1)S(1)}, s32[]{:S(2)}) async-start(s8[4718592]{0:T(1024)(128)(4,1)} %bitcast.248), calls=%async_computation.4 | async-start | bytes 8388608
  154.1 20.3 %copy-start.1 = (bf16[1,3072,512]{2,1,0:T(8,128)(2,1)}, bf16[1,3072,512]{2,1,0:T(8,128)(2,1)S(1)}, u32[]{:S(2)}) copy-start(bf16[1,3072,512]{2,1,0:T(8,128)(2,1)S(1)} %pad_maximum_fusion) | copy-start | bytes 9437188
  208.5 12.0 %copy-start.2 = (bf16[1,3072,512]{2,1,0:T(8,128)(2,1)S(1)}, bf16[1,3072,512]{2,1,0:T(8,128)(2,1)}, u32[]{:S(2)}) copy-start(bf16[1,3072,512]{2,1,0:T(8,128)(2,1)} %copy-done.1) | copy-start | bytes 9437188
  220.5 16.6 %copy-start.5 = (bf16[1,2048,512]{2,1,0:T(8,128)(2,1)S(1)}, bf16[1,2048,512]{2,1,0:T(8,128)(2,1)}, u32[]{:S(2)}) copy-start(bf16[1,2048,512]{2,1,0:T(8,128)(2,1)} %param.15) | copy-start | bytes 6291460
  258.1 141.2 %all-to-all-start.1 = ((bf16[1,32,2,128,512]{3,4,2,0,1:T(8,128)(2,1)}), bf16[1,32,2,128,512]{3,4,2,0,1:T(8,128)(2,1)}, u32[]{:S(2)}, u32[]{:S(2)}) async-start(bf16[1,32,2,128,512]{3,4,2,0,1:T(8,128)(2,1)} %convert_bitcast_fusion), calls=%async_computation.1 | async-start | bytes 16777216 | tf_op jit(solution)/shard_map/all_to_all | solution.py:97
  268.1 332.0 %all-reduce.2.cloned.1.call-start = ((), (), s32[]{:S(2)}) async-start(), calls=%async_computation.2 | async-start | bytes 2097152 | tf_op jit(solution)/shard_map/psum | solution.py:110
  269.4 103.8 %collective-permute-start.3 = (bf16[1,512,512]{2,1,0:T(8,128)(2,1)S(1)}, bf16[1,512,512]{2,1,0:T(8,128)(2,1)S(1)}, u32[]{:S(2)}, u32[]{:S(2)}) collective-permute-start(bf16[1,512,512]{2,1,0:T(8,128)(2,1)S(1)} %get-tuple-element.18), channel_id=1, source_target_pairs={{4,0},{8,4},{12,8},{16,12},{20,16},{24,20},{28,24},{32,28},{36,32}... | collective-permute-start | bytes 1572872 | tf_op jit(solution)/shard_map/ppermute | solution.py:23
  271.7 101.6 %collective-permute-start.2 = (bf16[1,512,512]{2,1,0:T(8,128)(2,1)S(1)}, bf16[1,512,512]{2,1,0:T(8,128)(2,1)S(1)}, u32[]{:S(2)}, u32[]{:S(2)}) collective-permute-start(bf16[1,512,512]{2,1,0:T(8,128)(2,1)S(1)} %get-tuple-element.17), channel_id=1, source_target_pairs={{0,4},{4,8},{8,12},{12,16},{16,20},{20,24},{24,28},{28,32},{32,36}... | collective-permute-start | bytes 1572872 | tf_op jit(solution)/shard_map/ppermute | solution.py:20
  373.2 9.9 %slice-start.2 = ((s8[4718592]{0:T(1024)(128)(4,1)}), s8[4194304]{0:T(1024)(128)(4,1)S(1)}, s32[]{:S(2)}) async-start(s8[4718592]{0:T(1024)(128)(4,1)} %bitcast.250), calls=%async_computation.5 | async-start | bytes 8388608
  375.1 21.5 %copy-start.3 = (bf16[1,3072,512]{2,1,0:T(8,128)(2,1)}, bf16[1,3072,512]{2,1,0:T(8,128)(2,1)S(1)}, u32[]{:S(2)}) copy-start(bf16[1,3072,512]{2,1,0:T(8,128)(2,1)S(1)} %pad_maximum_fusion.1) | copy-start | bytes 9437188
  375.1 8.1 %slice-start.3 = ((s8[4718592]{0:T(1024)(128)(4,1)}), s8[524288]{0:T(1024)(128)(4,1)S(1)}, s32[]{:S(2)}) async-start(s8[4718592]{0:T(1024)(128)(4,1)} %bitcast.250), calls=%async_computation.6 | async-start | bytes 1048576
  406.5 14.7 %copy-start.6 = (s32[1,1,32,2]{2,3,1,0:T(2,128)S(1)}, s32[1,1,32,2]{2,3,1,0:T(2,128)}, u32[]{:S(2)}) copy-start(s32[1,1,32,2]{2,3,1,0:T(2,128)} %param.12) | copy-start | bytes 772
  421.2 6.8 %copy-start.4 = (bf16[1,3072,512]{2,1,0:T(8,128)(2,1)S(1)}, bf16[1,3072,512]{2,1,0:T(8,128)(2,1)}, u32[]{:S(2)}) copy-start(bf16[1,3072,512]{2,1,0:T(8,128)(2,1)} %copy-done.3) | copy-start | bytes 9437188
  443.5 4.6 copy-start.9
Sparse Core Ops, SparseCore 0:
  448.1 151.8 all-reduce.1
where the time goes:
time: 611 us; the launch traced here: 609 us
  waiting for transfers between devices  343 us (56%)
  matrix products  131 us (21%)
  local copies, waits for them, and re-layouts  67 us (11%)
  starting transfers between devices  30.2 us (5%)
  other arithmetic  23.8 us (4%)
  between operations  14.2 us (2%)
    ppermute x2, waiting for transfers between devices, padded_2(): lax.ppermute(lax.slice_in_dim(block, 0, width, axis=dim), axis, backward)  195 us
    psum x1, waiting for transfers between devices, on_device(): grad_weight = lax.psum(local_weight, ('genome', 'cell'))  148 us
    dot_general x18, matrix products, band_sum(): jnp.einsum('cnij,cnjf->cnif', band_vals[:, :, offset], window, preferred_...  79.1 us
    gather x9, local copies, waits for them, and re-layouts, pick_rows(): return blocks[chosen]  26.2 us
    dot_general x1, local copies, waits for them, and re-layouts, on_device(): jnp.einsum('cpsij,cpsjf->cpsif', loop_vals, arrived, preferred_element_ty...  20 us
    another operation x1, local copies, waits for them, and re-layouts  14.7 us
  transfers between devices with their start and end apart: 7, of which 3 were waited for; matrix products, arithmetic and copies ran while one was open for 10% of the time, Pallas kernels for 0%

commit v1 on v0

v1 whole, which is shorter than its diff:
```python
import functools
import math

import jax
import jax.numpy as jnp
from jax import lax
from jax.experimental import pallas as pl
from jax.experimental.pallas import tpu as pltpu
from jax.sharding import PartitionSpec as P

BLK = 128
BAND = 4
WIDTH = 2 * BAND + 1
SLOTS_STEP = 4
ROWS_STEP = 512
VMEM_LIMIT = 48 * 1024 * 1024

band_gain = 3.0
FACTOR = band_gain / math.sqrt(WIDTH * BLK)


def dot(a, b):
    return jnp.dot(a, b, preferred_element_type=jnp.float32)


def dot_ta(a, b):
    return lax.dot_general(a, b, (((0,), (0,)), ((), ())), preferred_element_type=jnp.float32)


def dot_tb(a, b):
    return lax.dot_general(a, b, (((1,), (1,)), ((), ())), preferred_element_type=jnp.float32)


def params():
    return pltpu.CompilerParams(
        dimension_semantics=("arbitrary",), vmem_limit_bytes=VMEM_LIMIT
    )


def block_rows(index):
    return pl.ds(pl.multiple_of(index * BLK, BLK), BLK)


def gather_kernel(cap, index_ref, count_ref, x_ref, out_ref):
    step = pl.program_id(0)
    for j in range(SLOTS_STEP):
        slot = step * SLOTS_STEP + j
        live = lax.rem(slot, cap) < count_ref[slot // cap]

        @pl.when(live)
        def _():
            out_ref[pl.ds(j * BLK, BLK), :] = x_ref[block_rows(index_ref[slot]), :]

        @pl.when(jnp.logical_not(live))
        def _():
            out_ref[pl.ds(j * BLK, BLK), :] = jnp.zeros((BLK, out_ref.shape[1]), out_ref.dtype)


def gather_blocks(x, index, count, cap):
    slots = index.shape[0]
    features = x.shape[1]
    return pl.pallas_call(
        functools.partial(gather_kernel, cap),
        grid_spec=pltpu.PrefetchScalarGridSpec(
            num_scalar_prefetch=2,
            grid=(slots // SLOTS_STEP,),
            in_specs=[pl.BlockSpec(x.shape, lambda i, *_: (0, 0))],
            out_specs=pl.BlockSpec((SLOTS_STEP * BLK, features), lambda i, *_: (i, 0)),
        ),
        out_shape=jax.ShapeDtypeStruct((slots * BLK, features), x.dtype),
        compiler_params=params(),
        cost_estimate=pl.CostEstimate(
            flops=0, bytes_accessed=2 * (x.size + slots * BLK * features), transcendentals=0
        ),
        name="gather_blocks",
    )(index, count, x)


def band_kernel(low_ref, v_ref, high_ref, band_ref, out_ref, padded):
    step = pl.program_id(0)
    rim = low_ref.shape[0]
    rows = v_ref.shape[0]

    @pl.when(step == 0)
    def _():
        padded[pl.ds(0, rim), :] = low_ref[...]
        padded[pl.ds(rim, rows), :] = v_ref[...]
        padded[pl.ds(rim + rows, rim), :] = high_ref[...]

    left = jnp.concatenate([band_ref[0, d] for d in range(WIDTH)], axis=1)
    window = padded[pl.ds(pl.multiple_of(step * BLK, BLK), WIDTH * BLK), :]
    out_ref[...] = FACTOR * dot(left, window)


def band_sum(low, v, high, band):
    rows, features = v.shape
    blocks = band.shape[0]
    whole = lambda a: pl.BlockSpec(a.shape, lambda i: (0, 0))
    return pl.pallas_call(
        band_kernel,
        grid=(blocks,),
        in_specs=[
            whole(low),
            whole(v),
            whole(high),
            pl.BlockSpec((1, WIDTH, BLK, BLK), lambda i: (i, 0, 0, 0)),
        ],
        out_specs=pl.BlockSpec((BLK, features), lambda i: (i, 0)),
        out_shape=jax.ShapeDtypeStruct((rows, features), jnp.float32),
        scratch_shapes=[pltpu.VMEM((rows + 2 * low.shape[0], features), v.dtype)],
        compiler_params=params(),
        cost_estimate=pl.CostEstimate(
            flops=2 * band.size * features,
            bytes_accessed=2 * band.size + 6 * v.size,
            transcendentals=0,
        ),
        name="band_sum",
    )(low, v, high, band)


def middle_kernel(
    loop_steps,
    target_ref,
    arrived_ref,
    vals_ref,
    band_ref,
    weight_ref,
    grad_ref,
    output_ref,
    grads_ref,
    y_ref,
    total,
):
    step = pl.program_id(0)

    @pl.when(step == 0)
    def _():
        total[...] = jnp.zeros_like(total)

    @pl.when(step < loop_steps)
    def _():
        for j in range(SLOTS_STEP):
            rows = block_rows(target_ref[step * SLOTS_STEP + j])
            total[rows, :] += dot(vals_ref[j], arrived_ref[pl.ds(j * BLK, BLK), :])

    @pl.when(step >= loop_steps)
    def _():
        rows = pl.ds(pl.multiple_of((step - loop_steps) * ROWS_STEP, ROWS_STEP), ROWS_STEP)
        y = (total[rows, :] + band_ref[...]).astype(jnp.bfloat16)
        y_ref[...] = y
        preact = dot(y, weight_ref[...])
        sigma = jax.nn.sigmoid(preact)
        output_ref[...] = (preact * sigma).astype(jnp.bfloat16)
        slope = sigma * (1.0 + preact * (1.0 - sigma))
        grads_ref[...] = (grad_ref[...].astype(jnp.float32) * slope).astype(jnp.bfloat16)


def middle(target, arrived, vals, band, weight, grad_out):
    rows, features = grad_out.shape
    slots = target.shape[0]
    loop_steps = slots // SLOTS_STEP
    row_steps = rows // ROWS_STEP
    by_loop = lambda i, *_: (jnp.minimum(i, loop_steps - 1), 0)
    by_row = lambda i, *_: (jnp.maximum(i - loop_steps, 0), 0)
    row_spec = pl.BlockSpec((ROWS_STEP, features), by_row)
    out = jax.ShapeDtypeStruct((rows, features), jnp.bfloat16)
    return pl.pallas_call(
        functools.partial(middle_kernel, loop_steps),
        grid_spec=pltpu.PrefetchScalarGridSpec(
            num_scalar_prefetch=1,
            grid=(loop_steps + row_steps,),
            in_specs=[
                pl.BlockSpec((SLOTS_STEP * BLK, features), by_loop),
                pl.BlockSpec(
                    (SLOTS_STEP, BLK, BLK), lambda i, *_: (jnp.minimum(i, loop_steps - 1), 0, 0)
                ),
                row_spec,
                pl.BlockSpec(weight.shape, lambda i, *_: (0, 0)),
                row_spec,
            ],
            out_specs=[row_spec] * 3,
            scratch_shapes=[pltpu.VMEM((rows, features), jnp.float32)],
        ),
        out_shape=[out] * 3,
        compiler_params=params(),
        cost_estimate=pl.CostEstimate(
            flops=2 * (vals.size + rows * features) * features,
            bytes_accessed=2 * (arrived.size + vals.size + 6 * rows * features),
            transcendentals=rows * features,
        ),
        name="middle",
    )(target, arrived, vals, band, weight, grad_out)


def back_kernel(target_ref, grads_ref, vals_ref, out_ref):
    step = pl.program_id(0)
    for j in range(SLOTS_STEP):
        rows = block_rows(target_ref[step * SLOTS_STEP + j])
        term = dot_ta(vals_ref[j], grads_ref[rows, :])
        out_ref[pl.ds(j * BLK, BLK), :] = term.astype(jnp.bfloat16)


def back_terms(target, grads, vals):
    slots = target.shape[0]
    features = grads.shape[1]
    return pl.pallas_call(
        back_kernel,
        grid_spec=pltpu.PrefetchScalarGridSpec(
            num_scalar_prefetch=1,
            grid=(slots // SLOTS_STEP,),
            in_specs=[
                pl.BlockSpec(grads.shape, lambda i, *_: (0, 0)),
                pl.BlockSpec((SLOTS_STEP, BLK, BLK), lambda i, *_: (i, 0, 0)),
            ],
            out_specs=pl.BlockSpec((SLOTS_STEP * BLK, features), lambda i, *_: (i, 0)),
        ),
        out_shape=jax.ShapeDtypeStruct((slots * BLK, features), jnp.bfloat16),
        compiler_params=params(),
        cost_estimate=pl.CostEstimate(
            flops=2 * vals.size * features,
            bytes_accessed=2 * (slots * BLK * features + vals.size + grads.size),
            transcendentals=0,
        ),
        name="back_terms",
    )(target, grads, vals)


def tail_kernel(
    cap, loop_steps, index_ref, count_ref, back_ref, band_ref, weight_ref, out_ref, total
):
    step = pl.program_id(0)

    @pl.when(step == 0)
    def _():
        total[...] = jnp.zeros_like(total)

    @pl.when(step < loop_steps)
    def _():
        for j in range(SLOTS_STEP):
            slot = step * SLOTS_STEP + j

            @pl.when(lax.rem(slot, cap) < count_ref[slot // cap])
            def _():
                rows = block_rows(index_ref[slot])
                total[rows, :] += back_ref[pl.ds(j * BLK, BLK), :].astype(jnp.float32)

    @pl.when(step >= loop_steps)
    def _():
        rows = pl.ds(pl.multiple_of((step - loop_steps) * ROWS_STEP, ROWS_STEP), ROWS_STEP)
        grad_z = (total[rows, :] + band_ref[...]).astype(jnp.bfloat16)
        out_ref[...] = dot_tb(grad_z, weight_ref[...]).astype(jnp.bfloat16)


def tail(index, count, cap, back, band, weight):
    rows, features = band.shape
    slots = index.shape[0]
    loop_steps = slots // SLOTS_STEP
    row_steps = rows // ROWS_STEP
    row_spec = pl.BlockSpec(
        (ROWS_STEP, features), lambda i, *_: (jnp.maximum(i - loop_steps, 0), 0)
    )
    return pl.pallas_call(
        functools.partial(tail_kernel, cap, loop_steps),
        grid_spec=pltpu.PrefetchScalarGridSpec(
            num_scalar_prefetch=2,
            grid=(loop_steps + row_steps,),
            in_specs=[
                pl.BlockSpec(
                    (SLOTS_STEP * BLK, features),
                    lambda i, *_: (jnp.minimum(i, loop_steps - 1), 0),
                ),
                row_spec,
                pl.BlockSpec(weight.shape, lambda i, *_: (0, 0)),
            ],
            out_specs=row_spec,
            scratch_shapes=[pltpu.VMEM((rows, features), jnp.float32)],
        ),
        out_shape=jax.ShapeDtypeStruct((rows, features), jnp.bfloat16),
        compiler_params=params(),
        cost_estimate=pl.CostEstimate(
            flops=2 * band.size * features,
            bytes_accessed=2 * back.size + 6 * band.size,
            transcendentals=0,
        ),
        name="tail",
    )(index, count, back, band, weight)


def rims(v):
    count = lax.axis_size("genome")
    width = BAND * BLK
    forward = [(i, i + 1) for i in range(count - 1)]
    backward = [(target, source) for source, target in forward]
    low = lax.ppermute(v[v.shape[0] - width :], "genome", forward)
    high = lax.ppermute(v[:width], "genome", backward)
    return low, high


def exchange(blocks):
    peers = lax.axis_size("genome")
    cut = blocks.reshape(peers, -1, blocks.shape[-1])
    return lax.all_to_all(cut, "genome", 0, 0, tiled=True).reshape(blocks.shape)


def moved(index, kind, s):
    core, x, y = index & 1, (index >> 1) & 3, index >> 3
    if kind == "core":
        core = core ^ 1
    elif kind == "x":
        x = (x + s) & 3
    else:
        y = (y + s) & 3
    return y * 8 + x * 2 + core


def shift(v, kind, s):
    if kind == "cell":
        return lax.ppermute(v, "cell", [(i, (i + s) & 3) for i in range(4)])
    return lax.ppermute(v, "genome", [(i, moved(i, kind, s)) for i in range(32)])


def sum_everywhere(v):
    rows, columns = v.shape
    core = lax.axis_index("genome") & 1
    cell = lax.axis_index("cell")
    halves = v.reshape(2, rows // 2, columns)
    mine = lax.dynamic_index_in_dim(halves, core, 0, keepdims=False)
    other = lax.dynamic_index_in_dim(halves, 1 - core, 0, keepdims=False)
    mine = mine + shift(other, "core", 1)
    parts = mine.reshape(4, rows // 8, columns)
    total = lax.dynamic_index_in_dim(parts, cell, 0, keepdims=False)
    for s in (1, 2, 3):
        part = lax.dynamic_index_in_dim(parts, (cell + s) & 3, 0, keepdims=False)
        total = total + shift(part, "cell", s)
    for kind in ("y", "x"):
        total = total + sum(shift(total, kind, s) for s in (1, 2, 3))
    around = jnp.stack([total] + [shift(total, "cell", s) for s in (1, 2, 3)])
    full = jnp.take(around, (cell - jnp.arange(4)) & 3, axis=0).reshape(rows // 2, columns)
    other = shift(full, "core", 1)
    first = jnp.where(core == 0, full, other)
    second = jnp.where(core == 0, other, full)
    return jnp.concatenate([first, second])


def on_device(inputs, weight, band_vals, far_rows, far_send, far_count, far_vals, grad_out):
    x = inputs[0]
    band = band_vals[0]
    cap = far_send.shape[-1]
    send_index = far_send.reshape(-1)
    target_index = far_rows.reshape(-1)
    count = far_count.reshape(-1)
    vals = far_vals.reshape(-1, BLK, BLK)

    low, high = rims(x)
    arrived = exchange(gather_blocks(x, send_index, count, cap))
    band_part = band_sum(low, x, high, band)
    output, grads, y = middle(target_index, arrived, vals, band_part, weight, grad_out[0])
    low, high = rims(grads)
    came_back = exchange(back_terms(target_index, grads, vals))
    back_band = band_sum(low, grads, high, band)
    grad_weight = sum_everywhere(dot_ta(y, grads))
    grad_in = tail(send_index, count, cap, came_back, back_band, weight)
    return (output[None], grad_in[None], grad_weight)


def solution(mesh):
    return jax.shard_map(
        on_device,
        mesh=mesh,
        in_specs=(
            P("cell", "genome", None),
            P(),
            P("cell", "genome", None, None, None),
            P("cell", "genome", None, None),
            P("cell", "genome", None, None),
            P("cell", "genome", None),
            P("cell", "genome", None, None, None, None),
            P("cell", "genome", None),
        ),
        out_specs=(P("cell", "genome", None), P("cell", "genome", None), P()),
        check_vma=False,
    )
```

time: 611 us -> 348 us (0.57)
  waiting for transfers between devices: 343 us -> 192 us
  matrix products: 131 us -> 2.88 us
  Pallas kernels: 0 us -> 75.8 us
  local copies, waits for them, and re-layouts: 67 us -> 13.7 us
  starting transfers between devices: 30.2 us -> 50.5 us
  other arithmetic: 23.8 us -> 7.39 us
  between operations: 14.2 us -> 0.82 us
    psum x1 -> x0, waiting for transfers between devices: 148 us -> none  [on_device(): grad_weight = lax.psum(local_weight, ('genome', 'cell'))]
    dot_general x25 -> x1, matrix products: 131 us -> 2.88 us  [dot_ta(): lax.dot_general(a, b, (((0,), (0,)), ((), ())), preferred_element_type=jn...]
    pallas_call x0 -> x6, Pallas kernels: none -> 75.8 us  [the longest x2 26.1 us: band_sum(): pl.pallas_call(band_kernel, grid=(blocks,), in_specs=[whole(low), whole(v...]
    gather x9 -> x1, local copies, waits for them, and re-layouts: 26.2 us -> 2.43 us  [sum_everywhere(): jnp.take(around, cell - jnp.arange(4) & 3, axis=0)]
    ppermute x4 -> x18, starting transfers between devices: 11.3 us -> 31.7 us  [the longest x8 11.9 us: shift(): lax.ppermute(v, 'genome', [(i, moved(i, kind, s)) for i in range(32)])]
    dot_general x1 -> x0, local copies, waits for them, and re-layouts: 20 us -> none  [on_device(): jnp.einsum('cpsij,cpsjf->cpsif', loop_vals, arrived, preferred_element_ty...]
    another operation x1 -> x0, local copies, waits for them, and re-layouts: 14.7 us -> none
    another operation x1, other arithmetic: 7.23 us -> 0.82 us  [sum_everywhere(): around = jnp.stack([total] + [shift(total, 'cell', s) for s in (1, 2, 3)])]
  transfers between devices with their start and end apart: 7 -> 20, of which waited for: 3 -> 10; matrix products, arithmetic and copies ran while one was open for 10% -> 5% of each run, Pallas kernels for 0% -> 8%
where the time goes in v1:
time: 348 us; the launch traced here: 343 us
  waiting for transfers between devices  192 us (55%)
  Pallas kernels  75.8 us (22%)
  starting transfers between devices  50.5 us (15%)
  local copies, waits for them, and re-layouts  13.7 us (4%)
  other arithmetic  7.39 us (2%)
    ppermute x2, waiting for transfers between devices, rims(): low = lax.ppermute(v[v.shape[0] - width:], 'genome', forward)  93.5 us
    ppermute x8, waiting for transfers between devices, shift(): lax.ppermute(v, 'genome', [(i, moved(i, kind, s)) for i in range(32)])  83.4 us
    pallas_call x2, Pallas kernels, band_sum(): pl.pallas_call(band_kernel, grid=(blocks,), in_specs=[whole(low), whole(v...  26.1 us
    all_to_all x2, starting transfers between devices, exchange(): return lax.all_to_all(cut, 'genome', 0, 0, tiled=True).reshape(blocks.shape)  18.8 us
    pallas_call x1, Pallas kernels, middle(): pl.pallas_call(functools.partial(middle_kernel, loop_steps), grid_spec=pl...  18.5 us
    pallas_call x1, Pallas kernels, tail(): pl.pallas_call(functools.partial(tail_kernel, cap, loop_steps), grid_spec...  13.5 us
    ppermute x8, starting transfers between devices, shift(): lax.ppermute(v, 'genome', [(i, moved(i, kind, s)) for i in range(32)])  11.9 us
    ppermute x6, waiting for transfers between devices, shift(): return lax.ppermute(v, 'cell', [(i, i + s & 3) for i in range(4)])  10.1 us
  transfers between devices with their start and end apart: 20, of which 10 were waited for; matrix products, arithmetic and copies ran while one was open for 5% of the time, Pallas kernels for 8%

profile of v1, /device:TPU:1, one launch (start us, length us, event | category | flops | bytes accessed | tf_op | source)
XLA Modules:
  0.0 343.0 jit_solution(10157852215963096642)
XLA Ops:
  1.5 1.6 copy-done.1
  3.7 7.8 %gather_blocks.1 = bf16[8192,512]{1,0:T(8,128)(2,1)} custom-call(s32[64]{0:T(128)S(1)} %reshape.66.index_ref, s32[32]{0:T(128)S(1)} %bitcast.53, bf16[2048,512]{1,0:T(8,128)(2,1)S(1)} %bitcast.49), custom_call_target="tpu_custom_call" | custom-call | bytes 10485760 | tf_op jit(solution)/shard_map/gather_blocks/pallas_call | solution.py:62
  11.5 8.8 %all-to-all-start = ((bf16[32,256,512]{2,1,0:T(8,128)(2,1)}), bf16[32,256,512]{2,1,0:T(8,128)(2,1)}, u32[]{:S(2)}, u32[]{:S(2)}) async-start(bf16[32,256,512]{2,1,0:T(8,128)(2,1)} %bitcast.56), calls=%async_computation | async-start | bytes 16777216 | tf_op jit(solution)/shard_map/all_to_all | solution.py:302
  21.4 3.5 %collective-permute-start = (bf16[512,512]{1,0:T(8,128)(2,1)}, bf16[512,512]{1,0:T(8,128)(2,1)S(1)}, u32[]{:S(2)}, u32[]{:S(2)}) collective-permute-start(bf16[512,512]{1,0:T(8,128)(2,1)} %get-tuple-element.12), channel_id=1, source_target_pairs={{0,4},{4,8},{8,12},{12,16},{16,20},{20,24},{24,28},{28,32},{32,36}... | collective-permute-start | bytes 1572872 | tf_op jit(solution)/shard_map/ppermute | solution.py:294
  24.9 1.9 collective-permute-start.1
  27.1 93.5 %collective-permute-done.low_ref = bf16[512,512]{1,0:T(8,128)(2,1)S(1)} collective-permute-done((bf16[512,512]{1,0:T(8,128)(2,1)}, bf16[512,512]{1,0:T(8,128)(2,1)S(1)}, u32[]{:S(2)}, u32[]{:S(2)}) %collective-permute-start) | collective-permute-done | bytes 524320 | tf_op jit(solution)/shard_map/ppermute | solution.py:294
  120.6 4.9 %collective-permute-done.1.high_ref = bf16[512,512]{1,0:T(8,128)(2,1)S(1)} collective-permute-done((bf16[512,512]{1,0:T(8,128)(2,1)}, bf16[512,512]{1,0:T(8,128)(2,1)S(1)}, u32[]{:S(2)}, u32[]{:S(2)}) %collective-permute-start.1) | collective-permute-done | bytes 524320 | tf_op jit(solution)/shard_map/ppermute | solution.py:295
  127.3 13.0 %band_sum.2.band_ref = f32[2048,512]{1,0:T(8,128)} custom-call(bf16[512,512]{1,0:T(8,128)(2,1)S(1)} %collective-permute-done.low_ref, bf16[2048,512]{1,0:T(8,128)(2,1)S(1)} %bitcast.50, bf16[512,512]{1,0:T(8,128)(2,1)S(1)} %copy-done.6, bf16[16,9,128,128]{3,2,1,0:T(8,128)(2,1)} %bitcast.57), custom_call_target="tpu_custom_call" | custom-call | flops 2415919104 | bytes 11010048 | tf_op jit(solution)/shard_map/band_sum/pallas_call | solution.py:99
  140.2 18.5 %middle.1 = (bf16[2048,512]{1,0:T(8,128)(2,1)}, bf16[2048,512]{1,0:T(8,128)(2,1)S(1)}, bf16[2048,512]{1,0:T(8,128)(2,1)S(1)}) custom-call(s32[64]{0:T(128)S(1)} %reshape.65.target_ref, bf16[8192,512]{1,0:T(8,128)(2,1)} %bitcast.3.arrived_ref, bf16[64,128,128]{2,1,0:T(8,128)(2,1)} %bitcast.51, f32[2048,512]{1,0:T(8,128)} %band_sum.2.band_ref, ...), custom_call_target="tpu_custom_call" | custom-call | flops 2147483648 | bytes 23068672 | tf_op jit(solution)/shard_map/middle/pallas_call | solution.py:167
  158.8 9.9 %back_terms.1 = bf16[8192,512]{1,0:T(8,128)(2,1)} custom-call(s32[64]{0:T(128)S(1)} %reshape.65.target_ref, bf16[2048,512]{1,0:T(8,128)(2,1)S(1)} %get-tuple-element.7.grads_ref.v_ref, bf16[64,128,128]{2,1,0:T(8,128)(2,1)S(1)} %bitcast.52), custom_call_target="tpu_custom_call" | custom-call | flops 1073741824 | bytes 12582912 | tf_op jit(solution)/shard_map/back_terms/pallas_call | solution.py:206
  168.7 10.0 %all-to-all-start.1 = ((bf16[32,256,512]{2,1,0:T(8,128)(2,1)}), bf16[32,256,512]{2,1,0:T(8,128)(2,1)}, u32[]{:S(2)}, u32[]{:S(2)}) async-start(bf16[32,256,512]{2,1,0:T(8,128)(2,1)} %bitcast.55), calls=%async_computation.1 | async-start | bytes 16777216 | tf_op jit(solution)/shard_map/all_to_all | solution.py:302
  178.7 2.9 fusion.4
  183.0 1.7 collective-permute-done.4
  184.7 1.3 bitcast_add_fusion
  186.7 3.7 %collective-permute-start.7 = (f32[64,512]{1,0:T(8,128)}, f32[64,512]{1,0:T(8,128)S(1)}, u32[]{:S(2)}, u32[]{:S(2)}) collective-permute-start(f32[64,512]{1,0:T(8,128)} %get-tuple-element.16), channel_id=1, source_target_pairs={{0,3},{1,0},{2,1},{3,2},{4,7},{5,4},{6,5},{7,6},{8,11},{9,8},{10,9... | collective-permute-start | bytes 393224 | tf_op jit(solution)/shard_map/ppermute | solution.py:318
  191.1 5.3 %collective-permute-done.7 = f32[64,512]{1,0:T(8,128)S(1)} collective-permute-done((f32[64,512]{1,0:T(8,128)}, f32[64,512]{1,0:T(8,128)S(1)}, u32[]{:S(2)}, u32[]{:S(2)}) %collective-permute-start.7) | collective-permute-done | bytes 131104 | tf_op jit(solution)/shard_map/ppermute | solution.py:318
  196.6 3.1 collective-permute-done.5
  200.7 2.7 collective-permute-start.10
  203.4 1.7 collective-permute-start.9
  205.1 74.6 %collective-permute-done.10 = f32[64,512]{1,0:T(8,128)S(1)} collective-permute-done((f32[64,512]{1,0:T(8,128)S(1)}, f32[64,512]{1,0:T(8,128)S(1)}, u32[]{:S(2)}, u32[]{:S(2)}) %collective-permute-start.10) | collective-permute-done | bytes 131104 | tf_op jit(solution)/shard_map/ppermute | solution.py:319
  279.8 4.6 %collective-permute-start.13 = (f32[64,512]{1,0:T(8,128)S(1)}, f32[64,512]{1,0:T(8,128)S(1)}, u32[]{:S(2)}, u32[]{:S(2)}) collective-permute-start(f32[64,512]{1,0:T(8,128)S(1)} %add_add_fusion.1), channel_id=1, source_target_pairs={{0,24},{4,28},{8,0},{12,4},{16,8},{20,12},{24,16},{28,20},{32,56},... | collective-permute-start | bytes 393224 | tf_op jit(solution)/shard_map/ppermute | solution.py:319
  284.4 1.3 collective-permute-start.12
  286.4 6.6 %collective-permute-done.11 = f32[64,512]{1,0:T(8,128)S(1)} collective-permute-done((f32[64,512]{1,0:T(8,128)S(1)}, f32[64,512]{1,0:T(8,128)S(1)}, u32[]{:S(2)}, u32[]{:S(2)}) %collective-permute-start.11) | collective-permute-done | bytes 131104 | tf_op jit(solution)/shard_map/ppermute | solution.py:319
  293.0 3.8 %collective-permute-start.16 = (f32[64,512]{1,0:T(8,128)S(1)}, f32[64,512]{1,0:T(8,128)S(1)}, u32[]{:S(2)}, u32[]{:S(2)}) collective-permute-start(f32[64,512]{1,0:T(8,128)S(1)} %add_add_fusion), channel_id=1, source_target_pairs={{0,3},{1,0},{2,1},{3,2},{4,7},{5,4},{6,5},{7,6},{8,11},{9,8},{10,9... | collective-permute-start | bytes 393224 | tf_op jit(solution)/shard_map/ppermute | solution.py:318
  298.5 2.0 collective-permute-start.2
  300.5 3.5 %collective-permute-start.3 = (bf16[512,512]{1,0:T(8,128)(2,1)}, bf16[512,512]{1,0:T(8,128)(2,1)}, u32[]{:S(2)}, u32[]{:S(2)}) collective-permute-start(bf16[512,512]{1,0:T(8,128)(2,1)} %get-tuple-element.9), channel_id=1, source_target_pairs={{4,0},{8,4},{12,8},{16,12},{20,16},{24,20},{28,24},{32,28},{36,32}... | collective-permute-start | bytes 1572872 | tf_op jit(solution)/shard_map/ppermute | solution.py:295
  304.0 1.5 collective-permute-done.14
  306.3 2.4 gather_fusion
  308.8 2.0 bitcast_select_fusion
  311.9 13.1 %band_sum.3.band_ref = f32[2048,512]{1,0:T(8,128)} custom-call(bf16[512,512]{1,0:T(8,128)(2,1)S(1)} %collective-permute-done.2.low_ref, bf16[2048,512]{1,0:T(8,128)(2,1)S(1)} %get-tuple-element.7.grads_ref.v_ref, bf16[512,512]{1,0:T(8,128)(2,1)} %collective-permute-done.3.high_ref, bf16[16,9,128,128]{3,2,1,0:T(8,128)(2,1)} %bitcast.58), custom_call_target="tpu_custom_call" | custom-call | flops 2415919104 | bytes 11010048 | tf_op jit(solution)/shard_map/band_sum/pallas_call | solution.py:99
  327.3 2.2 copy-done
  329.5 13.5 %tail.1 = bf16[2048,512]{1,0:T(8,128)(2,1)} custom-call(s32[64]{0:T(128)S(1)} %reshape.66.index_ref, s32[32]{0:T(128)S(1)} %bitcast.54, bf16[8192,512]{1,0:T(8,128)(2,1)} %bitcast.11.back_ref, f32[2048,512]{1,0:T(8,128)S(1)} %copy-done, bf16[512,512]{1,0:T(8,128)(2,1)S(1)} %copy-done.4), custom_call_target="tpu_custom_call" | custom-call | flops 1073741824 | bytes 14680064 | tf_op jit(solution)/shard_map/tail/pallas_call | solution.py:262
  (63 shorter events, 15.4 us)
Async XLA Ops:
  1.5 1.6 copy-start.1
  11.5 8.8 %copy-start.2 = (bf16[1,2048,512]{2,1,0:T(8,128)(2,1)S(1)}, bf16[1,2048,512]{2,1,0:T(8,128)(2,1)}, u32[]{:S(2)}) copy-start(bf16[1,2048,512]{2,1,0:T(8,128)(2,1)} %param.8) | copy-start | bytes 6291460
  11.5 128.7 %all-to-all-start = ((bf16[32,256,512]{2,1,0:T(8,128)(2,1)}), bf16[32,256,512]{2,1,0:T(8,128)(2,1)}, u32[]{:S(2)}, u32[]{:S(2)}) async-start(bf16[32,256,512]{2,1,0:T(8,128)(2,1)} %bitcast.56), calls=%async_computation | async-start | bytes 16777216 | tf_op jit(solution)/shard_map/all_to_all | solution.py:302
  20.3 6.5 %copy-start.12 = (s32[1,1,32,2]{2,3,1,0:T(2,128)S(1)}, s32[1,1,32,2]{2,3,1,0:T(2,128)}, u32[]{:S(2)}) copy-start(s32[1,1,32,2]{2,3,1,0:T(2,128)} %param.11) | copy-start | bytes 772
  21.4 99.2 %collective-permute-start = (bf16[512,512]{1,0:T(8,128)(2,1)}, bf16[512,512]{1,0:T(8,128)(2,1)S(1)}, u32[]{:S(2)}, u32[]{:S(2)}) collective-permute-start(bf16[512,512]{1,0:T(8,128)(2,1)} %get-tuple-element.12), channel_id=1, source_target_pairs={{0,4},{4,8},{8,12},{12,16},{16,20},{20,24},{24,28},{28,32},{32,36}... | collective-permute-start | bytes 1572872 | tf_op jit(solution)/shard_map/ppermute | solution.py:294
  24.9 100.5 %collective-permute-start.1 = (bf16[512,512]{1,0:T(8,128)(2,1)}, bf16[512,512]{1,0:T(8,128)(2,1)S(1)}, u32[]{:S(2)}, u32[]{:S(2)}) collective-permute-start(bf16[512,512]{1,0:T(8,128)(2,1)} %get-tuple-element.11), channel_id=1, source_target_pairs={{4,0},{8,4},{12,8},{16,12},{20,16},{24,20},{28,24},{32,28},{36,32}... | collective-permute-start | bytes 1572872 | tf_op jit(solution)/shard_map/ppermute | solution.py:295
  125.4 0.8 copy-start.5
  126.2 1.0 copy-start.6
  127.3 13.0 %copy-start.4 = (bf16[512,512]{1,0:T(8,128)(2,1)S(1)}, bf16[512,512]{1,0:T(8,128)(2,1)}, u32[]{:S(2)}) copy-start(bf16[512,512]{1,0:T(8,128)(2,1)} %weight_ref.3) | copy-start | bytes 1572868
  140.2 18.5 %copy-start.3 = (bf16[1,1,32,2,128,128]{5,4,3,2,1,0:T(8,128)(2,1)S(1)}, bf16[1,1,32,2,128,128]{5,4,3,2,1,0:T(8,128)(2,1)}, u32[]{:S(2)}) copy-start(bf16[1,1,32,2,128,128]{5,4,3,2,1,0:T(8,128)(2,1)} %param.14) | copy-start | bytes 6291460
  158.8 9.9 %copy-start.9 = (bf16[2048,512]{1,0:T(8,128)(2,1)}, bf16[2048,512]{1,0:T(8,128)(2,1)S(1)}, u32[]{:S(2)}) copy-start(bf16[2048,512]{1,0:T(8,128)(2,1)S(1)} %get-tuple-element.8) | copy-start | bytes 6291460
  168.7 158.6 %all-to-all-start.1 = ((bf16[32,256,512]{2,1,0:T(8,128)(2,1)}), bf16[32,256,512]{2,1,0:T(8,128)(2,1)}, u32[]{:S(2)}, u32[]{:S(2)}) async-start(bf16[32,256,512]{2,1,0:T(8,128)(2,1)} %bitcast.55), calls=%async_computation.1 | async-start | bytes 16777216 | tf_op jit(solution)/shard_map/all_to_all | solution.py:302
  181.6 1.0 copy-start.11
  182.6 2.1 collective-permute-start.4
  186.7 9.7 %collective-permute-start.7 = (f32[64,512]{1,0:T(8,128)}, f32[64,512]{1,0:T(8,128)S(1)}, u32[]{:S(2)}, u32[]{:S(2)}) collective-permute-start(f32[64,512]{1,0:T(8,128)} %get-tuple-element.16), channel_id=1, source_target_pairs={{0,3},{1,0},{2,1},{3,2},{4,7},{5,4},{6,5},{7,6},{8,11},{9,8},{10,9... | collective-permute-start | bytes 393224 | tf_op jit(solution)/shard_map/ppermute | solution.py:318
  190.4 6.2 %collective-permute-start.6 = (f32[64,512]{1,0:T(8,128)S(1)}, f32[64,512]{1,0:T(8,128)}, u32[]{:S(2)}, u32[]{:S(2)}) collective-permute-start(f32[64,512]{1,0:T(8,128)S(1)} %get-tuple-element.17), channel_id=1, source_target_pairs={{0,2},{1,3},{2,0},{3,1},{4,6},{5,7},{6,4},{7,5},{8,10},{9,11},{10,... | collective-permute-start | bytes 393224 | tf_op jit(solution)/shard_map/ppermute | solution.py:318
  190.4 9.2 %collective-permute-start.5 = (f32[64,512]{1,0:T(8,128)S(1)}, f32[64,512]{1,0:T(8,128)}, u32[]{:S(2)}, u32[]{:S(2)}) collective-permute-start(f32[64,512]{1,0:T(8,128)S(1)} %get-tuple-element.15), channel_id=1, source_target_pairs={{0,1},{1,2},{2,3},{3,0},{4,5},{5,6},{6,7},{7,4},{8,9},{9,10},{10,1... | collective-permute-start | bytes 393224 | tf_op jit(solution)/shard_map/ppermute | solution.py:318
  200.7 79.0 %collective-permute-start.10 = (f32[64,512]{1,0:T(8,128)S(1)}, f32[64,512]{1,0:T(8,128)S(1)}, u32[]{:S(2)}, u32[]{:S(2)}) collective-permute-start(f32[64,512]{1,0:T(8,128)S(1)} %fusion.1), channel_id=1, source_target_pairs={{0,96},{4,100},{8,104},{12,108},{16,112},{20,116},{24,120},{28,124... | collective-permute-start | bytes 393224 | tf_op jit(solution)/shard_map/ppermute | solution.py:319
  203.4 76.3 %collective-permute-start.8 = (f32[64,512]{1,0:T(8,128)S(1)}, f32[64,512]{1,0:T(8,128)S(1)}, u32[]{:S(2)}, u32[]{:S(2)}) collective-permute-start(f32[64,512]{1,0:T(8,128)S(1)} %fusion.1), channel_id=1, source_target_pairs={{0,32},{4,36},{8,40},{12,44},{16,48},{20,52},{24,56},{28,60},{32,6... | collective-permute-start | bytes 393224 | tf_op jit(solution)/shard_map/ppermute | solution.py:319
  203.4 76.3 %collective-permute-start.9 = (f32[64,512]{1,0:T(8,128)S(1)}, f32[64,512]{1,0:T(8,128)S(1)}, u32[]{:S(2)}, u32[]{:S(2)}) collective-permute-start(f32[64,512]{1,0:T(8,128)S(1)} %fusion.1), channel_id=1, source_target_pairs={{0,64},{4,68},{8,72},{12,76},{16,80},{20,84},{24,88},{28,92},{32,9... | collective-permute-start | bytes 393224 | tf_op jit(solution)/shard_map/ppermute | solution.py:319
  279.8 6.6 %collective-permute-start.13 = (f32[64,512]{1,0:T(8,128)S(1)}, f32[64,512]{1,0:T(8,128)S(1)}, u32[]{:S(2)}, u32[]{:S(2)}) collective-permute-start(f32[64,512]{1,0:T(8,128)S(1)} %add_add_fusion.1), channel_id=1, source_target_pairs={{0,24},{4,28},{8,0},{12,4},{16,8},{20,12},{24,16},{28,20},{32,56},... | collective-permute-start | bytes 393224 | tf_op jit(solution)/shard_map/ppermute | solution.py:319
  284.4 8.5 %collective-permute-start.11 = (f32[64,512]{1,0:T(8,128)S(1)}, f32[64,512]{1,0:T(8,128)S(1)}, u32[]{:S(2)}, u32[]{:S(2)}) collective-permute-start(f32[64,512]{1,0:T(8,128)S(1)} %add_add_fusion.1), channel_id=1, source_target_pairs={{0,8},{4,12},{8,16},{12,20},{16,24},{20,28},{24,0},{28,4},{32,40},... | collective-permute-start | bytes 393224 | tf_op jit(solution)/shard_map/ppermute | solution.py:319
  284.4 8.5 %collective-permute-start.12 = (f32[64,512]{1,0:T(8,128)S(1)}, f32[64,512]{1,0:T(8,128)S(1)}, u32[]{:S(2)}, u32[]{:S(2)}) collective-permute-start(f32[64,512]{1,0:T(8,128)S(1)} %add_add_fusion.1), channel_id=1, source_target_pairs={{0,16},{4,20},{8,24},{12,28},{16,0},{20,4},{24,8},{28,12},{32,48},... | collective-permute-start | bytes 393224 | tf_op jit(solution)/shard_map/ppermute | solution.py:319
  293.0 11.0 %collective-permute-start.16 = (f32[64,512]{1,0:T(8,128)S(1)}, f32[64,512]{1,0:T(8,128)S(1)}, u32[]{:S(2)}, u32[]{:S(2)}) collective-permute-start(f32[64,512]{1,0:T(8,128)S(1)} %add_add_fusion), channel_id=1, source_target_pairs={{0,3},{1,0},{2,1},{3,2},{4,7},{5,4},{6,5},{7,6},{8,11},{9,8},{10,9... | collective-permute-start | bytes 393224 | tf_op jit(solution)/shard_map/ppermute | solution.py:318
  296.8 7.2 %collective-permute-start.15 = (f32[64,512]{1,0:T(8,128)S(1)}, f32[64,512]{1,0:T(8,128)S(1)}, u32[]{:S(2)}, u32[]{:S(2)}) collective-permute-start(f32[64,512]{1,0:T(8,128)S(1)} %add_add_fusion), channel_id=1, source_target_pairs={{0,2},{1,3},{2,0},{3,1},{4,6},{5,7},{6,4},{7,5},{8,10},{9,11},{10,... | collective-permute-start | bytes 393224 | tf_op jit(solution)/shard_map/ppermute | solution.py:318
  296.8 8.7 %collective-permute-start.14 = (f32[64,512]{1,0:T(8,128)S(1)}, f32[64,512]{1,0:T(8,128)S(1)}, u32[]{:S(2)}, u32[]{:S(2)}) collective-permute-start(f32[64,512]{1,0:T(8,128)S(1)} %add_add_fusion), channel_id=1, source_target_pairs={{0,1},{1,2},{2,3},{3,0},{4,5},{5,6},{6,7},{7,4},{8,9},{9,10},{10,1... | collective-permute-start | bytes 393224 | tf_op jit(solution)/shard_map/ppermute | solution.py:318
  298.5 13.4 %collective-permute-start.2 = (bf16[512,512]{1,0:T(8,128)(2,1)}, bf16[512,512]{1,0:T(8,128)(2,1)S(1)}, u32[]{:S(2)}, u32[]{:S(2)}) collective-permute-start(bf16[512,512]{1,0:T(8,128)(2,1)} %get-tuple-element.10), channel_id=1, source_target_pairs={{0,4},{4,8},{8,12},{12,16},{16,20},{20,24},{24,28},{28,32},{32,36}... | collective-permute-start | bytes 1572872 | tf_op jit(solution)/shard_map/ppermute | solution.py:294
  300.5 11.4 %collective-permute-start.3 = (bf16[512,512]{1,0:T(8,128)(2,1)}, bf16[512,512]{1,0:T(8,128)(2,1)}, u32[]{:S(2)}, u32[]{:S(2)}) collective-permute-start(bf16[512,512]{1,0:T(8,128)(2,1)} %get-tuple-element.9), channel_id=1, source_target_pairs={{4,0},{8,4},{12,8},{16,12},{20,16},{24,20},{28,24},{32,28},{36,32}... | collective-permute-start | bytes 1572872 | tf_op jit(solution)/shard_map/ppermute | solution.py:295
  310.7 14.4 %collective-permute-start.17 = (f32[256,512]{1,0:T(8,128)}, f32[256,512]{1,0:T(8,128)}, u32[]{:S(2)}, u32[]{:S(2)}) collective-permute-start(f32[256,512]{1,0:T(8,128)} %bitcast_select_fusion), channel_id=1, source_target_pairs={{0,4},{4,0},{8,12},{12,8},{16,20},{20,16},{24,28},{28,24},{32,36},... | collective-permute-start | bytes 1572872 | tf_op jit(solution)/shard_map/ppermute | solution.py:319
  311.9 13.1 %copy-start.10 = (f32[4,64,512]{2,1,0:T(8,128)S(1)}, f32[4,64,512]{2,1,0:T(8,128)}, u32[]{:S(2)}) copy-start(f32[4,64,512]{2,1,0:T(8,128)} %gather_fusion) | copy-start | bytes 1572868
  325.1 2.2 copy-start.8
  327.3 2.2 copy-start
  (1 other events, 0.7 us)

commit v2 on v0

v2 whole, which is shorter than its diff:
```python
import functools
import math

import jax
import jax.numpy as jnp
from jax import lax
from jax.experimental import pallas as pl
from jax.experimental.pallas import tpu as pltpu
from jax.sharding import PartitionSpec as P

BLK = 128
BAND = 4
WIDTH = 2 * BAND + 1
CHUNK = 16 * BLK
ROWS_STEP = 256
VMEM_LIMIT = 48 * 1024 * 1024

SMEM = pl.BlockSpec(memory_space=pltpu.SMEM)
VMEM = pl.BlockSpec(memory_space=pltpu.VMEM)
HBM = pl.BlockSpec(memory_space=pl.ANY)

band_gain = 3.0
FACTOR = band_gain / math.sqrt(WIDTH * BLK)


def dot(a, b):
    return jnp.dot(a, b, preferred_element_type=jnp.float32)


def dot_ta(a, b):
    return lax.dot_general(a, b, (((0,), (0,)), ((), ())), preferred_element_type=jnp.float32)


def dot_tb(a, b):
    return lax.dot_general(a, b, (((1,), (1,)), ((), ())), preferred_element_type=jnp.float32)


def params():
    return pltpu.CompilerParams(vmem_limit_bytes=VMEM_LIMIT)


def block_rows(index):
    return pl.ds(pl.multiple_of(index * BLK, BLK), BLK)


def gather_kernel(
    index_ref, count_ref, x_ref, out_ref, index, count, x, zeros, small_sems, in_sem, sem
):
    cap, peers = index_ref.shape
    copies = [
        pltpu.make_async_copy(index_ref, index, small_sems.at[0]),
        pltpu.make_async_copy(count_ref, count, small_sems.at[1]),
    ]
    for copy in copies:
        copy.start()
    for i in range(x.shape[0] // ROWS_STEP):
        rows = pl.ds(i * ROWS_STEP, ROWS_STEP)
        pltpu.make_async_copy(x_ref.at[rows], x.at[rows], in_sem).start()
    zeros[...] = jnp.zeros_like(zeros)
    for copy in copies:
        copy.wait()
    pltpu.make_async_copy(x_ref, x, in_sem).wait()

    def send(peer, carry):
        for s in range(cap):
            target = out_ref.at[block_rows(peer * cap + s)]
            live = s < count[0, peer]

            @pl.when(live)
            def _():
                pltpu.make_async_copy(x.at[block_rows(index[s, peer])], target, sem).start()

            @pl.when(jnp.logical_not(live))
            def _():
                pltpu.make_async_copy(zeros, target, sem).start()

        return carry

    lax.fori_loop(0, peers, send, 0)
    pltpu.make_async_copy(out_ref, out_ref, sem).wait()


def gather_blocks(x, index, count):
    cap, peers = index.shape
    features = x.shape[1]
    return pl.pallas_call(
        gather_kernel,
        in_specs=[HBM] * 3,
        out_specs=HBM,
        out_shape=jax.ShapeDtypeStruct((peers * cap * BLK, features), x.dtype),
        scratch_shapes=[
            pltpu.SMEM(index.shape, index.dtype),
            pltpu.SMEM(count.shape, count.dtype),
            pltpu.VMEM(x.shape, x.dtype),
            pltpu.VMEM((BLK, features), x.dtype),
            pltpu.SemaphoreType.DMA((2,)),
            pltpu.SemaphoreType.DMA,
            pltpu.SemaphoreType.DMA,
        ],
        compiler_params=params(),
        cost_estimate=pl.CostEstimate(
            flops=0,
            bytes_accessed=2 * (x.size + peers * cap * BLK * features),
            transcendentals=0,
        ),
        name="gather_blocks",
    )(index, count, x)


def band_kernel(v_ref, band_ref, out_ref, padded, kept, sem):
    step = pl.program_id(0)
    rim = BAND * BLK
    rows, features = v_ref.shape

    @pl.when(step == 0)
    def _():
        padded[pl.ds(0, rim), :] = jnp.zeros((rim, features), padded.dtype)
        padded[pl.ds(rim, rows), :] = v_ref[...]
        padded[pl.ds(rim + rows, rim), :] = jnp.zeros((rim, features), padded.dtype)

    left = jnp.concatenate([band_ref[0, d] for d in range(WIDTH)], axis=1)
    window = padded[pl.ds(pl.multiple_of(step * BLK, BLK), WIDTH * BLK), :]
    rows = block_rows(step)
    kept[rows, :] = FACTOR * dot(left, window)
    pltpu.make_async_copy(kept.at[rows], out_ref.at[rows], sem).start()

    @pl.when(step == pl.num_programs(0) - 1)
    def _():
        pltpu.make_async_copy(kept, out_ref, sem).wait()


def band_sum(v, band):
    rows, features = v.shape
    return pl.pallas_call(
        band_kernel,
        grid=(band.shape[0],),
        in_specs=[
            pl.BlockSpec(v.shape, lambda i: (0, 0)),
            pl.BlockSpec((1, WIDTH, BLK, BLK), lambda i: (i, 0, 0, 0)),
        ],
        out_specs=HBM,
        out_shape=jax.ShapeDtypeStruct((rows, features), jnp.float32),
        scratch_shapes=[
            pltpu.VMEM((rows + 2 * BAND * BLK, features), v.dtype),
            pltpu.VMEM((rows, features), jnp.float32),
            pltpu.SemaphoreType.DMA,
        ],
        compiler_params=params(),
        cost_estimate=pl.CostEstimate(
            flops=2 * band.size * features,
            bytes_accessed=2 * band.size + 6 * v.size,
            transcendentals=0,
        ),
        name="band_sum",
    )(v, band)


def rim_kernel(v_ref, first_ref, last_ref, low_ref, high_ref):
    start = v_ref.shape[0] - BAND * BLK
    for m in range(BAND):
        rows = pl.ds(m * BLK, BLK)
        left = jnp.concatenate([first_ref[j, m - j] for j in range(m + 1)], axis=0)
        term = dot_ta(left, v_ref[pl.ds(0, (m + 1) * BLK), :])
        low_ref[rows, :] = (FACTOR * term).astype(low_ref.dtype)
        left = jnp.concatenate([last_ref[j, 2 * BAND + m - j] for j in range(m, BAND)], axis=0)
        term = dot_ta(left, v_ref[pl.ds(start + m * BLK, (BAND - m) * BLK), :])
        high_ref[rows, :] = (FACTOR * term).astype(high_ref.dtype)


def rim_terms(v, band):
    blocks = band.shape[0]
    features = v.shape[1]
    part = (BAND,) + band.shape[1:]
    out = jax.ShapeDtypeStruct((BAND * BLK, features), v.dtype)
    return pl.pallas_call(
        rim_kernel,
        grid=(1,),
        in_specs=[
            pl.BlockSpec(v.shape, lambda i: (0, 0)),
            pl.BlockSpec(part, lambda i: (0, 0, 0, 0)),
            pl.BlockSpec(part, lambda i: (blocks // BAND - 1, 0, 0, 0)),
        ],
        out_specs=[pl.BlockSpec(out.shape, lambda i: (0, 0))] * 2,
        out_shape=[out] * 2,
        compiler_params=params(),
        cost_estimate=pl.CostEstimate(
            flops=2 * 20 * BLK * BLK * features, bytes_accessed=6 << 20, transcendentals=0
        ),
        name="rim_terms",
    )(v, band, band)


def neighbour_terms(v, band):
    count = lax.axis_size("genome")
    forward = [(i, i + 1) for i in range(count - 1)]
    backward = [(target, source) for source, target in forward]
    low, high = rim_terms(v, band)
    return lax.ppermute(high, "genome", forward), lax.ppermute(low, "genome", backward)


def start_total(total, band_ref, low_ref, high_ref):
    rows = total.shape[0]
    rim = low_ref.shape[0]
    total[pl.ds(0, rim), :] = band_ref[pl.ds(0, rim), :] + low_ref[...].astype(jnp.float32)
    total[pl.ds(rim, rows - 2 * rim), :] = band_ref[pl.ds(rim, rows - 2 * rim), :]
    total[pl.ds(rows - rim, rim), :] = band_ref[pl.ds(rows - rim, rim), :] + high_ref[
        ...
    ].astype(jnp.float32)


def middle_kernel(
    target_ref,
    arrived_ref,
    vals_ref,
    band_ref,
    low_ref,
    high_ref,
    weight_ref,
    grad_ref,
    output_ref,
    grads_ref,
    y_ref,
    terms_ref,
    blocks,
    total,
    kept,
    in_sems,
    out_sems,
):
    chunks = blocks.shape[0] // CHUNK
    slots = CHUNK // BLK
    steps = total.shape[0] // ROWS_STEP
    for i in range(chunks):
        rows = pl.ds(i * CHUNK, CHUNK)
        pltpu.make_async_copy(arrived_ref.at[rows], blocks.at[rows], in_sems.at[i]).start()
    start_total(total, band_ref, low_ref, high_ref)

    def add_chunk(i, carry):
        rows = pl.ds(pl.multiple_of(i * CHUNK, CHUNK), CHUNK)
        pltpu.make_async_copy(arrived_ref.at[rows], blocks.at[rows], in_sems.at[i]).wait()
        for j in range(slots):
            slot = i * slots + j
            rows = block_rows(target_ref[slot])
            total[rows, :] += dot(vals_ref[slot], blocks[block_rows(slot), :])
        return carry

    lax.fori_loop(0, chunks, add_chunk, 0)

    outs = (output_ref, grads_ref, y_ref)
    for i in range(steps):
        rows = pl.ds(i * ROWS_STEP, ROWS_STEP)
        y = total[rows, :].astype(jnp.bfloat16)
        kept[2, rows, :] = y
        preact = dot(y, weight_ref[...])
        sigma = jax.nn.sigmoid(preact)
        kept[0, rows, :] = (preact * sigma).astype(jnp.bfloat16)
        slope = sigma * (1.0 + preact * (1.0 - sigma))
        kept[1, rows, :] = (grad_ref[rows, :].astype(jnp.float32) * slope).astype(jnp.bfloat16)
        for k in range(3):
            pltpu.make_async_copy(kept.at[k, rows], outs[k].at[rows], out_sems.at[k]).start()

    def back_chunk(i, carry):
        for j in range(slots):
            slot = i * slots + j
            rows = block_rows(target_ref[slot])
            term = dot_ta(vals_ref[slot], kept[1, rows, :])
            blocks[block_rows(slot), :] = term.astype(jnp.bfloat16)
        rows = pl.ds(pl.multiple_of(i * CHUNK, CHUNK), CHUNK)
        pltpu.make_async_copy(blocks.at[rows], terms_ref.at[rows], out_sems.at[3]).start()
        return carry

    lax.fori_loop(0, chunks, back_chunk, 0)
    for k in range(3):
        pltpu.make_async_copy(kept.at[k], outs[k], out_sems.at[k]).wait()
    pltpu.make_async_copy(blocks, terms_ref, out_sems.at[3]).wait()


def middle(target, arrived, vals, band, low, high, weight, grad_out):
    rows, features = grad_out.shape
    out = jax.ShapeDtypeStruct((rows, features), jnp.bfloat16)
    return pl.pallas_call(
        middle_kernel,
        in_specs=[SMEM, HBM] + [VMEM] * 6,
        out_specs=[HBM] * 4,
        out_shape=[out] * 3 + [jax.ShapeDtypeStruct(arrived.shape, jnp.bfloat16)],
        scratch_shapes=[
            pltpu.VMEM(arrived.shape, jnp.bfloat16),
            pltpu.VMEM((rows, features), jnp.float32),
            pltpu.VMEM((3, rows, features), jnp.bfloat16),
            pltpu.SemaphoreType.DMA((arrived.shape[0] // CHUNK,)),
            pltpu.SemaphoreType.DMA((4,)),
        ],
        compiler_params=params(),
        cost_estimate=pl.CostEstimate(
            flops=2 * (2 * vals.size + rows * features) * features,
            bytes_accessed=2 * (2 * arrived.size + vals.size + 6 * rows * features),
            transcendentals=rows * features,
        ),
        name="middle",
    )(target, arrived, vals, band, low, high, weight, grad_out)


def tail_kernel(
    cap,
    index_ref,
    count_ref,
    back_ref,
    band_ref,
    low_ref,
    high_ref,
    weight_ref,
    out_ref,
    back,
    total,
    kept,
    in_sems,
    sem,
):
    chunks = back_ref.shape[0] // CHUNK
    steps = total.shape[0] // ROWS_STEP
    for i in range(chunks):
        rows = pl.ds(i * CHUNK, CHUNK)
        pltpu.make_async_copy(back_ref.at[rows], back.at[rows], in_sems.at[i]).start()
    start_total(total, band_ref, low_ref, high_ref)

    def add_chunk(i, carry):
        rows = pl.ds(pl.multiple_of(i * CHUNK, CHUNK), CHUNK)
        pltpu.make_async_copy(back_ref.at[rows], back.at[rows], in_sems.at[i]).wait()
        for j in range(CHUNK // BLK):
            slot = i * (CHUNK // BLK) + j

            @pl.when(lax.rem(slot, cap) < count_ref[slot // cap])
            def _():
                rows = block_rows(index_ref[slot])
                total[rows, :] += back[block_rows(slot), :].astype(jnp.float32)

        return carry

    lax.fori_loop(0, chunks, add_chunk, 0)
    for i in range(steps):
        rows = pl.ds(i * ROWS_STEP, ROWS_STEP)
        grad_z = total[rows, :].astype(jnp.bfloat16)
        kept[rows, :] = dot(grad_z, weight_ref[...]).astype(jnp.bfloat16)
        pltpu.make_async_copy(kept.at[rows], out_ref.at[rows], sem).start()
    pltpu.make_async_copy(kept, out_ref, sem).wait()


def tail(index, count, cap, back, band, low, high, weight_t):
    rows, features = band.shape
    return pl.pallas_call(
        functools.partial(tail_kernel, cap),
        in_specs=[SMEM, SMEM, HBM] + [VMEM] * 4,
        out_specs=HBM,
        out_shape=jax.ShapeDtypeStruct((rows, features), jnp.bfloat16),
        scratch_shapes=[
            pltpu.VMEM(back.shape, jnp.bfloat16),
            pltpu.VMEM((rows, features), jnp.float32),
            pltpu.VMEM((rows, features), jnp.bfloat16),
            pltpu.SemaphoreType.DMA((back.shape[0] // CHUNK,)),
            pltpu.SemaphoreType.DMA,
        ],
        compiler_params=params(),
        cost_estimate=pl.CostEstimate(
            flops=2 * band.size * features,
            bytes_accessed=2 * back.size + 6 * band.size,
            transcendentals=0,
        ),
        name="tail",
    )(index, count, back, band, low, high, weight_t)


def exchange(blocks):
    peers = lax.axis_size("genome")
    cut = blocks.reshape(peers, -1, blocks.shape[-1])
    return lax.all_to_all(cut, "genome", 0, 0, tiled=True).reshape(blocks.shape)


def moved(index, kind, s):
    core, x, y = index & 1, (index >> 1) & 3, index >> 3
    if kind == "x":
        x = (x + s) & 3
    else:
        y = (y + s) & 3
    return y * 8 + x * 2 + core


def shift(v, kind, s):
    return lax.ppermute(v, "genome", [(i, moved(i, kind, s)) for i in range(32)])


def within(v, flip, s):
    pairs = [
        (g * 4 + c, (g ^ flip) * 4 + ((c + s) & 3)) for g in range(32) for c in range(4)
    ]
    return lax.ppermute(v, ("genome", "cell"), pairs)


def scatter_sum(v, core, cell):
    rows = v.shape[0] // 8
    total = None
    for flip in (0, 1):
        for s in range(4):
            owner = (core ^ flip) * 4 + ((cell + s) & 3)
            part = lax.dynamic_slice_in_dim(v, owner * rows, rows, axis=0)
            part = part if (flip, s) == (0, 0) else within(part, flip, s)
            total = part if total is None else total + part
    return total


def put_kernel(cell_ref, *refs):
    out_ref = refs[-1]
    rows = refs[0].shape[0]
    for s, ref in enumerate(refs[:-1]):
        place = ((cell_ref[0] - s) & 3) * rows
        out_ref[pl.ds(pl.multiple_of(place, rows), rows), :] = ref[...]


def join_kernel(core_ref, mine_ref, other_ref, out_ref):
    rows = mine_ref.shape[0]
    for ref, core in ((mine_ref, core_ref[0]), (other_ref, 1 - core_ref[0])):
        out_ref[pl.ds(pl.multiple_of(core * rows, rows), rows), :] = ref[...].astype(
            jnp.float32
        )


def gather_sum(v, core, cell):
    rows, features = v.shape
    parts = [v] + [within(v, 0, s) for s in (1, 2, 3)]
    mine = pl.pallas_call(
        put_kernel,
        in_specs=[SMEM] + [VMEM] * 4,
        out_specs=VMEM,
        out_shape=jax.ShapeDtypeStruct((4 * rows, features), v.dtype),
        compiler_params=params(),
        name="put_parts",
    )(cell[None], *parts)
    return pl.pallas_call(
        join_kernel,
        in_specs=[SMEM] + [VMEM] * 2,
        out_specs=VMEM,
        out_shape=jax.ShapeDtypeStruct((8 * rows, features), jnp.float32),
        compiler_params=params(),
        name="join_halves",
    )(core[None], mine, within(mine, 1, 0))


def on_device(inputs, weight, band_vals, far_rows, far_send, far_count, far_vals, grad_out):
    x = inputs[0]
    band = band_vals[0]
    cap = far_send.shape[-1]
    send_index = far_send.reshape(-1)
    target_index = far_rows.reshape(-1)
    count = far_count.reshape(-1)
    vals = far_vals.reshape(-1, BLK, BLK)
    core = lax.axis_index("genome") & 1
    cell = lax.axis_index("cell")

    arrived = exchange(gather_blocks(x, far_send[0, 0].T, far_count[0]))
    low, high = neighbour_terms(x, band)
    band_part = band_sum(x, band)
    output, grads, y, terms = middle(
        target_index, arrived, vals, band_part, low, high, weight, grad_out[0]
    )
    came_back = exchange(terms)
    low, high = neighbour_terms(grads, band)
    part = scatter_sum(dot_ta(y, grads), core, cell)
    back_band = band_sum(grads, band)
    part, back_band = lax.optimization_barrier((part, back_band))
    sent = part.astype(jnp.bfloat16)
    part = part + sum(shift(sent, "y", s).astype(jnp.float32) for s in (1, 2, 3))
    sent = part.astype(jnp.bfloat16)
    moved_on = [shift(sent, "x", s) for s in (1, 2, 3)]
    grad_in = tail(send_index, count, cap, came_back, back_band, low, high, weight.T)
    moved_on, grad_in = lax.optimization_barrier((moved_on, grad_in))
    part = part + sum(v.astype(jnp.float32) for v in moved_on)
    grad_weight = gather_sum(part.astype(jnp.bfloat16), core, cell)
    return (output[None], grad_in[None], grad_weight)


def solution(mesh):
    return jax.shard_map(
        on_device,
        mesh=mesh,
        in_specs=(
            P("cell", "genome", None),
            P(),
            P("cell", "genome", None, None, None),
            P("cell", "genome", None, None),
            P("cell", "genome", None, None),
            P("cell", "genome", None),
            P("cell", "genome", None, None, None, None),
            P("cell", "genome", None),
        ),
        out_specs=(P("cell", "genome", None), P("cell", "genome", None), P()),
        check_vma=False,
    )
```

time: 611 us -> 281 us (0.46)
  waiting for transfers between devices: 343 us -> 148 us
  matrix products: 131 us -> 2.86 us
  Pallas kernels: 0 us -> 59 us
  local copies, waits for them, and re-layouts: 67 us -> 8.83 us
  starting transfers between devices: 30.2 us -> 59.1 us
  other arithmetic: 23.8 us -> 1.16 us
  between operations: 14.2 us -> 1 us
    psum x1 -> x0, waiting for transfers between devices: 148 us -> none  [on_device(): grad_weight = lax.psum(local_weight, ('genome', 'cell'))]
    dot_general x25 -> x1, matrix products: 131 us -> 2.86 us  [dot_ta(): lax.dot_general(a, b, (((0,), (0,)), ((), ())), preferred_element_type=jn...]
    pallas_call x0 -> x9, Pallas kernels: none -> 59 us  [the longest x2 25.2 us: band_sum(): pl.pallas_call(band_kernel, grid=(band.shape[0],), in_specs=[pl.BlockSpec...]
    ppermute x4 -> x21, waiting for transfers between devices: 195 us -> 148 us  [the longest x2 78.7 us: neighbour_terms(): lax.ppermute(high, 'genome', forward)]
    ppermute x4 -> x21, starting transfers between devices: 11.3 us -> 40.3 us  [the longest x11 17.9 us: within(): return lax.ppermute(v, ('genome', 'cell'), pairs)]
    gather x9 -> x0, local copies, waits for them, and re-layouts: 26.2 us -> none  [pick_rows(): return blocks[chosen]]
    dot_general x1 -> x0, local copies, waits for them, and re-layouts: 20 us -> none  [on_device(): jnp.einsum('cpsij,cpsjf->cpsif', loop_vals, arrived, preferred_element_ty...]
    another operation x1 -> x0, local copies, waits for them, and re-layouts: 14.7 us -> none
  transfers between devices with their start and end apart: 7 -> 23, of which waited for: 3 -> 8; matrix products, arithmetic and copies ran while one was open for 10% -> 2% of each run, Pallas kernels for 0% -> 14%
where the time goes in v2:
time: 281 us; the launch traced here: 280 us
  waiting for transfers between devices  148 us (53%)
  starting transfers between devices  59.1 us (21%)
  Pallas kernels  59 us (21%)
  local copies, waits for them, and re-layouts  8.83 us (3%)
  matrix products  2.86 us (1%)
    ppermute x2, waiting for transfers between devices, neighbour_terms(): lax.ppermute(high, 'genome', forward)  78.7 us
    ppermute x6, waiting for transfers between devices, shift(): lax.ppermute(v, 'genome', [(i, moved(i, kind, s)) for i in range(32)])  60.3 us
    pallas_call x2, Pallas kernels, band_sum(): pl.pallas_call(band_kernel, grid=(band.shape[0],), in_specs=[pl.BlockSpec...  25.2 us
    all_to_all x2, starting transfers between devices, exchange(): return lax.all_to_all(cut, 'genome', 0, 0, tiled=True).reshape(blocks.shape)  18.7 us
    ppermute x11, starting transfers between devices, within(): return lax.ppermute(v, ('genome', 'cell'), pairs)  17.9 us
    pallas_call x1, Pallas kernels, middle(): pl.pallas_call(middle_kernel, in_specs=[SMEM, HBM] + [VMEM] * 6, out_spec...  16.2 us
    ppermute x6, starting transfers between devices, shift(): lax.ppermute(v, 'genome', [(i, moved(i, kind, s)) for i in range(32)])  11.8 us
    unnamed x25, local copies, waits for them, and re-layouts  7.8 us
  transfers between devices with their start and end apart: 23, of which 8 were waited for; matrix products, arithmetic and copies ran while one was open for 2% of the time, Pallas kernels for 14%

profile of v2, /device:TPU:1, one launch (start us, length us, event | category | flops | bytes accessed | tf_op | source)
XLA Modules:
  0.0 280.2 jit_solution(12735348016728733488)
XLA Ops:
  0.6 1.6 copy-done
  3.6 3.9 %gather_blocks.1 = bf16[8192,512]{1,0:T(8,128)(2,1)} custom-call(s32[2,32]{1,0:T(2,128)S(1)} %bitcast.28, s32[1,32]{1,0:T(1,128)S(1)} %bitcast.29, bf16[2048,512]{1,0:T(8,128)(2,1)S(1)} %bitcast.24), custom_call_target="tpu_custom_call" | custom-call | bytes 10485760 | tf_op jit(solution)/shard_map/gather_blocks/pallas_call | solution.py:86
  7.5 8.8 %all-to-all-start = ((bf16[32,256,512]{2,1,0:T(8,128)(2,1)}), bf16[32,256,512]{2,1,0:T(8,128)(2,1)}, u32[]{:S(2)}, u32[]{:S(2)}) async-start(bf16[32,256,512]{2,1,0:T(8,128)(2,1)} %bitcast.37), calls=%async_computation | async-start | bytes 16777216 | tf_op jit(solution)/shard_map/all_to_all | solution.py:375
  16.3 3.2 %rim_terms.2 = (bf16[512,512]{1,0:T(8,128)(2,1)}, bf16[512,512]{1,0:T(8,128)(2,1)}) custom-call(bf16[2048,512]{1,0:T(8,128)(2,1)S(1)} %bitcast.25, bf16[16,9,128,128]{3,2,1,0:T(8,128)(2,1)} %bitcast.31, bf16[16,9,128,128]{3,2,1,0:T(8,128)(2,1)} %bitcast.32), custom_call_target="tpu_custom_call" | custom-call | flops 335544320 | bytes 6291456 | tf_op jit(solution)/shard_map/rim_terms/pallas_call | solution.py:175
  19.5 3.5 %collective-permute-start = (bf16[512,512]{1,0:T(8,128)(2,1)}, bf16[512,512]{1,0:T(8,128)(2,1)S(1)}, u32[]{:S(2)}, u32[]{:S(2)}) collective-permute-start(bf16[512,512]{1,0:T(8,128)(2,1)} %get-tuple-element.17), channel_id=1, source_target_pairs={{0,4},{4,8},{8,12},{12,16},{16,20},{20,24},{24,28},{28,32},{32,36}... | collective-permute-start | bytes 1572872 | tf_op jit(solution)/shard_map/ppermute | solution.py:198
  23.0 1.9 collective-permute-start.1
  25.1 12.7 %band_sum.2.band_ref = f32[2048,512]{1,0:T(8,128)} custom-call(bf16[2048,512]{1,0:T(8,128)(2,1)S(1)} %bitcast.26, bf16[16,9,128,128]{3,2,1,0:T(8,128)(2,1)} %bitcast.33), custom_call_target="tpu_custom_call" | custom-call | flops 2415919104 | bytes 11010048 | tf_op jit(solution)/shard_map/band_sum/pallas_call | solution.py:134
  37.8 78.7 %collective-permute-done.low_ref = bf16[512,512]{1,0:T(8,128)(2,1)S(1)} collective-permute-done((bf16[512,512]{1,0:T(8,128)(2,1)}, bf16[512,512]{1,0:T(8,128)(2,1)S(1)}, u32[]{:S(2)}, u32[]{:S(2)}) %collective-permute-start) | collective-permute-done | bytes 524320 | tf_op jit(solution)/shard_map/ppermute | solution.py:198
  116.5 4.9 %collective-permute-done.1.high_ref = bf16[512,512]{1,0:T(8,128)(2,1)} collective-permute-done((bf16[512,512]{1,0:T(8,128)(2,1)}, bf16[512,512]{1,0:T(8,128)(2,1)}, u32[]{:S(2)}, u32[]{:S(2)}) %collective-permute-start.1) | collective-permute-done | bytes 524320 | tf_op jit(solution)/shard_map/ppermute | solution.py:198
  121.4 16.2 %middle.1 = (bf16[2048,512]{1,0:T(8,128)(2,1)}, bf16[2048,512]{1,0:T(8,128)(2,1)S(1)}, bf16[2048,512]{1,0:T(8,128)(2,1)S(1)}, bf16[8192,512]{1,0:T(8,128)(2,1)}) custom-call(s32[64]{0:T(128)S(1)} %reshape.30.target_ref, bf16[8192,512]{1,0:T(8,128)(2,1)} %bitcast.5.arrived_ref, bf16[64,128,128]{2,1,0:T(8,128)(2,1)} %bitcast.39, ...), custom_call_target="tpu_custom_call" | custom-call | flops 3221225472 | bytes 31457280 | tf_op jit(solution)/shard_map/middle/pallas_call | solution.py:281
  137.5 1.3 copy-done.8
  138.9 10.0 %all-to-all-start.1 = ((bf16[32,256,512]{2,1,0:T(8,128)(2,1)}), bf16[32,256,512]{2,1,0:T(8,128)(2,1)}, u32[]{:S(2)}, u32[]{:S(2)}) async-start(bf16[32,256,512]{2,1,0:T(8,128)(2,1)} %bitcast.38), calls=%async_computation.1 | async-start | bytes 16777216 | tf_op jit(solution)/shard_map/all_to_all | solution.py:375
  148.9 2.9 %fusion.1 = f32[512,512]{1,0:T(8,128)S(1)} fusion(bf16[2048,512]{1,0:T(8,128)(2,1)} %copy-done.8, bf16[2048,512]{1,0:T(8,128)(2,1)S(1)} %get-tuple-element.21.v_ref), kind=kOutput, calls=%fused_computation.11 | convolution fusion | flops 1073741824 | bytes 5242880 | tf_op jit(solution)/shard_map/dot_general | solution.py:31
  153.5 1.6 collective-permute-start.2
  155.2 3.3 %collective-permute-start.3 = (f32[64,512]{1,0:T(8,128)}, f32[64,512]{1,0:T(8,128)}, u32[]{:S(2)}, u32[]{:S(2)}) collective-permute-start(f32[64,512]{1,0:T(8,128)} %get-tuple-element.37), channel_id=1, source_target_pairs={{0,2},{1,3},{2,0},{3,1},{4,6},{5,7},{6,4},{7,5},{8,10},{9,11},{10,... | collective-permute-start | bytes 393224 | tf_op jit(solution)/shard_map/ppermute | solution.py:395
  161.0 3.0 %rim_terms.3 = (bf16[512,512]{1,0:T(8,128)(2,1)S(1)}, bf16[512,512]{1,0:T(8,128)(2,1)}) custom-call(bf16[2048,512]{1,0:T(8,128)(2,1)S(1)} %get-tuple-element.21.v_ref, bf16[16,9,128,128]{3,2,1,0:T(8,128)(2,1)} %bitcast.34, bf16[16,9,128,128]{3,2,1,0:T(8,128)(2,1)} %bitcast.35), custom_call_target="tpu_custom_call" | custom-call | flops 335544320 | bytes 6291456 | tf_op jit(solution)/shard_map/rim_terms/pallas_call | solution.py:175
  164.9 1.9 collective-permute-start.8
  166.8 12.6 %band_sum.3.band_ref = f32[2048,512]{1,0:T(8,128)} custom-call(bf16[2048,512]{1,0:T(8,128)(2,1)S(1)} %get-tuple-element.21.v_ref, bf16[16,9,128,128]{3,2,1,0:T(8,128)(2,1)} %bitcast.36), custom_call_target="tpu_custom_call" | custom-call | flops 2415919104 | bytes 11010048 | tf_op jit(solution)/shard_map/band_sum/pallas_call | solution.py:134
  179.4 3.3 %collective-permute-start.15 = (bf16[512,512]{1,0:T(8,128)(2,1)}, bf16[512,512]{1,0:T(8,128)(2,1)S(1)}, u32[]{:S(2)}, u32[]{:S(2)}) collective-permute-start(bf16[512,512]{1,0:T(8,128)(2,1)} %get-tuple-element.25), channel_id=1, source_target_pairs={{0,4},{4,8},{8,12},{12,16},{16,20},{20,24},{24,28},{28,32},{32,36}... | collective-permute-start | bytes 1572872 | tf_op jit(solution)/shard_map/ppermute | solution.py:198
  182.7 1.9 collective-permute-start.16
  185.7 2.7 collective-permute-start.10
  190.4 56.1 %collective-permute-done.10 = bf16[64,512]{1,0:T(8,128)(2,1)S(1)} collective-permute-done((bf16[64,512]{1,0:T(8,128)(2,1)S(1)}, bf16[64,512]{1,0:T(8,128)(2,1)S(1)}, u32[]{:S(2)}, u32[]{:S(2)}) %collective-permute-start.10) | collective-permute-done | bytes 65568 | tf_op jit(solution)/shard_map/ppermute | solution.py:388
  246.4 4.2 %collective-permute-done.11 = bf16[64,512]{1,0:T(8,128)(2,1)S(1)} collective-permute-done((bf16[64,512]{1,0:T(8,128)(2,1)S(1)}, bf16[64,512]{1,0:T(8,128)(2,1)S(1)}, u32[]{:S(2)}, u32[]{:S(2)}) %collective-permute-start.11) | collective-permute-done | bytes 65568 | tf_op jit(solution)/shard_map/ppermute | solution.py:388
  250.7 7.5 %collective-permute-start.13 = (bf16[64,512]{1,0:T(8,128)(2,1)S(1)}, bf16[64,512]{1,0:T(8,128)(2,1)S(1)}, u32[]{:S(2)}, u32[]{:S(2)}) collective-permute-start(bf16[64,512]{1,0:T(8,128)(2,1)S(1)} %fusion), channel_id=1, source_target_pairs={{0,16},{4,20},{8,24},{12,28},{16,0},{20,4},{24,8},{28,12},{32,48},... | collective-permute-start | bytes 196616 | tf_op jit(solution)/shard_map/ppermute | solution.py:388
  258.3 2.2 copy-done.2
  260.5 6.5 %tail.1 = bf16[2048,512]{1,0:T(8,128)(2,1)} custom-call(s32[64]{0:T(128)S(1)} %reshape.34.index_ref, s32[32]{0:T(128)S(1)} %bitcast.30, bf16[8192,512]{1,0:T(8,128)(2,1)} %bitcast.12.back_ref, f32[2048,512]{1,0:T(8,128)S(1)} %copy-done.2, bf16[512,512]{1,0:T(8,128)(2,1)S(1)} %collective-permute-done.15.low_ref, ...), custom_call_target="tpu_custom_call" | custom-call | flops 1073741824 | bytes 14680064 | tf_op jit(solution)/shard_map/tail/pallas_call | solution.py:350
  267.0 1.7 collective-permute-start.17
  268.8 3.4 %collective-permute-start.18 = (bf16[64,512]{1,0:T(8,128)(2,1)S(1)}, bf16[64,512]{1,0:T(8,128)(2,1)S(1)}, u32[]{:S(2)}, u32[]{:S(2)}) collective-permute-start(bf16[64,512]{1,0:T(8,128)(2,1)S(1)} %add_convert_fusion.refs_0_), channel_id=1, source_target_pairs={{0,2},{1,3},{2,0},{3,1},{4,6},{5,7},{6,4},{7,5},{8,10},{9,11},{10,... | collective-permute-start | bytes 196616 | tf_op jit(solution)/shard_map/ppermute | solution.py:395
  272.7 1.8 collective-permute-done.18.refs_2_
  274.5 1.2 collective-permute-done.19.refs_3_
  275.7 2.3 collective-permute-start.20
  278.0 1.2 collective-permute-done.20.other_ref
  (56 shorter events, 11.6 us)
Async XLA Ops:
  0.6 1.6 copy-start
  7.5 8.8 %copy-start.1 = (bf16[1,2048,512]{2,1,0:T(8,128)(2,1)S(1)}, bf16[1,2048,512]{2,1,0:T(8,128)(2,1)}, u32[]{:S(2)}) copy-start(bf16[1,2048,512]{2,1,0:T(8,128)(2,1)} %param.8) | copy-start | bytes 6291460
  7.5 113.9 %all-to-all-start = ((bf16[32,256,512]{2,1,0:T(8,128)(2,1)}), bf16[32,256,512]{2,1,0:T(8,128)(2,1)}, u32[]{:S(2)}, u32[]{:S(2)}) async-start(bf16[32,256,512]{2,1,0:T(8,128)(2,1)} %bitcast.37), calls=%async_computation | async-start | bytes 16777216 | tf_op jit(solution)/shard_map/all_to_all | solution.py:375
  16.3 8.6 %copy-start.10 = (s32[1,1,32,2]{2,3,1,0:T(2,128)S(1)}, s32[1,1,32,2]{2,3,1,0:T(2,128)}, u32[]{:S(2)}) copy-start(s32[1,1,32,2]{2,3,1,0:T(2,128)} %param.11) | copy-start | bytes 772
  19.5 97.1 %collective-permute-start = (bf16[512,512]{1,0:T(8,128)(2,1)}, bf16[512,512]{1,0:T(8,128)(2,1)S(1)}, u32[]{:S(2)}, u32[]{:S(2)}) collective-permute-start(bf16[512,512]{1,0:T(8,128)(2,1)} %get-tuple-element.17), channel_id=1, source_target_pairs={{0,4},{4,8},{8,12},{12,16},{16,20},{20,24},{24,28},{28,32},{32,36}... | collective-permute-start | bytes 1572872 | tf_op jit(solution)/shard_map/ppermute | solution.py:198
  23.0 98.4 %collective-permute-start.1 = (bf16[512,512]{1,0:T(8,128)(2,1)}, bf16[512,512]{1,0:T(8,128)(2,1)}, u32[]{:S(2)}, u32[]{:S(2)}) collective-permute-start(bf16[512,512]{1,0:T(8,128)(2,1)} %get-tuple-element.18), channel_id=1, source_target_pairs={{4,0},{8,4},{12,8},{16,12},{20,16},{24,20},{28,24},{32,28},{36,32}... | collective-permute-start | bytes 1572872 | tf_op jit(solution)/shard_map/ppermute | solution.py:198
  25.1 96.3 %copy-start.3 = (bf16[512,512]{1,0:T(8,128)(2,1)S(1)}, bf16[512,512]{1,0:T(8,128)(2,1)}, u32[]{:S(2)}) copy-start(bf16[512,512]{1,0:T(8,128)(2,1)} %weight_ref.1) | copy-start | bytes 1572868
  137.5 1.3 copy-start.8
  138.9 119.4 %all-to-all-start.1 = ((bf16[32,256,512]{2,1,0:T(8,128)(2,1)}), bf16[32,256,512]{2,1,0:T(8,128)(2,1)}, u32[]{:S(2)}, u32[]{:S(2)}) async-start(bf16[32,256,512]{2,1,0:T(8,128)(2,1)} %bitcast.38), calls=%async_computation.1 | async-start | bytes 16777216 | tf_op jit(solution)/shard_map/all_to_all | solution.py:375
  151.7 1.0 copy-start.9
  153.5 10.5 %collective-permute-start.2 = (f32[64,512]{1,0:T(8,128)}, f32[64,512]{1,0:T(8,128)S(1)}, u32[]{:S(2)}, u32[]{:S(2)}) collective-permute-start(f32[64,512]{1,0:T(8,128)} %get-tuple-element.31), channel_id=1, source_target_pairs={{0,1},{1,2},{2,3},{3,0},{4,5},{5,6},{6,7},{7,4},{8,9},{9,10},{10,1... | collective-permute-start | bytes 393224 | tf_op jit(solution)/shard_map/ppermute | solution.py:395
  155.2 9.8 %collective-permute-start.3 = (f32[64,512]{1,0:T(8,128)}, f32[64,512]{1,0:T(8,128)}, u32[]{:S(2)}, u32[]{:S(2)}) collective-permute-start(f32[64,512]{1,0:T(8,128)} %get-tuple-element.37), channel_id=1, source_target_pairs={{0,2},{1,3},{2,0},{3,1},{4,6},{5,7},{6,4},{7,5},{8,10},{9,11},{10,... | collective-permute-start | bytes 393224 | tf_op jit(solution)/shard_map/ppermute | solution.py:395
  158.5 20.9 %collective-permute-start.4 = (f32[64,512]{1,0:T(8,128)}, f32[64,512]{1,0:T(8,128)S(1)}, u32[]{:S(2)}, u32[]{:S(2)}) collective-permute-start(f32[64,512]{1,0:T(8,128)} %get-tuple-element.36), channel_id=1, source_target_pairs={{0,3},{1,0},{2,1},{3,2},{4,7},{5,4},{6,5},{7,6},{8,11},{9,8},{10,9... | collective-permute-start | bytes 393224 | tf_op jit(solution)/shard_map/ppermute | solution.py:395
  159.2 23.5 %collective-permute-start.5 = (f32[64,512]{1,0:T(8,128)}, f32[64,512]{1,0:T(8,128)S(1)}, u32[]{:S(2)}, u32[]{:S(2)}) collective-permute-start(f32[64,512]{1,0:T(8,128)} %get-tuple-element.35), channel_id=1, source_target_pairs={{0,4},{1,5},{2,6},{3,7},{4,0},{5,1},{6,2},{7,3},{8,12},{9,13},{10,... | collective-permute-start | bytes 393224 | tf_op jit(solution)/shard_map/ppermute | solution.py:395
  160.4 24.3 %collective-permute-start.6 = (f32[64,512]{1,0:T(8,128)}, f32[64,512]{1,0:T(8,128)S(1)}, u32[]{:S(2)}, u32[]{:S(2)}) collective-permute-start(f32[64,512]{1,0:T(8,128)} %get-tuple-element.34), channel_id=1, source_target_pairs={{0,5},{1,6},{2,7},{3,4},{4,1},{5,2},{6,3},{7,0},{8,13},{9,14},{10,... | collective-permute-start | bytes 393224 | tf_op jit(solution)/shard_map/ppermute | solution.py:395
  164.0 20.6 %collective-permute-start.7 = (f32[64,512]{1,0:T(8,128)S(1)}, f32[64,512]{1,0:T(8,128)S(1)}, u32[]{:S(2)}, u32[]{:S(2)}) collective-permute-start(f32[64,512]{1,0:T(8,128)S(1)} %get-tuple-element.33), channel_id=1, source_target_pairs={{0,6},{1,7},{2,4},{3,5},{4,2},{5,3},{6,0},{7,1},{8,14},{9,15},{10,... | collective-permute-start | bytes 393224 | tf_op jit(solution)/shard_map/ppermute | solution.py:395
  164.9 19.7 %collective-permute-start.8 = (f32[64,512]{1,0:T(8,128)S(1)}, f32[64,512]{1,0:T(8,128)S(1)}, u32[]{:S(2)}, u32[]{:S(2)}) collective-permute-start(f32[64,512]{1,0:T(8,128)S(1)} %get-tuple-element.32), channel_id=1, source_target_pairs={{0,7},{1,4},{2,5},{3,6},{4,3},{5,0},{6,1},{7,2},{8,15},{9,12},{10,... | collective-permute-start | bytes 393224 | tf_op jit(solution)/shard_map/ppermute | solution.py:395
  179.4 10.8 %copy-start.5 = (s32[1,1,32,2]{2,3,1,0:T(2,128)S(1)}, s32[1,1,32,2]{2,3,1,0:T(2,128)}, u32[]{:S(2)}) copy-start(s32[1,1,32,2]{2,3,1,0:T(2,128)} %param.12) | copy-start | bytes 772
  179.4 78.9 %copy-start.7 = (s32[1,1,32]{2,1,0:T(1,128)S(1)}, s32[1,1,32]{2,1,0:T(1,128)}, u32[]{:S(2)}) copy-start(s32[1,1,32]{2,1,0:T(1,128)} %param.13) | copy-start | bytes 388
  179.4 78.8 %collective-permute-start.15 = (bf16[512,512]{1,0:T(8,128)(2,1)}, bf16[512,512]{1,0:T(8,128)(2,1)S(1)}, u32[]{:S(2)}, u32[]{:S(2)}) collective-permute-start(bf16[512,512]{1,0:T(8,128)(2,1)} %get-tuple-element.25), channel_id=1, source_target_pairs={{0,4},{4,8},{8,12},{12,16},{16,20},{20,24},{24,28},{28,32},{32,36}... | collective-permute-start | bytes 1572872 | tf_op jit(solution)/shard_map/ppermute | solution.py:198
  182.7 75.5 %collective-permute-start.16 = (bf16[512,512]{1,0:T(8,128)(2,1)S(1)}, bf16[512,512]{1,0:T(8,128)(2,1)S(1)}, u32[]{:S(2)}, u32[]{:S(2)}) collective-permute-start(bf16[512,512]{1,0:T(8,128)(2,1)S(1)} %get-tuple-element.26), channel_id=1, source_target_pairs={{4,0},{8,4},{12,8},{16,12},{20,16},{24,20},{28,24},{32,28},{36,32}... | collective-permute-start | bytes 1572872 | tf_op jit(solution)/shard_map/ppermute | solution.py:198
  185.7 60.7 %collective-permute-start.10 = (bf16[64,512]{1,0:T(8,128)(2,1)S(1)}, bf16[64,512]{1,0:T(8,128)(2,1)S(1)}, u32[]{:S(2)}, u32[]{:S(2)}) collective-permute-start(bf16[64,512]{1,0:T(8,128)(2,1)S(1)} %convert_element_type.27), channel_id=1, source_target_pairs={{0,64},{4,68},{8,72},{12,76},{16,80},{20,84},{24,88},{28,92},{32,9... | collective-permute-start | bytes 196616 | tf_op jit(solution)/shard_map/ppermute | solution.py:388
  188.5 62.1 %collective-permute-start.11 = (bf16[64,512]{1,0:T(8,128)(2,1)S(1)}, bf16[64,512]{1,0:T(8,128)(2,1)S(1)}, u32[]{:S(2)}, u32[]{:S(2)}) collective-permute-start(bf16[64,512]{1,0:T(8,128)(2,1)S(1)} %convert_element_type.27), channel_id=1, source_target_pairs={{0,96},{4,100},{8,104},{12,108},{16,112},{20,116},{24,120},{28,124... | collective-permute-start | bytes 196616 | tf_op jit(solution)/shard_map/ppermute | solution.py:388
  189.4 61.2 %collective-permute-start.9 = (bf16[64,512]{1,0:T(8,128)(2,1)S(1)}, bf16[64,512]{1,0:T(8,128)(2,1)S(1)}, u32[]{:S(2)}, u32[]{:S(2)}) collective-permute-start(bf16[64,512]{1,0:T(8,128)(2,1)S(1)} %convert_element_type.27), channel_id=1, source_target_pairs={{0,32},{4,36},{8,40},{12,44},{16,48},{20,52},{24,56},{28,60},{32,6... | collective-permute-start | bytes 196616 | tf_op jit(solution)/shard_map/ppermute | solution.py:388
  250.7 16.3 %collective-permute-start.12 = (bf16[64,512]{1,0:T(8,128)(2,1)S(1)}, bf16[64,512]{1,0:T(8,128)(2,1)S(1)}, u32[]{:S(2)}, u32[]{:S(2)}) collective-permute-start(bf16[64,512]{1,0:T(8,128)(2,1)S(1)} %fusion), channel_id=1, source_target_pairs={{0,8},{4,12},{8,16},{12,20},{16,24},{20,28},{24,0},{28,4},{32,40},... | collective-permute-start | bytes 196616 | tf_op jit(solution)/shard_map/ppermute | solution.py:388
  250.7 16.2 %collective-permute-start.13 = (bf16[64,512]{1,0:T(8,128)(2,1)S(1)}, bf16[64,512]{1,0:T(8,128)(2,1)S(1)}, u32[]{:S(2)}, u32[]{:S(2)}) collective-permute-start(bf16[64,512]{1,0:T(8,128)(2,1)S(1)} %fusion), channel_id=1, source_target_pairs={{0,16},{4,20},{8,24},{12,28},{16,0},{20,4},{24,8},{28,12},{32,48},... | collective-permute-start | bytes 196616 | tf_op jit(solution)/shard_map/ppermute | solution.py:388
  258.2 8.7 %collective-permute-start.14 = (bf16[64,512]{1,0:T(8,128)(2,1)S(1)}, bf16[64,512]{1,0:T(8,128)(2,1)S(1)}, u32[]{:S(2)}, u32[]{:S(2)}) collective-permute-start(bf16[64,512]{1,0:T(8,128)(2,1)S(1)} %fusion), channel_id=1, source_target_pairs={{0,24},{4,28},{8,0},{12,4},{16,8},{20,12},{24,16},{28,20},{32,56},... | collective-permute-start | bytes 196616 | tf_op jit(solution)/shard_map/ppermute | solution.py:388
  258.3 2.2 copy-start.2
  267.0 5.7 %collective-permute-start.17 = (bf16[64,512]{1,0:T(8,128)(2,1)S(1)}, bf16[64,512]{1,0:T(8,128)(2,1)S(1)}, u32[]{:S(2)}, u32[]{:S(2)}) collective-permute-start(bf16[64,512]{1,0:T(8,128)(2,1)S(1)} %add_convert_fusion.refs_0_), channel_id=1, source_target_pairs={{0,1},{1,2},{2,3},{3,0},{4,5},{5,6},{6,7},{7,4},{8,9},{9,10},{10,1... | collective-permute-start | bytes 196616 | tf_op jit(solution)/shard_map/ppermute | solution.py:395
  268.8 5.7 %collective-permute-start.18 = (bf16[64,512]{1,0:T(8,128)(2,1)S(1)}, bf16[64,512]{1,0:T(8,128)(2,1)S(1)}, u32[]{:S(2)}, u32[]{:S(2)}) collective-permute-start(bf16[64,512]{1,0:T(8,128)(2,1)S(1)} %add_convert_fusion.refs_0_), channel_id=1, source_target_pairs={{0,2},{1,3},{2,0},{3,1},{4,6},{5,7},{6,4},{7,5},{8,10},{9,11},{10,... | collective-permute-start | bytes 196616 | tf_op jit(solution)/shard_map/ppermute | solution.py:395
  272.1 3.5 %collective-permute-start.19 = (bf16[64,512]{1,0:T(8,128)(2,1)S(1)}, bf16[64,512]{1,0:T(8,128)(2,1)S(1)}, u32[]{:S(2)}, u32[]{:S(2)}) collective-permute-start(bf16[64,512]{1,0:T(8,128)(2,1)S(1)} %add_convert_fusion.refs_0_), channel_id=1, source_target_pairs={{0,3},{1,0},{2,1},{3,2},{4,7},{5,4},{6,5},{7,6},{8,11},{9,8},{10,9... | collective-permute-start | bytes 196616 | tf_op jit(solution)/shard_map/ppermute | solution.py:395
  275.7 3.5 %collective-permute-start.20 = (bf16[256,512]{1,0:T(8,128)(2,1)S(1)}, bf16[256,512]{1,0:T(8,128)(2,1)S(1)}, u32[]{:S(2)}, u32[]{:S(2)}) collective-permute-start(bf16[256,512]{1,0:T(8,128)(2,1)S(1)} %put_parts.1.mine_ref), channel_id=1, source_target_pairs={{0,4},{1,5},{2,6},{3,7},{4,0},{5,1},{6,2},{7,3},{8,12},{9,13},{10,... | collective-permute-start | bytes 786440 | tf_op jit(solution)/shard_map/ppermute | solution.py:395
  (2 other events, 1.3 us)

commit v3 on v2

--- a/solution.py
+++ b/solution.py
@@ -13,11 +13,12 @@
 WIDTH = 2 * BAND + 1
 CHUNK = 16 * BLK
 ROWS_STEP = 256
-VMEM_LIMIT = 48 * 1024 * 1024
+VMEM_LIMIT = 65_400_000
 
 SMEM = pl.BlockSpec(memory_space=pltpu.SMEM)
 VMEM = pl.BlockSpec(memory_space=pltpu.VMEM)
-HBM = pl.BlockSpec(memory_space=pl.ANY)
+HBM = pl.BlockSpec(memory_space=pltpu.HBM)
+ANY = pl.BlockSpec(memory_space=pl.ANY)
 
 band_gain = 3.0
 FACTOR = band_gain / math.sqrt(WIDTH * BLK)
@@ -138,7 +139,7 @@
             pl.BlockSpec(v.shape, lambda i: (0, 0)),
             pl.BlockSpec((1, WIDTH, BLK, BLK), lambda i: (i, 0, 0, 0)),
         ],
-        out_specs=HBM,
+        out_specs=ANY,
         out_shape=jax.ShapeDtypeStruct((rows, features), jnp.float32),
         scratch_shapes=[
             pltpu.VMEM((rows + 2 * BAND * BLK, features), v.dtype),
@@ -190,25 +191,48 @@
     )(v, band, band)
 
 
-def neighbour_terms(v, band):
+def to_neighbours(low, high):
     count = lax.axis_size("genome")
     forward = [(i, i + 1) for i in range(count - 1)]
     backward = [(target, source) for source, target in forward]
-    low, high = rim_terms(v, band)
     return lax.ppermute(high, "genome", forward), lax.ppermute(low, "genome", backward)
 
 
-def start_total(total, band_ref, low_ref, high_ref):
-    rows = total.shape[0]
-    rim = low_ref.shape[0]
-    total[pl.ds(0, rim), :] = band_ref[pl.ds(0, rim), :] + low_ref[...].astype(jnp.float32)
-    total[pl.ds(rim, rows - 2 * rim), :] = band_ref[pl.ds(rim, rows - 2 * rim), :]
-    total[pl.ds(rows - rim, rim), :] = band_ref[pl.ds(rows - rim, rim), :] + high_ref[
-        ...
-    ].astype(jnp.float32)
+def fetches(sources, targets, sems):
+    copies = [
+        pltpu.make_async_copy(source, target, sems.at[k])
+        for k, (source, target) in enumerate(zip(sources, targets))
+    ]
+    for copy in copies:
+        copy.start()
+    return copies
+
+
+def chunk_copy(source, target, sems, i):
+    rows = pl.ds(i * CHUNK, CHUNK)
+    return pltpu.make_async_copy(source.at[rows], target.at[rows], sems.at[i])
+
+
+def send_terms(s, cap, target_ref, grads, vals, blocks, terms_ref, sem):
+    peers = terms_ref.shape[0] // BLK
+    group = CHUNK // BLK
+
+    def chunk(i, carry):
+        for j in range(group):
+            peer = i * group + j
+            slot = peer * cap + s
+            term = dot_ta(vals[slot], grads[block_rows(target_ref[slot]), :])
+            blocks[block_rows(peer), :] = term.astype(jnp.bfloat16)
+            if j % 4 == 3:
+                rows = pl.ds(pl.multiple_of((peer - 3) * BLK, 4 * BLK), 4 * BLK)
+                pltpu.make_async_copy(blocks.at[rows], terms_ref.at[rows], sem).start()
+        return carry
+
+    lax.fori_loop(0, peers // group, chunk, 0)
 
 
 def middle_kernel(
+    cap,
     target_ref,
     arrived_ref,
     vals_ref,
@@ -222,72 +246,84 @@
     y_ref,
     terms_ref,
     blocks,
+    vals,
     total,
+    low,
+    high,
+    weight,
+    grad,
     kept,
-    in_sems,
+    block_sems,
+    sems,
     out_sems,
 ):
     chunks = blocks.shape[0] // CHUNK
     slots = CHUNK // BLK
-    steps = total.shape[0] // ROWS_STEP
+    count = total.shape[0]
+    steps = count // ROWS_STEP
+    rim = low.shape[0]
+    first = fetches((band_ref, vals_ref), (total, vals), sems)
     for i in range(chunks):
-        rows = pl.ds(i * CHUNK, CHUNK)
-        pltpu.make_async_copy(arrived_ref.at[rows], blocks.at[rows], in_sems.at[i]).start()
-    start_total(total, band_ref, low_ref, high_ref)
+        chunk_copy(arrived_ref, blocks, block_sems, i).start()
+    later = fetches(
+        (low_ref, high_ref, weight_ref, grad_ref), (low, high, weight, grad), sems.at[pl.ds(2, 4)]
+    )
+    for copy in first:
+        copy.wait()
 
     def add_chunk(i, carry):
         rows = pl.ds(pl.multiple_of(i * CHUNK, CHUNK), CHUNK)
-        pltpu.make_async_copy(arrived_ref.at[rows], blocks.at[rows], in_sems.at[i]).wait()
+        pltpu.make_async_copy(arrived_ref.at[rows], blocks.at[rows], block_sems.at[i]).wait()
         for j in range(slots):
             slot = i * slots + j
             rows = block_rows(target_ref[slot])
-            total[rows, :] += dot(vals_ref[slot], blocks[block_rows(slot), :])
+            total[rows, :] += dot(vals[slot], blocks[block_rows(slot), :])
         return carry
 
     lax.fori_loop(0, chunks, add_chunk, 0)
+    for copy in later:
+        copy.wait()
 
     outs = (output_ref, grads_ref, y_ref)
     for i in range(steps):
-        rows = pl.ds(i * ROWS_STEP, ROWS_STEP)
-        y = total[rows, :].astype(jnp.bfloat16)
+        start = i * ROWS_STEP
+        rows = pl.ds(start, ROWS_STEP)
+        summed = total[rows, :]
+        if start < rim:
+            summed = summed + low[rows, :].astype(jnp.float32)
+        if start >= count - rim:
+            edge = pl.ds(start - (count - rim), ROWS_STEP)
+            summed = summed + high[edge, :].astype(jnp.float32)
+        y = summed.astype(jnp.bfloat16)
         kept[2, rows, :] = y
-        preact = dot(y, weight_ref[...])
+        preact = dot(y, weight[...])
         sigma = jax.nn.sigmoid(preact)
         kept[0, rows, :] = (preact * sigma).astype(jnp.bfloat16)
         slope = sigma * (1.0 + preact * (1.0 - sigma))
-        kept[1, rows, :] = (grad_ref[rows, :].astype(jnp.float32) * slope).astype(jnp.bfloat16)
+        kept[1, rows, :] = (grad[rows, :].astype(jnp.float32) * slope).astype(jnp.bfloat16)
         for k in range(3):
             pltpu.make_async_copy(kept.at[k, rows], outs[k].at[rows], out_sems.at[k]).start()
 
-    def back_chunk(i, carry):
-        for j in range(slots):
-            slot = i * slots + j
-            rows = block_rows(target_ref[slot])
-            term = dot_ta(vals_ref[slot], kept[1, rows, :])
-            blocks[block_rows(slot), :] = term.astype(jnp.bfloat16)
-        rows = pl.ds(pl.multiple_of(i * CHUNK, CHUNK), CHUNK)
-        pltpu.make_async_copy(blocks.at[rows], terms_ref.at[rows], out_sems.at[3]).start()
-        return carry
-
-    lax.fori_loop(0, chunks, back_chunk, 0)
+    send_terms(0, cap, target_ref, kept.at[1], vals, blocks, terms_ref, out_sems.at[3])
     for k in range(3):
         pltpu.make_async_copy(kept.at[k], outs[k], out_sems.at[k]).wait()
-    pltpu.make_async_copy(blocks, terms_ref, out_sems.at[3]).wait()
-
-
-def middle(target, arrived, vals, band, low, high, weight, grad_out):
+    pltpu.make_async_copy(terms_ref, terms_ref, out_sems.at[3]).wait()
+
+
+def middle(cap, target, arrived, vals, band, low, high, weight, grad_out):
     rows, features = grad_out.shape
     out = jax.ShapeDtypeStruct((rows, features), jnp.bfloat16)
-    return pl.pallas_call(
-        middle_kernel,
-        in_specs=[SMEM, HBM] + [VMEM] * 6,
+    same = lambda v: pltpu.VMEM(v.shape, v.dtype)
+    return pl.pallas_call(
+        functools.partial(middle_kernel, cap),
+        in_specs=[SMEM] + [HBM] * 3 + [ANY] * 2 + [HBM] * 2,
         out_specs=[HBM] * 4,
-        out_shape=[out] * 3 + [jax.ShapeDtypeStruct(arrived.shape, jnp.bfloat16)],
+        out_shape=[out] * 3 + [jax.ShapeDtypeStruct((arrived.shape[0] // cap, features), jnp.bfloat16)],
         scratch_shapes=[
-            pltpu.VMEM(arrived.shape, jnp.bfloat16),
-            pltpu.VMEM((rows, features), jnp.float32),
+            *(same(v) for v in (arrived, vals, band, low, high, weight, grad_out)),
             pltpu.VMEM((3, rows, features), jnp.bfloat16),
             pltpu.SemaphoreType.DMA((arrived.shape[0] // CHUNK,)),
+            pltpu.SemaphoreType.DMA((6,)),
             pltpu.SemaphoreType.DMA((4,)),
         ],
         compiler_params=params(),
@@ -300,7 +336,56 @@
     )(target, arrived, vals, band, low, high, weight, grad_out)
 
 
-def tail_kernel(
+def back_kernel(s, cap, target_ref, grads_ref, vals_ref, terms_ref, grads, vals, blocks, sems, sem):
+    for copy in fetches((grads_ref, vals_ref), (grads, vals), sems):
+        copy.wait()
+    send_terms(s, cap, target_ref, grads, vals, blocks, terms_ref, sem)
+    pltpu.make_async_copy(blocks, terms_ref, sem).wait()
+
+
+def back_terms(s, cap, target, grads, vals):
+    shape = (vals.shape[0] // cap * BLK, grads.shape[1])
+    return pl.pallas_call(
+        functools.partial(back_kernel, s, cap),
+        in_specs=[SMEM, HBM, HBM],
+        out_specs=HBM,
+        out_shape=jax.ShapeDtypeStruct(shape, jnp.bfloat16),
+        scratch_shapes=[
+            pltpu.VMEM(grads.shape, grads.dtype),
+            pltpu.VMEM(vals.shape, vals.dtype),
+            pltpu.VMEM(shape, jnp.bfloat16),
+            pltpu.SemaphoreType.DMA((2,)),
+            pltpu.SemaphoreType.DMA,
+        ],
+        compiler_params=params(),
+        cost_estimate=pl.CostEstimate(
+            flops=2 * vals.size * shape[1] // cap, bytes_accessed=8 << 20, transcendentals=0
+        ),
+        name="back_terms",
+    )(target, grads, vals)
+
+
+def add_back(s, cap, index_ref, count_ref, back_ref, back, sems, total):
+    group = CHUNK // BLK
+
+    def chunk(i, carry):
+        rows = pl.ds(pl.multiple_of(i * CHUNK, CHUNK), CHUNK)
+        pltpu.make_async_copy(back_ref.at[rows], back.at[rows], sems.at[i]).wait()
+        for j in range(group):
+            peer = i * group + j
+
+            @pl.when(s < count_ref[peer])
+            def _():
+                rows = block_rows(index_ref[peer * cap + s])
+                total[rows, :] += back[block_rows(peer), :].astype(jnp.float32)
+
+        return carry
+
+    lax.fori_loop(0, back.shape[0] // CHUNK, chunk, 0)
+
+
+def sum_kernel(
+    s,
     cap,
     index_ref,
     count_ref,
@@ -308,65 +393,103 @@
     band_ref,
     low_ref,
     high_ref,
+    out_ref,
+    back,
+    total,
+    low,
+    high,
+    sems,
+    sem,
+):
+    rim = low.shape[0]
+    first = fetches((band_ref, low_ref, high_ref), (total, low, high), sem)
+    for i in range(back.shape[0] // CHUNK):
+        chunk_copy(back_ref, back, sems, i).start()
+    for copy in first:
+        copy.wait()
+    total[pl.ds(0, rim), :] += low[...].astype(jnp.float32)
+    total[pl.ds(total.shape[0] - rim, rim), :] += high[...].astype(jnp.float32)
+    add_back(s, cap, index_ref, count_ref, back_ref, back, sems, total)
+    out = pltpu.make_async_copy(total, out_ref, sem.at[0])
+    out.start()
+    out.wait()
+
+
+def sum_back(s, cap, index, count, back, band, low, high):
+    return pl.pallas_call(
+        functools.partial(sum_kernel, s, cap),
+        in_specs=[SMEM] * 2 + [HBM] * 2 + [ANY] * 2,
+        out_specs=HBM,
+        out_shape=jax.ShapeDtypeStruct(band.shape, jnp.float32),
+        scratch_shapes=[
+            *(pltpu.VMEM(v.shape, v.dtype) for v in (back, band, low, high)),
+            pltpu.SemaphoreType.DMA((back.shape[0] // CHUNK,)),
+            pltpu.SemaphoreType.DMA((3,)),
+        ],
+        compiler_params=params(),
+        cost_estimate=pl.CostEstimate(
+            flops=band.size, bytes_accessed=12 << 20, transcendentals=0
+        ),
+        name="sum_back",
+    )(index, count, back, band, low, high)
+
+
+def tail_kernel(
+    s,
+    cap,
+    index_ref,
+    count_ref,
+    back_ref,
+    sum_ref,
     weight_ref,
     out_ref,
     back,
     total,
+    weight,
     kept,
-    in_sems,
+    back_sems,
+    sems,
     sem,
 ):
-    chunks = back_ref.shape[0] // CHUNK
-    steps = total.shape[0] // ROWS_STEP
-    for i in range(chunks):
-        rows = pl.ds(i * CHUNK, CHUNK)
-        pltpu.make_async_copy(back_ref.at[rows], back.at[rows], in_sems.at[i]).start()
-    start_total(total, band_ref, low_ref, high_ref)
-
-    def add_chunk(i, carry):
-        rows = pl.ds(pl.multiple_of(i * CHUNK, CHUNK), CHUNK)
-        pltpu.make_async_copy(back_ref.at[rows], back.at[rows], in_sems.at[i]).wait()
-        for j in range(CHUNK // BLK):
-            slot = i * (CHUNK // BLK) + j
-
-            @pl.when(lax.rem(slot, cap) < count_ref[slot // cap])
-            def _():
-                rows = block_rows(index_ref[slot])
-                total[rows, :] += back[block_rows(slot), :].astype(jnp.float32)
-
-        return carry
-
-    lax.fori_loop(0, chunks, add_chunk, 0)
-    for i in range(steps):
+    first = fetches((sum_ref,), (total,), sems)
+    for i in range(back.shape[0] // CHUNK):
+        chunk_copy(back_ref, back, back_sems, i).start()
+    later = fetches((weight_ref,), (weight,), sems.at[pl.ds(1, 1)])
+    for copy in first:
+        copy.wait()
+    add_back(s, cap, index_ref, count_ref, back_ref, back, back_sems, total)
+    for copy in later:
+        copy.wait()
+    for i in range(total.shape[0] // ROWS_STEP):
         rows = pl.ds(i * ROWS_STEP, ROWS_STEP)
         grad_z = total[rows, :].astype(jnp.bfloat16)
-        kept[rows, :] = dot(grad_z, weight_ref[...]).astype(jnp.bfloat16)
+        kept[rows, :] = dot(grad_z, weight[...]).astype(jnp.bfloat16)
         pltpu.make_async_copy(kept.at[rows], out_ref.at[rows], sem).start()
     pltpu.make_async_copy(kept, out_ref, sem).wait()
 
 
-def tail(index, count, cap, back, band, low, high, weight_t):
-    rows, features = band.shape
-    return pl.pallas_call(
-        functools.partial(tail_kernel, cap),
-        in_specs=[SMEM, SMEM, HBM] + [VMEM] * 4,
+def tail(s, cap, index, count, back, so_far, weight_t):
+    same = lambda v: pltpu.VMEM(v.shape, v.dtype)
+    return pl.pallas_call(
+        functools.partial(tail_kernel, s, cap),
+        in_specs=[SMEM] * 2 + [HBM] * 3,
         out_specs=HBM,
-        out_shape=jax.ShapeDtypeStruct((rows, features), jnp.bfloat16),
+        out_shape=jax.ShapeDtypeStruct(so_far.shape, jnp.bfloat16),
         scratch_shapes=[
-            pltpu.VMEM(back.shape, jnp.bfloat16),
-            pltpu.VMEM((rows, features), jnp.float32),
-            pltpu.VMEM((rows, features), jnp.bfloat16),
+            *(same(v) for v in (back, so_far, weight_t)),
+            pltpu.VMEM(so_far.shape, jnp.bfloat16),
             pltpu.SemaphoreType.DMA((back.shape[0] // CHUNK,)),
+            pltpu.SemaphoreType.DMA((2,)),
             pltpu.SemaphoreType.DMA,
         ],
         compiler_params=params(),
         cost_estimate=pl.CostEstimate(
-            flops=2 * band.size * features,
-            bytes_accessed=2 * back.size + 6 * band.size,
+            flops=2 * so_far.size * weight_t.shape[1],
+            bytes_accessed=2 * back.size + 6 * so_far.size,
             transcendentals=0,
         ),
         name="tail",
-    )(index, count, back, band, low, high, weight_t)
+    )(index, count, back, so_far, weight_t)
 
 
 def exchange(blocks):
@@ -423,14 +546,13 @@
         )
 
 
-def gather_sum(v, core, cell):
-    rows, features = v.shape
-    parts = [v] + [within(v, 0, s) for s in (1, 2, 3)]
+def gather_sum(parts, core, cell):
+    rows, features = parts[0].shape
     mine = pl.pallas_call(
         put_kernel,
         in_specs=[SMEM] + [VMEM] * 4,
         out_specs=VMEM,
-        out_shape=jax.ShapeDtypeStruct((4 * rows, features), v.dtype),
+        out_shape=jax.ShapeDtypeStruct((4 * rows, features), parts[0].dtype),
         compiler_params=params(),
         name="put_parts",
     )(cell[None], *parts)
@@ -456,24 +578,32 @@
     cell = lax.axis_index("cell")
 
     arrived = exchange(gather_blocks(x, far_send[0, 0].T, far_count[0]))
-    low, high = neighbour_terms(x, band)
+    low, high = to_neighbours(*rim_terms(x, band))
     band_part = band_sum(x, band)
     output, grads, y, terms = middle(
-        target_index, arrived, vals, band_part, low, high, weight, grad_out[0]
+        cap, target_index, arrived, vals, band_part, low, high, weight, grad_out[0]
     )
+
+    so_far = exchange(terms)
+    rims = rim_terms(grads, band)
+    rims, y = lax.optimization_barrier((rims, y))
+    low, high = to_neighbours(*rims)
+    part = scatter_sum(dot_ta(y, grads), core, cell)
+    terms = back_terms(1, cap, target_index, grads, vals)
+    part, terms = lax.optimization_barrier((part, terms))
+    for kind in ("x", "y"):
+        sent = part.astype(jnp.bfloat16)
+        part = part + sum(shift(sent, kind, s).astype(jnp.float32) for s in (1, 2, 3))
+    terms, so_far, part, low, high, grads = lax.optimization_barrier(
+        (terms, so_far, part, low, high, grads)
+    )
+
     came_back = exchange(terms)
-    low, high = neighbour_terms(grads, band)
-    part = scatter_sum(dot_ta(y, grads), core, cell)
-    back_band = band_sum(grads, band)
-    part, back_band = lax.optimization_barrier((part, back_band))
+    so_far = sum_back(0, cap, send_index, count, so_far, band_sum(grads, band), low, high)
     sent = part.astype(jnp.bfloat16)
-    part = part + sum(shift(sent, "y", s).astype(jnp.float32) for s in (1, 2, 3))
-    sent = part.astype(jnp.bfloat16)
-    moved_on = [shift(sent, "x", s) for s in (1, 2, 3)]
-    grad_in = tail(send_index, count, cap, came_back, back_band, low, high, weight.T)
-    moved_on, grad_in = lax.optimization_barrier((moved_on, grad_in))
-    part = part + sum(v.astype(jnp.float32) for v in moved_on)
-    grad_weight = gather_sum(part.astype(jnp.bfloat16), core, cell)
+    grad_weight = gather_sum([sent] + [within(sent, 0, s) for s in (1, 2, 3)], core, cell)
+    came_back, so_far, grad_weight = lax.optimization_barrier((came_back, so_far, grad_weight))
+    grad_in = tail(1, cap, send_index, count, came_back, so_far, weight.T)
     return (output[None], grad_in[None], grad_weight)
 
 

time: 281 us -> 271 us (0.964)
  waiting for transfers between devices: 148 us -> 120 us
  Pallas kernels: 59 us -> 73.1 us
    ppermute x6, waiting for transfers between devices: 60.3 us -> 20.6 us  [shift(): lax.ppermute(v, 'genome', [(i, moved(i, kind, s)) for i in range(32)])]
    all_to_all x2 -> x3, waiting for transfers between devices: 0.01 us -> 13.1 us  [exchange(): return lax.all_to_all(cut, 'genome', 0, 0, tiled=True).reshape(blocks.shape)]
    pallas_call x2 -> x4, Pallas kernels: 22.6 us -> 30.3 us  [the longest x1 11.7 us: middle(): pl.pallas_call(functools.partial(middle_kernel, cap), in_specs=[SMEM] + [...]
    all_to_all x2 -> x3, starting transfers between devices: 18.7 us -> 23.7 us  [exchange(): return lax.all_to_all(cut, 'genome', 0, 0, tiled=True).reshape(blocks.shape)]
    ppermute x6, starting transfers between devices: 11.8 us -> 8.9 us  [shift(): lax.ppermute(v, 'genome', [(i, moved(i, kind, s)) for i in range(32)])]
    unnamed x25 -> x29, local copies, waits for them, and re-layouts: 7.8 us -> 4.91 us
  transfers between devices with their start and end apart: 23 -> 24, of which waited for: 8 -> 10; matrix products, arithmetic and copies ran while one was open for 2% -> 3% of each run, Pallas kernels for 14% -> 19%
where the time goes in v3:
time: 271 us; the launch traced here: 268 us
  waiting for transfers between devices  120 us (44%)
  Pallas kernels  73.1 us (27%)
  starting transfers between devices  61.5 us (23%)
  local copies, waits for them, and re-layouts  7 us (3%)
  matrix products  3.49 us (1%)
    ppermute x2, waiting for transfers between devices, to_neighbours(): lax.ppermute(high, 'genome', forward)  76.9 us
    pallas_call x2, Pallas kernels, band_sum(): pl.pallas_call(band_kernel, grid=(band.shape[0],), in_specs=[pl.BlockSpec...  26.7 us
    all_to_all x3, starting transfers between devices, exchange(): return lax.all_to_all(cut, 'genome', 0, 0, tiled=True).reshape(blocks.shape)  23.7 us
    ppermute x6, waiting for transfers between devices, shift(): lax.ppermute(v, 'genome', [(i, moved(i, kind, s)) for i in range(32)])  20.6 us
    ppermute x11, starting transfers between devices, within(): return lax.ppermute(v, ('genome', 'cell'), pairs)  17.2 us
    all_to_all x3, waiting for transfers between devices, exchange(): return lax.all_to_all(cut, 'genome', 0, 0, tiled=True).reshape(blocks.shape)  13.1 us
    pallas_call x1, Pallas kernels, middle(): pl.pallas_call(functools.partial(middle_kernel, cap), in_specs=[SMEM] + [...  11.7 us
    ppermute x6, starting transfers between devices, shift(): lax.ppermute(v, 'genome', [(i, moved(i, kind, s)) for i in range(32)])  8.9 us
  transfers between devices with their start and end apart: 24, of which 10 were waited for; matrix products, arithmetic and copies ran while one was open for 3% of the time, Pallas kernels for 19%

profile of v3, /device:TPU:1, one launch (start us, length us, event | category | flops | bytes accessed | tf_op | source)
XLA Modules:
  0.0 267.7 jit_solution(9268821373980311906)
XLA Ops:
  0.6 4.8 %gather_blocks.1 = bf16[8192,512]{1,0:T(8,128)(2,1)} custom-call(s32[2,32]{1,0:T(2,128)} %bitcast.46, s32[1,32]{1,0:T(1,128)} %bitcast.43, bf16[2048,512]{1,0:T(8,128)(2,1)} %bitcast.33), custom_call_target="tpu_custom_call" | custom-call | bytes 10485760 | tf_op jit(solution)/shard_map/gather_blocks/pallas_call | solution.py:87
  5.4 8.7 %all-to-all-start = ((bf16[32,256,512]{2,1,0:T(8,128)(2,1)}), bf16[32,256,512]{2,1,0:T(8,128)(2,1)}, u32[]{:S(2)}, u32[]{:S(2)}) async-start(bf16[32,256,512]{2,1,0:T(8,128)(2,1)} %bitcast.32), calls=%async_computation | async-start | bytes 16777216 | tf_op jit(solution)/shard_map/all_to_all | solution.py:498
  14.1 3.8 %rim_terms.2 = (bf16[512,512]{1,0:T(8,128)(2,1)}, bf16[512,512]{1,0:T(8,128)(2,1)}) custom-call(bf16[2048,512]{1,0:T(8,128)(2,1)} %bitcast.34, bf16[16,9,128,128]{3,2,1,0:T(8,128)(2,1)} %bitcast.26, bf16[16,9,128,128]{3,2,1,0:T(8,128)(2,1)} %bitcast.27), custom_call_target="tpu_custom_call" | custom-call | flops 335544320 | bytes 6291456 | tf_op jit(solution)/shard_map/rim_terms/pallas_call | solution.py:176
  17.9 3.5 %collective-permute-start = (bf16[512,512]{1,0:T(8,128)(2,1)}, bf16[512,512]{1,0:T(8,128)(2,1)S(1)}, u32[]{:S(2)}, u32[]{:S(2)}) collective-permute-start(bf16[512,512]{1,0:T(8,128)(2,1)} %get-tuple-element.25), channel_id=1, source_target_pairs={{0,4},{4,8},{8,12},{12,16},{16,20},{20,24},{24,28},{28,32},{32,36}... | collective-permute-start | bytes 1572872 | tf_op jit(solution)/shard_map/ppermute | solution.py:198
  21.4 1.9 collective-permute-start.1
  24.1 13.3 %band_sum.2.band_ref = f32[2048,512]{1,0:T(8,128)} custom-call(bf16[2048,512]{1,0:T(8,128)(2,1)} %bitcast.35, bf16[16,9,128,128]{3,2,1,0:T(8,128)(2,1)} %bitcast.28), custom_call_target="tpu_custom_call" | custom-call | flops 2415919104 | bytes 11010048 | tf_op jit(solution)/shard_map/band_sum/pallas_call | solution.py:135
  37.5 76.9 %collective-permute-done.low_ref = bf16[512,512]{1,0:T(8,128)(2,1)S(1)} collective-permute-done((bf16[512,512]{1,0:T(8,128)(2,1)}, bf16[512,512]{1,0:T(8,128)(2,1)S(1)}, u32[]{:S(2)}, u32[]{:S(2)}) %collective-permute-start) | collective-permute-done | bytes 524320 | tf_op jit(solution)/shard_map/ppermute | solution.py:198
  114.3 4.9 %collective-permute-done.1.high_ref = bf16[512,512]{1,0:T(8,128)(2,1)S(1)} collective-permute-done((bf16[512,512]{1,0:T(8,128)(2,1)}, bf16[512,512]{1,0:T(8,128)(2,1)S(1)}, u32[]{:S(2)}, u32[]{:S(2)}) %collective-permute-start.1) | collective-permute-done | bytes 524320 | tf_op jit(solution)/shard_map/ppermute | solution.py:198
  120.0 11.7 %middle.1 = (bf16[2048,512]{1,0:T(8,128)(2,1)}, bf16[2048,512]{1,0:T(8,128)(2,1)}, bf16[2048,512]{1,0:T(8,128)(2,1)}, bf16[4096,512]{1,0:T(8,128)(2,1)}) custom-call(s32[64]{0:T(128)} %reshape.36.target_ref, bf16[8192,512]{1,0:T(8,128)(2,1)} %bitcast.5.arrived_ref, bf16[64,128,128]{2,1,0:T(8,128)(2,1)} %bitcast.37, f32[2048,512]{1,0:T(8,128)} %band_sum.2.band_ref, ...), custom_call_target="tpu_custom_call" | custom-call | flops 3221225472 | bytes 31457280 | tf_op jit(solution)/shard_map/middle/pallas_call | solution.py:317
  131.7 10.1 %all-to-all-start.1 = ((bf16[32,128,512]{2,1,0:T(8,128)(2,1)}), bf16[32,128,512]{2,1,0:T(8,128)(2,1)}, u32[]{:S(2)}, u32[]{:S(2)}) async-start(bf16[32,128,512]{2,1,0:T(8,128)(2,1)} %bitcast.39), calls=%async_computation.1 | async-start | bytes 8388608 | tf_op jit(solution)/shard_map/all_to_all | solution.py:498
  141.9 3.8 %rim_terms.3 = (bf16[512,512]{1,0:T(8,128)(2,1)}, bf16[512,512]{1,0:T(8,128)(2,1)}) custom-call(bf16[2048,512]{1,0:T(8,128)(2,1)} %get-tuple-element.40.v_ref.grads_ref, bf16[16,9,128,128]{3,2,1,0:T(8,128)(2,1)} %bitcast.29, bf16[16,9,128,128]{3,2,1,0:T(8,128)(2,1)} %bitcast.30), custom_call_target="tpu_custom_call" | custom-call | flops 335544320 | bytes 6291456 | tf_op jit(solution)/shard_map/rim_terms/pallas_call | solution.py:176
  145.7 3.5 %fusion.1 = f32[512,512]{1,0:T(8,128)S(1)} fusion(bf16[2048,512]{1,0:T(8,128)(2,1)} %get-tuple-element.32, bf16[2048,512]{1,0:T(8,128)(2,1)} %get-tuple-element.40.v_ref.grads_ref), kind=kOutput, calls=%fused_computation.11 | convolution fusion | flops 1073741824 | bytes 5242880 | tf_op jit(solution)/shard_map/dot_general | solution.py:32
  151.7 3.3 %collective-permute-start.3 = (f32[64,512]{1,0:T(8,128)S(1)}, f32[64,512]{1,0:T(8,128)S(1)}, u32[]{:S(2)}, u32[]{:S(2)}) collective-permute-start(f32[64,512]{1,0:T(8,128)S(1)} %get-tuple-element.53), channel_id=1, source_target_pairs={{0,2},{1,3},{2,0},{3,1},{4,6},{5,7},{6,4},{7,5},{8,10},{9,11},{10,... | collective-permute-start | bytes 393224 | tf_op jit(solution)/shard_map/ppermute | solution.py:518
  157.5 1.9 collective-permute-start.7
  159.4 1.8 collective-permute-done.3
  162.2 5.4 %back_terms.1 = bf16[4096,512]{1,0:T(8,128)(2,1)} custom-call(s32[64]{0:T(128)} %reshape.36.target_ref, bf16[2048,512]{1,0:T(8,128)(2,1)} %get-tuple-element.40.v_ref.grads_ref, bf16[64,128,128]{2,1,0:T(8,128)(2,1)} %bitcast.38), custom_call_target="tpu_custom_call" | custom-call | flops 536870912 | bytes 8388608 | tf_op jit(solution)/shard_map/back_terms/pallas_call | solution.py:348
  169.0 3.0 %collective-permute-start.10 = (bf16[64,512]{1,0:T(8,128)(2,1)S(1)}, bf16[64,512]{1,0:T(8,128)(2,1)S(1)}, u32[]{:S(2)}, u32[]{:S(2)}) collective-permute-start(bf16[64,512]{1,0:T(8,128)(2,1)S(1)} %convert_element_type.27), channel_id=1, source_target_pairs={{0,16},{4,20},{8,24},{12,28},{16,0},{20,4},{24,8},{28,12},{32,48},... | collective-permute-start | bytes 196616 | tf_op jit(solution)/shard_map/ppermute | solution.py:511
  173.4 4.4 %collective-permute-start.15 = (bf16[512,512]{1,0:T(8,128)(2,1)}, bf16[512,512]{1,0:T(8,128)(2,1)S(1)}, u32[]{:S(2)}, u32[]{:S(2)}) collective-permute-start(bf16[512,512]{1,0:T(8,128)(2,1)} %get-tuple-element.36), channel_id=1, source_target_pairs={{0,4},{4,8},{8,12},{12,16},{16,20},{20,24},{24,28},{28,32},{32,36}... | collective-permute-start | bytes 1572872 | tf_op jit(solution)/shard_map/ppermute | solution.py:198
  177.8 1.9 collective-permute-start.16
  179.7 14.3 %collective-permute-done.10 = bf16[64,512]{1,0:T(8,128)(2,1)S(1)} collective-permute-done((bf16[64,512]{1,0:T(8,128)(2,1)S(1)}, bf16[64,512]{1,0:T(8,128)(2,1)S(1)}, u32[]{:S(2)}, u32[]{:S(2)}) %collective-permute-start.10) | collective-permute-done | bytes 65568 | tf_op jit(solution)/shard_map/ppermute | solution.py:511
  194.1 1.8 collective-permute-start.12
  195.9 2.2 collective-permute-start.13
  199.9 4.9 %collective-permute-done.13 = bf16[64,512]{1,0:T(8,128)(2,1)S(1)} collective-permute-done((bf16[64,512]{1,0:T(8,128)(2,1)S(1)}, bf16[64,512]{1,0:T(8,128)(2,1)S(1)}, u32[]{:S(2)}, u32[]{:S(2)}) %collective-permute-start.13) | collective-permute-done | bytes 65568 | tf_op jit(solution)/shard_map/ppermute | solution.py:511
  205.9 4.9 %all-to-all-start.2 = ((bf16[32,128,512]{2,1,0:T(8,128)(2,1)}), bf16[32,128,512]{2,1,0:T(8,128)(2,1)}, u32[]{:S(2)}, u32[]{:S(2)}) async-start(bf16[32,128,512]{2,1,0:T(8,128)(2,1)} %bitcast.36), calls=%async_computation.2 | async-start | bytes 8388608 | tf_op jit(solution)/shard_map/all_to_all | solution.py:498
  212.5 3.3 %collective-permute-start.18 = (bf16[64,512]{1,0:T(8,128)(2,1)S(1)}, bf16[64,512]{1,0:T(8,128)(2,1)S(1)}, u32[]{:S(2)}, u32[]{:S(2)}) collective-permute-start(bf16[64,512]{1,0:T(8,128)(2,1)S(1)} %add_add_fusion.refs_0_), channel_id=1, source_target_pairs={{0,2},{1,3},{2,0},{3,1},{4,6},{5,7},{6,4},{7,5},{8,10},{9,11},{10,... | collective-permute-start | bytes 196616 | tf_op jit(solution)/shard_map/ppermute | solution.py:518
  216.8 2.3 collective-permute-done.18.refs_2_
  221.6 1.7 collective-permute-start.20
  225.1 13.3 %band_sum.3.band_ref = f32[2048,512]{1,0:T(8,128)} custom-call(bf16[2048,512]{1,0:T(8,128)(2,1)} %get-tuple-element.40.v_ref.grads_ref, bf16[16,9,128,128]{3,2,1,0:T(8,128)(2,1)} %bitcast.31), custom_call_target="tpu_custom_call" | custom-call | flops 2415919104 | bytes 11010048 | tf_op jit(solution)/shard_map/band_sum/pallas_call | solution.py:135
  238.5 6.8 %sum_back.1.sum_ref = f32[2048,512]{1,0:T(8,128)} custom-call(s32[64]{0:T(128)} %reshape.40.index_ref, s32[32]{0:T(128)} %bitcast.44, bf16[4096,512]{1,0:T(8,128)(2,1)} %bitcast.12.back_ref, f32[2048,512]{1,0:T(8,128)} %band_sum.3.band_ref, bf16[512,512]{1,0:T(8,128)(2,1)} %copy-done.1, bf16[512,512]{1,0:T(8,128)(2,1)} %copy-done.2), custom_call_target="tpu_custom_call" | custom-call | flops 1048576 | bytes 12582912 | tf_op jit(solution)/shard_map/sum_back/pallas_call | solution.py:419
  246.0 2.1 join_halves.1
  248.1 13.1 %all-to-all-done.2 = bf16[32,128,512]{2,1,0:T(8,128)(2,1)} async-done(((bf16[32,128,512]{2,1,0:T(8,128)(2,1)}), bf16[32,128,512]{2,1,0:T(8,128)(2,1)}, u32[]{:S(2)}, u32[]{:S(2)}) %all-to-all-start.2) | async-done | bytes 4194336 | tf_op jit(solution)/shard_map/all_to_all | solution.py:498
  261.2 6.4 %tail.1 = bf16[2048,512]{1,0:T(8,128)(2,1)} custom-call(s32[64]{0:T(128)} %reshape.40.index_ref, s32[32]{0:T(128)} %bitcast.45, bf16[4096,512]{1,0:T(8,128)(2,1)} %bitcast.14.back_ref, f32[2048,512]{1,0:T(8,128)} %sum_back.1.sum_ref, bf16[512,512]{1,0:T(8,128)(2,1)} %bitcast.40), custom_call_target="tpu_custom_call" | custom-call | flops 1073741824 | bytes 10485760 | tf_op jit(solution)/shard_map/tail/pallas_call | solution.py:473
  (64 shorter events, 20.9 us)
Async XLA Ops:
  5.4 113.8 %all-to-all-start = ((bf16[32,256,512]{2,1,0:T(8,128)(2,1)}), bf16[32,256,512]{2,1,0:T(8,128)(2,1)}, u32[]{:S(2)}, u32[]{:S(2)}) async-start(bf16[32,256,512]{2,1,0:T(8,128)(2,1)} %bitcast.32), calls=%async_computation | async-start | bytes 16777216 | tf_op jit(solution)/shard_map/all_to_all | solution.py:498
  14.1 9.3 %copy-start.12 = (s32[1,1,32,2]{2,3,1,0:T(2,128)S(1)}, s32[1,1,32,2]{2,3,1,0:T(2,128)}, u32[]{:S(2)}) copy-start(s32[1,1,32,2]{2,3,1,0:T(2,128)} %param.11) | copy-start | bytes 772
  17.9 96.4 %collective-permute-start = (bf16[512,512]{1,0:T(8,128)(2,1)}, bf16[512,512]{1,0:T(8,128)(2,1)S(1)}, u32[]{:S(2)}, u32[]{:S(2)}) collective-permute-start(bf16[512,512]{1,0:T(8,128)(2,1)} %get-tuple-element.25), channel_id=1, source_target_pairs={{0,4},{4,8},{8,12},{12,16},{16,20},{20,24},{24,28},{28,32},{32,36}... | collective-permute-start | bytes 1572872 | tf_op jit(solution)/shard_map/ppermute | solution.py:198
  21.4 97.8 %collective-permute-start.1 = (bf16[512,512]{1,0:T(8,128)(2,1)}, bf16[512,512]{1,0:T(8,128)(2,1)S(1)}, u32[]{:S(2)}, u32[]{:S(2)}) collective-permute-start(bf16[512,512]{1,0:T(8,128)(2,1)} %get-tuple-element.26), channel_id=1, source_target_pairs={{4,0},{8,4},{12,8},{16,12},{20,16},{24,20},{28,24},{32,28},{36,32}... | collective-permute-start | bytes 1572872 | tf_op jit(solution)/shard_map/ppermute | solution.py:198
  114.3 4.9 %copy-start.3 = (bf16[512,512]{1,0:T(8,128)(2,1)}, bf16[512,512]{1,0:T(8,128)(2,1)S(1)}, u32[]{:S(2)}) copy-start(bf16[512,512]{1,0:T(8,128)(2,1)S(1)} %collective-permute-done.low_ref) | copy-start | bytes 1572868
  131.7 73.2 %all-to-all-start.1 = ((bf16[32,128,512]{2,1,0:T(8,128)(2,1)}), bf16[32,128,512]{2,1,0:T(8,128)(2,1)}, u32[]{:S(2)}, u32[]{:S(2)}) async-start(bf16[32,128,512]{2,1,0:T(8,128)(2,1)} %bitcast.39), calls=%async_computation.1 | async-start | bytes 8388608 | tf_op jit(solution)/shard_map/all_to_all | solution.py:498
  150.0 7.5 %collective-permute-start.2 = (f32[64,512]{1,0:T(8,128)S(1)}, f32[64,512]{1,0:T(8,128)S(1)}, u32[]{:S(2)}, u32[]{:S(2)}) collective-permute-start(f32[64,512]{1,0:T(8,128)S(1)} %get-tuple-element.47), channel_id=1, source_target_pairs={{0,1},{1,2},{2,3},{3,0},{4,5},{5,6},{6,7},{7,4},{8,9},{9,10},{10,1... | collective-permute-start | bytes 393224 | tf_op jit(solution)/shard_map/ppermute | solution.py:518
  151.7 9.5 %collective-permute-start.3 = (f32[64,512]{1,0:T(8,128)S(1)}, f32[64,512]{1,0:T(8,128)S(1)}, u32[]{:S(2)}, u32[]{:S(2)}) collective-permute-start(f32[64,512]{1,0:T(8,128)S(1)} %get-tuple-element.53), channel_id=1, source_target_pairs={{0,2},{1,3},{2,0},{3,1},{4,6},{5,7},{6,4},{7,5},{8,10},{9,11},{10,... | collective-permute-start | bytes 393224 | tf_op jit(solution)/shard_map/ppermute | solution.py:518
  155.0 12.6 %collective-permute-start.4 = (f32[64,512]{1,0:T(8,128)}, f32[64,512]{1,0:T(8,128)}, u32[]{:S(2)}, u32[]{:S(2)}) collective-permute-start(f32[64,512]{1,0:T(8,128)} %get-tuple-element.52), channel_id=1, source_target_pairs={{0,3},{1,0},{2,1},{3,2},{4,7},{5,4},{6,5},{7,6},{8,11},{9,8},{10,9... | collective-permute-start | bytes 393224 | tf_op jit(solution)/shard_map/ppermute | solution.py:518
  155.7 11.9 %collective-permute-start.5 = (f32[64,512]{1,0:T(8,128)}, f32[64,512]{1,0:T(8,128)}, u32[]{:S(2)}, u32[]{:S(2)}) collective-permute-start(f32[64,512]{1,0:T(8,128)} %get-tuple-element.51), channel_id=1, source_target_pairs={{0,4},{1,5},{2,6},{3,7},{4,0},{5,1},{6,2},{7,3},{8,12},{9,13},{10,... | collective-permute-start | bytes 393224 | tf_op jit(solution)/shard_map/ppermute | solution.py:518
  156.9 10.8 %collective-permute-start.6 = (f32[64,512]{1,0:T(8,128)S(1)}, f32[64,512]{1,0:T(8,128)}, u32[]{:S(2)}, u32[]{:S(2)}) collective-permute-start(f32[64,512]{1,0:T(8,128)S(1)} %get-tuple-element.50), channel_id=1, source_target_pairs={{0,5},{1,6},{2,7},{3,4},{4,1},{5,2},{6,3},{7,0},{8,13},{9,14},{10,... | collective-permute-start | bytes 393224 | tf_op jit(solution)/shard_map/ppermute | solution.py:518
  157.5 10.1 %collective-permute-start.7 = (f32[64,512]{1,0:T(8,128)S(1)}, f32[64,512]{1,0:T(8,128)}, u32[]{:S(2)}, u32[]{:S(2)}) collective-permute-start(f32[64,512]{1,0:T(8,128)S(1)} %get-tuple-element.49), channel_id=1, source_target_pairs={{0,6},{1,7},{2,4},{3,5},{4,2},{5,3},{6,0},{7,1},{8,14},{9,15},{10,... | collective-permute-start | bytes 393224 | tf_op jit(solution)/shard_map/ppermute | solution.py:518
  161.9 5.8 %collective-permute-start.8 = (f32[64,512]{1,0:T(8,128)S(1)}, f32[64,512]{1,0:T(8,128)}, u32[]{:S(2)}, u32[]{:S(2)}) collective-permute-start(f32[64,512]{1,0:T(8,128)S(1)} %get-tuple-element.48), channel_id=1, source_target_pairs={{0,7},{1,4},{2,5},{3,6},{4,3},{5,0},{6,1},{7,2},{8,15},{9,12},{10,... | collective-permute-start | bytes 393224 | tf_op jit(solution)/shard_map/ppermute | solution.py:518
  169.0 25.1 %collective-permute-start.10 = (bf16[64,512]{1,0:T(8,128)(2,1)S(1)}, bf16[64,512]{1,0:T(8,128)(2,1)S(1)}, u32[]{:S(2)}, u32[]{:S(2)}) collective-permute-start(bf16[64,512]{1,0:T(8,128)(2,1)S(1)} %convert_element_type.27), channel_id=1, source_target_pairs={{0,16},{4,20},{8,24},{12,28},{16,0},{20,4},{24,8},{28,12},{32,48},... | collective-permute-start | bytes 196616 | tf_op jit(solution)/shard_map/ppermute | solution.py:511
  172.0 22.1 %collective-permute-start.11 = (bf16[64,512]{1,0:T(8,128)(2,1)S(1)}, bf16[64,512]{1,0:T(8,128)(2,1)S(1)}, u32[]{:S(2)}, u32[]{:S(2)}) collective-permute-start(bf16[64,512]{1,0:T(8,128)(2,1)S(1)} %convert_element_type.27), channel_id=1, source_target_pairs={{0,24},{4,28},{8,0},{12,4},{16,8},{20,12},{24,16},{28,20},{32,56},... | collective-permute-start | bytes 196616 | tf_op jit(solution)/shard_map/ppermute | solution.py:511
  172.8 21.2 %collective-permute-start.9 = (bf16[64,512]{1,0:T(8,128)(2,1)S(1)}, bf16[64,512]{1,0:T(8,128)(2,1)S(1)}, u32[]{:S(2)}, u32[]{:S(2)}) collective-permute-start(bf16[64,512]{1,0:T(8,128)(2,1)S(1)} %convert_element_type.27), channel_id=1, source_target_pairs={{0,8},{4,12},{8,16},{12,20},{16,24},{20,28},{24,0},{28,4},{32,40},... | collective-permute-start | bytes 196616 | tf_op jit(solution)/shard_map/ppermute | solution.py:511
  173.4 31.4 %collective-permute-start.15 = (bf16[512,512]{1,0:T(8,128)(2,1)}, bf16[512,512]{1,0:T(8,128)(2,1)S(1)}, u32[]{:S(2)}, u32[]{:S(2)}) collective-permute-start(bf16[512,512]{1,0:T(8,128)(2,1)} %get-tuple-element.36), channel_id=1, source_target_pairs={{0,4},{4,8},{8,12},{12,16},{16,20},{20,24},{24,28},{28,32},{32,36}... | collective-permute-start | bytes 1572872 | tf_op jit(solution)/shard_map/ppermute | solution.py:198
  177.8 27.1 %collective-permute-start.16 = (bf16[512,512]{1,0:T(8,128)(2,1)}, bf16[512,512]{1,0:T(8,128)(2,1)S(1)}, u32[]{:S(2)}, u32[]{:S(2)}) collective-permute-start(bf16[512,512]{1,0:T(8,128)(2,1)} %get-tuple-element.37), channel_id=1, source_target_pairs={{4,0},{8,4},{12,8},{16,12},{20,16},{24,20},{28,24},{32,28},{36,32}... | collective-permute-start | bytes 1572872 | tf_op jit(solution)/shard_map/ppermute | solution.py:198
  194.1 5.8 %collective-permute-start.12 = (bf16[64,512]{1,0:T(8,128)(2,1)S(1)}, bf16[64,512]{1,0:T(8,128)(2,1)S(1)}, u32[]{:S(2)}, u32[]{:S(2)}) collective-permute-start(bf16[64,512]{1,0:T(8,128)(2,1)S(1)} %fusion), channel_id=1, source_target_pairs={{0,32},{4,36},{8,40},{12,44},{16,48},{20,52},{24,56},{28,60},{32,6... | collective-permute-start | bytes 196616 | tf_op jit(solution)/shard_map/ppermute | solution.py:511
  195.9 8.9 %collective-permute-start.13 = (bf16[64,512]{1,0:T(8,128)(2,1)S(1)}, bf16[64,512]{1,0:T(8,128)(2,1)S(1)}, u32[]{:S(2)}, u32[]{:S(2)}) collective-permute-start(bf16[64,512]{1,0:T(8,128)(2,1)S(1)} %fusion), channel_id=1, source_target_pairs={{0,64},{4,68},{8,72},{12,76},{16,80},{20,84},{24,88},{28,92},{32,9... | collective-permute-start | bytes 196616 | tf_op jit(solution)/shard_map/ppermute | solution.py:511
  198.1 6.7 %collective-permute-start.14 = (bf16[64,512]{1,0:T(8,128)(2,1)S(1)}, bf16[64,512]{1,0:T(8,128)(2,1)S(1)}, u32[]{:S(2)}, u32[]{:S(2)}) collective-permute-start(bf16[64,512]{1,0:T(8,128)(2,1)S(1)} %fusion), channel_id=1, source_target_pairs={{0,96},{4,100},{8,104},{12,108},{16,112},{20,116},{24,120},{28,124... | collective-permute-start | bytes 196616 | tf_op jit(solution)/shard_map/ppermute | solution.py:511
  204.9 11.0 %copy-start.5 = (bf16[64,512]{1,0:T(8,128)(2,1)}, bf16[64,512]{1,0:T(8,128)(2,1)S(1)}, u32[]{:S(2)}) copy-start(bf16[64,512]{1,0:T(8,128)(2,1)S(1)} %add_add_fusion.refs_0_) | copy-start | bytes 196612
  204.9 0.8 copy-start.1
  204.9 1.0 copy-start.2
  204.9 18.4 %copy-start.11 = (s32[1,1,32,2]{2,3,1,0:T(2,128)S(1)}, s32[1,1,32,2]{2,3,1,0:T(2,128)}, u32[]{:S(2)}) copy-start(s32[1,1,32,2]{2,3,1,0:T(2,128)} %param.12) | copy-start | bytes 772
  204.9 18.5 %copy-start = (bf16[512,512]{1,0:T(8,128)(2,1)S(1)}, bf16[512,512]{1,0:T(8,128)(2,1)}, u32[]{:S(2)}) copy-start(bf16[512,512]{1,0:T(8,128)(2,1)} %weight_ref.1) | copy-start | bytes 1572868
  205.9 55.3 %all-to-all-start.2 = ((bf16[32,128,512]{2,1,0:T(8,128)(2,1)}), bf16[32,128,512]{2,1,0:T(8,128)(2,1)}, u32[]{:S(2)}, u32[]{:S(2)}) async-start(bf16[32,128,512]{2,1,0:T(8,128)(2,1)} %bitcast.36), calls=%async_computation.2 | async-start | bytes 8388608 | tf_op jit(solution)/shard_map/all_to_all | solution.py:498
  210.8 6.0 %collective-permute-start.17 = (bf16[64,512]{1,0:T(8,128)(2,1)S(1)}, bf16[64,512]{1,0:T(8,128)(2,1)S(1)}, u32[]{:S(2)}, u32[]{:S(2)}) collective-permute-start(bf16[64,512]{1,0:T(8,128)(2,1)S(1)} %add_add_fusion.refs_0_), channel_id=1, source_target_pairs={{0,1},{1,2},{2,3},{3,0},{4,5},{5,6},{6,7},{7,4},{8,9},{9,10},{10,1... | collective-permute-start | bytes 196616 | tf_op jit(solution)/shard_map/ppermute | solution.py:518
  212.5 6.6 %collective-permute-start.18 = (bf16[64,512]{1,0:T(8,128)(2,1)S(1)}, bf16[64,512]{1,0:T(8,128)(2,1)S(1)}, u32[]{:S(2)}, u32[]{:S(2)}) collective-permute-start(bf16[64,512]{1,0:T(8,128)(2,1)S(1)} %add_add_fusion.refs_0_), channel_id=1, source_target_pairs={{0,2},{1,3},{2,0},{3,1},{4,6},{5,7},{6,4},{7,5},{8,10},{9,11},{10,... | collective-permute-start | bytes 196616 | tf_op jit(solution)/shard_map/ppermute | solution.py:518
  215.8 3.5 %collective-permute-start.19 = (bf16[64,512]{1,0:T(8,128)(2,1)S(1)}, bf16[64,512]{1,0:T(8,128)(2,1)S(1)}, u32[]{:S(2)}, u32[]{:S(2)}) collective-permute-start(bf16[64,512]{1,0:T(8,128)(2,1)S(1)} %add_add_fusion.refs_0_), channel_id=1, source_target_pairs={{0,3},{1,0},{2,1},{3,2},{4,7},{5,4},{6,5},{7,6},{8,11},{9,8},{10,9... | collective-permute-start | bytes 196616 | tf_op jit(solution)/shard_map/ppermute | solution.py:518
  216.8 2.5 copy-start.8
  221.6 23.7 %collective-permute-start.20 = (bf16[256,512]{1,0:T(8,128)(2,1)}, bf16[256,512]{1,0:T(8,128)(2,1)S(1)}, u32[]{:S(2)}, u32[]{:S(2)}) collective-permute-start(bf16[256,512]{1,0:T(8,128)(2,1)} %put_parts.1.mine_ref), channel_id=1, source_target_pairs={{0,4},{1,5},{2,6},{3,7},{4,0},{5,1},{6,2},{7,3},{8,12},{9,13},{10,... | collective-permute-start | bytes 786440 | tf_op jit(solution)/shard_map/ppermute | solution.py:518
  (5 other events, 3.4 us)

commit v4 on v3

--- a/solution.py
+++ b/solution.py
@@ -148,8 +148,8 @@
         ],
         compiler_params=params(),
         cost_estimate=pl.CostEstimate(
-            flops=2 * band.size * features,
-            bytes_accessed=2 * band.size + 6 * v.size,
+            flops=17 * 2 * band.size * features,
+            bytes_accessed=17 * (2 * band.size + 6 * v.size),
             transcendentals=0,
         ),
         name="band_sum",
@@ -591,15 +591,16 @@
     part = scatter_sum(dot_ta(y, grads), core, cell)
     terms = back_terms(1, cap, target_index, grads, vals)
     part, terms = lax.optimization_barrier((part, terms))
-    for kind in ("x", "y"):
-        sent = part.astype(jnp.bfloat16)
-        part = part + sum(shift(sent, kind, s).astype(jnp.float32) for s in (1, 2, 3))
+    sent = part.astype(jnp.bfloat16)
+    part = part + sum(shift(sent, "x", s).astype(jnp.float32) for s in (1, 2, 3))
     terms, so_far, part, low, high, grads = lax.optimization_barrier(
         (terms, so_far, part, low, high, grads)
     )
 
     came_back = exchange(terms)
     so_far = sum_back(0, cap, send_index, count, so_far, band_sum(grads, band), low, high)
+    sent = part.astype(jnp.bfloat16)
+    part = part + sum(shift(sent, "y", s).astype(jnp.float32) for s in (1, 2, 3))
     sent = part.astype(jnp.bfloat16)
     grad_weight = gather_sum([sent] + [within(sent, 0, s) for s in (1, 2, 3)], core, cell)
     came_back, so_far, grad_weight = lax.optimization_barrier((came_back, so_far, grad_weight))

time: 271 us -> 271 us (level)
  transfers between devices with their start and end apart: 24 -> 24, of which waited for: 10 -> 8; matrix products, arithmetic and copies ran while one was open for 3% -> 3% of each run, Pallas kernels for 19% -> 19%
where the time goes in v4:
time: 271 us; the launch traced here: 268 us
  waiting for transfers between devices  121 us (45%)
  Pallas kernels  73.2 us (27%)
  starting transfers between devices  62 us (23%)
  local copies, waits for them, and re-layouts  5.49 us (2%)
  matrix products  3.49 us (1%)
    ppermute x2, waiting for transfers between devices, to_neighbours(): lax.ppermute(high, 'genome', forward)  76.9 us
    pallas_call x2, Pallas kernels, band_sum(): pl.pallas_call(band_kernel, grid=(band.shape[0],), in_specs=[pl.BlockSpec...  26.7 us
    all_to_all x3, starting transfers between devices, exchange(): return lax.all_to_all(cut, 'genome', 0, 0, tiled=True).reshape(blocks.shape)  23.8 us
    ppermute x6, waiting for transfers between devices, shift(): lax.ppermute(v, 'genome', [(i, moved(i, kind, s)) for i in range(32)])  21.4 us
    ppermute x11, starting transfers between devices, within(): return lax.ppermute(v, ('genome', 'cell'), pairs)  17.6 us
    all_to_all x3, waiting for transfers between devices, exchange(): return lax.all_to_all(cut, 'genome', 0, 0, tiled=True).reshape(blocks.shape)  15.4 us
    pallas_call x1, Pallas kernels, middle(): pl.pallas_call(functools.partial(middle_kernel, cap), in_specs=[SMEM] + [...  11.7 us
    ppermute x6, starting transfers between devices, shift(): lax.ppermute(v, 'genome', [(i, moved(i, kind, s)) for i in range(32)])  8.81 us
  transfers between devices with their start and end apart: 24, of which 8 were waited for; matrix products, arithmetic and copies ran while one was open for 3% of the time, Pallas kernels for 19%

profile of v4, /device:TPU:1, one launch (start us, length us, event | category | flops | bytes accessed | tf_op | source)
XLA Modules:
  0.0 268.0 jit_solution(3430127879263561480)
XLA Ops:
  0.6 4.8 %gather_blocks.1 = bf16[8192,512]{1,0:T(8,128)(2,1)} custom-call(s32[2,32]{1,0:T(2,128)} %bitcast.46, s32[1,32]{1,0:T(1,128)} %bitcast.43, bf16[2048,512]{1,0:T(8,128)(2,1)} %bitcast.34), custom_call_target="tpu_custom_call" | custom-call | bytes 10485760 | tf_op jit(solution)/shard_map/gather_blocks/pallas_call | solution.py:87
  5.4 8.7 %all-to-all-start = ((bf16[32,256,512]{2,1,0:T(8,128)(2,1)}), bf16[32,256,512]{2,1,0:T(8,128)(2,1)}, u32[]{:S(2)}, u32[]{:S(2)}) async-start(bf16[32,256,512]{2,1,0:T(8,128)(2,1)} %bitcast.32), calls=%async_computation | async-start | bytes 16777216 | tf_op jit(solution)/shard_map/all_to_all | solution.py:498
  14.1 3.8 %rim_terms.2 = (bf16[512,512]{1,0:T(8,128)(2,1)}, bf16[512,512]{1,0:T(8,128)(2,1)}) custom-call(bf16[2048,512]{1,0:T(8,128)(2,1)} %bitcast.35, bf16[16,9,128,128]{3,2,1,0:T(8,128)(2,1)} %bitcast.26, bf16[16,9,128,128]{3,2,1,0:T(8,128)(2,1)} %bitcast.27), custom_call_target="tpu_custom_call" | custom-call | flops 335544320 | bytes 6291456 | tf_op jit(solution)/shard_map/rim_terms/pallas_call | solution.py:176
  17.9 3.5 %collective-permute-start = (bf16[512,512]{1,0:T(8,128)(2,1)}, bf16[512,512]{1,0:T(8,128)(2,1)S(1)}, u32[]{:S(2)}, u32[]{:S(2)}) collective-permute-start(bf16[512,512]{1,0:T(8,128)(2,1)} %get-tuple-element.25), channel_id=1, source_target_pairs={{0,4},{4,8},{8,12},{12,16},{16,20},{20,24},{24,28},{28,32},{32,36}... | collective-permute-start | bytes 1572872 | tf_op jit(solution)/shard_map/ppermute | solution.py:198
  21.4 1.9 collective-permute-start.1
  23.4 13.4 %band_sum.2.band_ref = f32[2048,512]{1,0:T(8,128)} custom-call(bf16[2048,512]{1,0:T(8,128)(2,1)} %bitcast.36, bf16[16,9,128,128]{3,2,1,0:T(8,128)(2,1)} %bitcast.28), custom_call_target="tpu_custom_call" | custom-call | flops 41070624768 | bytes 187170816 | tf_op jit(solution)/shard_map/band_sum/pallas_call | solution.py:135
  37.5 76.9 %collective-permute-done.low_ref = bf16[512,512]{1,0:T(8,128)(2,1)S(1)} collective-permute-done((bf16[512,512]{1,0:T(8,128)(2,1)}, bf16[512,512]{1,0:T(8,128)(2,1)S(1)}, u32[]{:S(2)}, u32[]{:S(2)}) %collective-permute-start) | collective-permute-done | bytes 524320 | tf_op jit(solution)/shard_map/ppermute | solution.py:198
  114.3 4.9 %collective-permute-done.1.high_ref = bf16[512,512]{1,0:T(8,128)(2,1)S(1)} collective-permute-done((bf16[512,512]{1,0:T(8,128)(2,1)}, bf16[512,512]{1,0:T(8,128)(2,1)S(1)}, u32[]{:S(2)}, u32[]{:S(2)}) %collective-permute-start.1) | collective-permute-done | bytes 524320 | tf_op jit(solution)/shard_map/ppermute | solution.py:198
  120.0 11.7 %middle.1 = (bf16[2048,512]{1,0:T(8,128)(2,1)}, bf16[2048,512]{1,0:T(8,128)(2,1)}, bf16[2048,512]{1,0:T(8,128)(2,1)}, bf16[4096,512]{1,0:T(8,128)(2,1)}) custom-call(s32[64]{0:T(128)} %reshape.36.target_ref, bf16[8192,512]{1,0:T(8,128)(2,1)} %bitcast.5.arrived_ref, bf16[64,128,128]{2,1,0:T(8,128)(2,1)} %bitcast.37, f32[2048,512]{1,0:T(8,128)} %band_sum.2.band_ref, ...), custom_call_target="tpu_custom_call" | custom-call | flops 3221225472 | bytes 31457280 | tf_op jit(solution)/shard_map/middle/pallas_call | solution.py:317
  131.7 10.1 %all-to-all-start.1 = ((bf16[32,128,512]{2,1,0:T(8,128)(2,1)}), bf16[32,128,512]{2,1,0:T(8,128)(2,1)}, u32[]{:S(2)}, u32[]{:S(2)}) async-start(bf16[32,128,512]{2,1,0:T(8,128)(2,1)} %bitcast.39), calls=%async_computation.1 | async-start | bytes 8388608 | tf_op jit(solution)/shard_map/all_to_all | solution.py:498
  141.9 3.8 %rim_terms.3 = (bf16[512,512]{1,0:T(8,128)(2,1)}, bf16[512,512]{1,0:T(8,128)(2,1)}) custom-call(bf16[2048,512]{1,0:T(8,128)(2,1)} %get-tuple-element.40.v_ref.grads_ref, bf16[16,9,128,128]{3,2,1,0:T(8,128)(2,1)} %bitcast.29, bf16[16,9,128,128]{3,2,1,0:T(8,128)(2,1)} %bitcast.30), custom_call_target="tpu_custom_call" | custom-call | flops 335544320 | bytes 6291456 | tf_op jit(solution)/shard_map/rim_terms/pallas_call | solution.py:176
  145.7 3.5 %fusion = f32[512,512]{1,0:T(8,128)S(1)} fusion(bf16[2048,512]{1,0:T(8,128)(2,1)} %get-tuple-element.32, bf16[2048,512]{1,0:T(8,128)(2,1)} %get-tuple-element.40.v_ref.grads_ref), kind=kOutput, calls=%fused_computation.10 | convolution fusion | flops 1073741824 | bytes 5242880 | tf_op jit(solution)/shard_map/dot_general | solution.py:32
  151.7 3.3 %collective-permute-start.3 = (f32[64,512]{1,0:T(8,128)S(1)}, f32[64,512]{1,0:T(8,128)}, u32[]{:S(2)}, u32[]{:S(2)}) collective-permute-start(f32[64,512]{1,0:T(8,128)S(1)} %get-tuple-element.53), channel_id=1, source_target_pairs={{0,2},{1,3},{2,0},{3,1},{4,6},{5,7},{6,4},{7,5},{8,10},{9,11},{10,... | collective-permute-start | bytes 393224 | tf_op jit(solution)/shard_map/ppermute | solution.py:518
  157.6 2.0 collective-permute-start.7
  159.6 1.7 collective-permute-done.3
  162.0 5.4 %back_terms.1 = bf16[4096,512]{1,0:T(8,128)(2,1)} custom-call(s32[64]{0:T(128)} %reshape.36.target_ref, bf16[2048,512]{1,0:T(8,128)(2,1)} %get-tuple-element.40.v_ref.grads_ref, bf16[64,128,128]{2,1,0:T(8,128)(2,1)} %bitcast.38), custom_call_target="tpu_custom_call" | custom-call | flops 536870912 | bytes 8388608 | tf_op jit(solution)/shard_map/back_terms/pallas_call | solution.py:348
  167.4 4.4 %collective-permute-start.12 = (bf16[512,512]{1,0:T(8,128)(2,1)}, bf16[512,512]{1,0:T(8,128)(2,1)S(1)}, u32[]{:S(2)}, u32[]{:S(2)}) collective-permute-start(bf16[512,512]{1,0:T(8,128)(2,1)} %get-tuple-element.36), channel_id=1, source_target_pairs={{0,4},{4,8},{8,12},{12,16},{16,20},{20,24},{24,28},{28,32},{32,36}... | collective-permute-start | bytes 1572872 | tf_op jit(solution)/shard_map/ppermute | solution.py:198
  171.8 1.9 collective-permute-start.13
  175.1 2.5 collective-permute-start.10
  179.1 21.4 %collective-permute-done.10 = bf16[64,512]{1,0:T(8,128)(2,1)S(1)} collective-permute-done((bf16[64,512]{1,0:T(8,128)(2,1)S(1)}, bf16[64,512]{1,0:T(8,128)(2,1)S(1)}, u32[]{:S(2)}, u32[]{:S(2)}) %collective-permute-start.10) | collective-permute-done | bytes 65568 | tf_op jit(solution)/shard_map/ppermute | solution.py:511
  200.6 2.2 collective-permute-start.14
  202.8 2.0 collective-permute-start.15
  205.5 5.0 %all-to-all-start.2 = ((bf16[32,128,512]{2,1,0:T(8,128)(2,1)}), bf16[32,128,512]{2,1,0:T(8,128)(2,1)}, u32[]{:S(2)}, u32[]{:S(2)}) async-start(bf16[32,128,512]{2,1,0:T(8,128)(2,1)} %bitcast.33), calls=%async_computation.2 | async-start | bytes 8388608 | tf_op jit(solution)/shard_map/all_to_all | solution.py:498
  210.6 1.7 collective-permute-start.17
  212.3 3.3 %collective-permute-start.18 = (bf16[64,512]{1,0:T(8,128)(2,1)S(1)}, bf16[64,512]{1,0:T(8,128)(2,1)S(1)}, u32[]{:S(2)}, u32[]{:S(2)}) collective-permute-start(bf16[64,512]{1,0:T(8,128)(2,1)S(1)} %add_convert_fusion.refs_0_), channel_id=1, source_target_pairs={{0,2},{1,3},{2,0},{3,1},{4,6},{5,7},{6,4},{7,5},{8,10},{9,11},{10,... | collective-permute-start | bytes 196616 | tf_op jit(solution)/shard_map/ppermute | solution.py:518
  219.7 1.7 put_parts.1.mine_ref
  221.4 1.7 collective-permute-start.20
  223.1 13.4 %band_sum.3.band_ref = f32[2048,512]{1,0:T(8,128)} custom-call(bf16[2048,512]{1,0:T(8,128)(2,1)} %get-tuple-element.40.v_ref.grads_ref, bf16[16,9,128,128]{3,2,1,0:T(8,128)(2,1)} %bitcast.31), custom_call_target="tpu_custom_call" | custom-call | flops 41070624768 | bytes 187170816 | tf_op jit(solution)/shard_map/band_sum/pallas_call | solution.py:135
  236.5 6.8 %sum_back.1.sum_ref = f32[2048,512]{1,0:T(8,128)} custom-call(s32[64]{0:T(128)} %reshape.40.index_ref, s32[32]{0:T(128)} %bitcast.44, bf16[4096,512]{1,0:T(8,128)(2,1)} %bitcast.12.back_ref, f32[2048,512]{1,0:T(8,128)} %band_sum.3.band_ref, bf16[512,512]{1,0:T(8,128)(2,1)} %copy-done.1, bf16[512,512]{1,0:T(8,128)(2,1)} %copy-done.2), custom_call_target="tpu_custom_call" | custom-call | flops 1048576 | bytes 12582912 | tf_op jit(solution)/shard_map/sum_back/pallas_call | solution.py:419
  244.0 2.1 join_halves.1
  246.1 15.4 %all-to-all-done.2 = bf16[32,128,512]{2,1,0:T(8,128)(2,1)} async-done(((bf16[32,128,512]{2,1,0:T(8,128)(2,1)}), bf16[32,128,512]{2,1,0:T(8,128)(2,1)}, u32[]{:S(2)}, u32[]{:S(2)}) %all-to-all-start.2) | async-done | bytes 4194336 | tf_op jit(solution)/shard_map/all_to_all | solution.py:498
  261.5 6.4 %tail.1 = bf16[2048,512]{1,0:T(8,128)(2,1)} custom-call(s32[64]{0:T(128)} %reshape.40.index_ref, s32[32]{0:T(128)} %bitcast.45, bf16[4096,512]{1,0:T(8,128)(2,1)} %bitcast.14.back_ref, f32[2048,512]{1,0:T(8,128)} %sum_back.1.sum_ref, bf16[512,512]{1,0:T(8,128)(2,1)} %bitcast.40), custom_call_target="tpu_custom_call" | custom-call | flops 1073741824 | bytes 10485760 | tf_op jit(solution)/shard_map/tail/pallas_call | solution.py:473
  (63 shorter events, 15.7 us)
Async XLA Ops:
  5.4 113.8 %all-to-all-start = ((bf16[32,256,512]{2,1,0:T(8,128)(2,1)}), bf16[32,256,512]{2,1,0:T(8,128)(2,1)}, u32[]{:S(2)}, u32[]{:S(2)}) async-start(bf16[32,256,512]{2,1,0:T(8,128)(2,1)} %bitcast.32), calls=%async_computation | async-start | bytes 16777216 | tf_op jit(solution)/shard_map/all_to_all | solution.py:498
  17.9 96.5 %collective-permute-start = (bf16[512,512]{1,0:T(8,128)(2,1)}, bf16[512,512]{1,0:T(8,128)(2,1)S(1)}, u32[]{:S(2)}, u32[]{:S(2)}) collective-permute-start(bf16[512,512]{1,0:T(8,128)(2,1)} %get-tuple-element.25), channel_id=1, source_target_pairs={{0,4},{4,8},{8,12},{12,16},{16,20},{20,24},{24,28},{28,32},{32,36}... | collective-permute-start | bytes 1572872 | tf_op jit(solution)/shard_map/ppermute | solution.py:198
  21.4 15.3 %copy-start.11 = (s32[1,1,32,2]{2,3,1,0:T(2,128)S(1)}, s32[1,1,32,2]{2,3,1,0:T(2,128)}, u32[]{:S(2)}) copy-start(s32[1,1,32,2]{2,3,1,0:T(2,128)} %param.11) | copy-start | bytes 772
  21.4 97.8 %collective-permute-start.1 = (bf16[512,512]{1,0:T(8,128)(2,1)}, bf16[512,512]{1,0:T(8,128)(2,1)S(1)}, u32[]{:S(2)}, u32[]{:S(2)}) collective-permute-start(bf16[512,512]{1,0:T(8,128)(2,1)} %get-tuple-element.26), channel_id=1, source_target_pairs={{4,0},{8,4},{12,8},{16,12},{20,16},{24,20},{28,24},{32,28},{36,32}... | collective-permute-start | bytes 1572872 | tf_op jit(solution)/shard_map/ppermute | solution.py:198
  114.3 4.9 %copy-start.3 = (bf16[512,512]{1,0:T(8,128)(2,1)}, bf16[512,512]{1,0:T(8,128)(2,1)S(1)}, u32[]{:S(2)}) copy-start(bf16[512,512]{1,0:T(8,128)(2,1)S(1)} %collective-permute-done.low_ref) | copy-start | bytes 1572868
  131.7 68.8 %all-to-all-start.1 = ((bf16[32,128,512]{2,1,0:T(8,128)(2,1)}), bf16[32,128,512]{2,1,0:T(8,128)(2,1)}, u32[]{:S(2)}, u32[]{:S(2)}) async-start(bf16[32,128,512]{2,1,0:T(8,128)(2,1)} %bitcast.39), calls=%async_computation.1 | async-start | bytes 8388608 | tf_op jit(solution)/shard_map/all_to_all | solution.py:498
  150.1 7.5 %collective-permute-start.2 = (f32[64,512]{1,0:T(8,128)S(1)}, f32[64,512]{1,0:T(8,128)}, u32[]{:S(2)}, u32[]{:S(2)}) collective-permute-start(f32[64,512]{1,0:T(8,128)S(1)} %get-tuple-element.47), channel_id=1, source_target_pairs={{0,1},{1,2},{2,3},{3,0},{4,5},{5,6},{6,7},{7,4},{8,9},{9,10},{10,1... | collective-permute-start | bytes 393224 | tf_op jit(solution)/shard_map/ppermute | solution.py:518
  151.7 9.5 %collective-permute-start.3 = (f32[64,512]{1,0:T(8,128)S(1)}, f32[64,512]{1,0:T(8,128)}, u32[]{:S(2)}, u32[]{:S(2)}) collective-permute-start(f32[64,512]{1,0:T(8,128)S(1)} %get-tuple-element.53), channel_id=1, source_target_pairs={{0,2},{1,3},{2,0},{3,1},{4,6},{5,7},{6,4},{7,5},{8,10},{9,11},{10,... | collective-permute-start | bytes 393224 | tf_op jit(solution)/shard_map/ppermute | solution.py:518
  155.0 12.3 %collective-permute-start.4 = (f32[64,512]{1,0:T(8,128)S(1)}, f32[64,512]{1,0:T(8,128)}, u32[]{:S(2)}, u32[]{:S(2)}) collective-permute-start(f32[64,512]{1,0:T(8,128)S(1)} %get-tuple-element.52), channel_id=1, source_target_pairs={{0,3},{1,0},{2,1},{3,2},{4,7},{5,4},{6,5},{7,6},{8,11},{9,8},{10,9... | collective-permute-start | bytes 393224 | tf_op jit(solution)/shard_map/ppermute | solution.py:518
  155.8 16.0 %collective-permute-start.5 = (f32[64,512]{1,0:T(8,128)}, f32[64,512]{1,0:T(8,128)}, u32[]{:S(2)}, u32[]{:S(2)}) collective-permute-start(f32[64,512]{1,0:T(8,128)} %get-tuple-element.51), channel_id=1, source_target_pairs={{0,4},{1,5},{2,6},{3,7},{4,0},{5,1},{6,2},{7,3},{8,12},{9,13},{10,... | collective-permute-start | bytes 393224 | tf_op jit(solution)/shard_map/ppermute | solution.py:518
  156.9 16.8 %collective-permute-start.6 = (f32[64,512]{1,0:T(8,128)}, f32[64,512]{1,0:T(8,128)}, u32[]{:S(2)}, u32[]{:S(2)}) collective-permute-start(f32[64,512]{1,0:T(8,128)} %get-tuple-element.50), channel_id=1, source_target_pairs={{0,5},{1,6},{2,7},{3,4},{4,1},{5,2},{6,3},{7,0},{8,13},{9,14},{10,... | collective-permute-start | bytes 393224 | tf_op jit(solution)/shard_map/ppermute | solution.py:518
  157.6 16.1 %collective-permute-start.7 = (f32[64,512]{1,0:T(8,128)}, f32[64,512]{1,0:T(8,128)}, u32[]{:S(2)}, u32[]{:S(2)}) collective-permute-start(f32[64,512]{1,0:T(8,128)} %get-tuple-element.49), channel_id=1, source_target_pairs={{0,6},{1,7},{2,4},{3,5},{4,2},{5,3},{6,0},{7,1},{8,14},{9,15},{10,... | collective-permute-start | bytes 393224 | tf_op jit(solution)/shard_map/ppermute | solution.py:518
  161.3 12.5 %collective-permute-start.8 = (f32[64,512]{1,0:T(8,128)}, f32[64,512]{1,0:T(8,128)}, u32[]{:S(2)}, u32[]{:S(2)}) collective-permute-start(f32[64,512]{1,0:T(8,128)} %get-tuple-element.48), channel_id=1, source_target_pairs={{0,7},{1,4},{2,5},{3,6},{4,3},{5,0},{6,1},{7,2},{8,15},{9,12},{10,... | collective-permute-start | bytes 393224 | tf_op jit(solution)/shard_map/ppermute | solution.py:518
  167.4 33.1 %collective-permute-start.12 = (bf16[512,512]{1,0:T(8,128)(2,1)}, bf16[512,512]{1,0:T(8,128)(2,1)S(1)}, u32[]{:S(2)}, u32[]{:S(2)}) collective-permute-start(bf16[512,512]{1,0:T(8,128)(2,1)} %get-tuple-element.36), channel_id=1, source_target_pairs={{0,4},{4,8},{8,12},{12,16},{16,20},{20,24},{24,28},{28,32},{32,36}... | collective-permute-start | bytes 1572872 | tf_op jit(solution)/shard_map/ppermute | solution.py:198
  171.8 28.7 %collective-permute-start.13 = (bf16[512,512]{1,0:T(8,128)(2,1)}, bf16[512,512]{1,0:T(8,128)(2,1)S(1)}, u32[]{:S(2)}, u32[]{:S(2)}) collective-permute-start(bf16[512,512]{1,0:T(8,128)(2,1)} %get-tuple-element.37), channel_id=1, source_target_pairs={{4,0},{8,4},{12,8},{16,12},{20,16},{24,20},{28,24},{32,28},{36,32}... | collective-permute-start | bytes 1572872 | tf_op jit(solution)/shard_map/ppermute | solution.py:198
  175.1 25.4 %collective-permute-start.10 = (bf16[64,512]{1,0:T(8,128)(2,1)S(1)}, bf16[64,512]{1,0:T(8,128)(2,1)S(1)}, u32[]{:S(2)}, u32[]{:S(2)}) collective-permute-start(bf16[64,512]{1,0:T(8,128)(2,1)S(1)} %convert_element_type.27), channel_id=1, source_target_pairs={{0,16},{4,20},{8,24},{12,28},{16,0},{20,4},{24,8},{28,12},{32,48},... | collective-permute-start | bytes 196616 | tf_op jit(solution)/shard_map/ppermute | solution.py:511
  177.6 22.9 %collective-permute-start.11 = (bf16[64,512]{1,0:T(8,128)(2,1)S(1)}, bf16[64,512]{1,0:T(8,128)(2,1)S(1)}, u32[]{:S(2)}, u32[]{:S(2)}) collective-permute-start(bf16[64,512]{1,0:T(8,128)(2,1)S(1)} %convert_element_type.27), channel_id=1, source_target_pairs={{0,24},{4,28},{8,0},{12,4},{16,8},{20,12},{24,16},{28,20},{32,56},... | collective-permute-start | bytes 196616 | tf_op jit(solution)/shard_map/ppermute | solution.py:511
  178.8 21.7 %collective-permute-start.9 = (bf16[64,512]{1,0:T(8,128)(2,1)S(1)}, bf16[64,512]{1,0:T(8,128)(2,1)S(1)}, u32[]{:S(2)}, u32[]{:S(2)}) collective-permute-start(bf16[64,512]{1,0:T(8,128)(2,1)S(1)} %convert_element_type.27), channel_id=1, source_target_pairs={{0,8},{4,12},{8,16},{12,20},{16,24},{20,28},{24,0},{28,4},{32,40},... | collective-permute-start | bytes 196616 | tf_op jit(solution)/shard_map/ppermute | solution.py:511
  200.5 4.9 %copy-start.1 = (bf16[512,512]{1,0:T(8,128)(2,1)}, bf16[512,512]{1,0:T(8,128)(2,1)S(1)}, u32[]{:S(2)}) copy-start(bf16[512,512]{1,0:T(8,128)(2,1)S(1)} %collective-permute-done.12.low_ref) | copy-start | bytes 1572868
  200.5 4.9 %copy-start.2 = (bf16[512,512]{1,0:T(8,128)(2,1)}, bf16[512,512]{1,0:T(8,128)(2,1)S(1)}, u32[]{:S(2)}) copy-start(bf16[512,512]{1,0:T(8,128)(2,1)S(1)} %collective-permute-done.13.high_ref) | copy-start | bytes 1572868
  200.6 9.9 %collective-permute-start.14 = (bf16[64,512]{1,0:T(8,128)(2,1)S(1)}, bf16[64,512]{1,0:T(8,128)(2,1)S(1)}, u32[]{:S(2)}, u32[]{:S(2)}) collective-permute-start(bf16[64,512]{1,0:T(8,128)(2,1)S(1)} %convert_element_type.31), channel_id=1, source_target_pairs={{0,32},{4,36},{8,40},{12,44},{16,48},{20,52},{24,56},{28,60},{32,6... | collective-permute-start | bytes 196616 | tf_op jit(solution)/shard_map/ppermute | solution.py:511
  202.8 7.7 %collective-permute-start.15 = (bf16[64,512]{1,0:T(8,128)(2,1)S(1)}, bf16[64,512]{1,0:T(8,128)(2,1)S(1)}, u32[]{:S(2)}, u32[]{:S(2)}) collective-permute-start(bf16[64,512]{1,0:T(8,128)(2,1)S(1)} %convert_element_type.31), channel_id=1, source_target_pairs={{0,64},{4,68},{8,72},{12,76},{16,80},{20,84},{24,88},{28,92},{32,9... | collective-permute-start | bytes 196616 | tf_op jit(solution)/shard_map/ppermute | solution.py:511
  204.8 5.7 %collective-permute-start.16 = (bf16[64,512]{1,0:T(8,128)(2,1)S(1)}, bf16[64,512]{1,0:T(8,128)(2,1)S(1)}, u32[]{:S(2)}, u32[]{:S(2)}) collective-permute-start(bf16[64,512]{1,0:T(8,128)(2,1)S(1)} %convert_element_type.31), channel_id=1, source_target_pairs={{0,96},{4,100},{8,104},{12,108},{16,112},{20,116},{24,120},{28,124... | collective-permute-start | bytes 196616 | tf_op jit(solution)/shard_map/ppermute | solution.py:511
  205.5 10.9 %copy-start.10 = (s32[1,1,32,2]{2,3,1,0:T(2,128)S(1)}, s32[1,1,32,2]{2,3,1,0:T(2,128)}, u32[]{:S(2)}) copy-start(s32[1,1,32,2]{2,3,1,0:T(2,128)} %param.12) | copy-start | bytes 772
  205.5 11.0 %copy-start = (bf16[512,512]{1,0:T(8,128)(2,1)S(1)}, bf16[512,512]{1,0:T(8,128)(2,1)}, u32[]{:S(2)}) copy-start(bf16[512,512]{1,0:T(8,128)(2,1)} %weight_ref.1) | copy-start | bytes 1572868
  205.5 56.0 %all-to-all-start.2 = ((bf16[32,128,512]{2,1,0:T(8,128)(2,1)}), bf16[32,128,512]{2,1,0:T(8,128)(2,1)}, u32[]{:S(2)}, u32[]{:S(2)}) async-start(bf16[32,128,512]{2,1,0:T(8,128)(2,1)} %bitcast.33), calls=%async_computation.2 | async-start | bytes 8388608 | tf_op jit(solution)/shard_map/all_to_all | solution.py:498
  210.6 8.5 %copy-start.5 = (bf16[64,512]{1,0:T(8,128)(2,1)}, bf16[64,512]{1,0:T(8,128)(2,1)S(1)}, u32[]{:S(2)}) copy-start(bf16[64,512]{1,0:T(8,128)(2,1)S(1)} %add_convert_fusion.refs_0_) | copy-start | bytes 196612
  210.6 7.5 %collective-permute-start.17 = (bf16[64,512]{1,0:T(8,128)(2,1)S(1)}, bf16[64,512]{1,0:T(8,128)(2,1)S(1)}, u32[]{:S(2)}, u32[]{:S(2)}) collective-permute-start(bf16[64,512]{1,0:T(8,128)(2,1)S(1)} %add_convert_fusion.refs_0_), channel_id=1, source_target_pairs={{0,1},{1,2},{2,3},{3,0},{4,5},{5,6},{6,7},{7,4},{8,9},{9,10},{10,1... | collective-permute-start | bytes 196616 | tf_op jit(solution)/shard_map/ppermute | solution.py:518
  212.3 6.6 %collective-permute-start.18 = (bf16[64,512]{1,0:T(8,128)(2,1)S(1)}, bf16[64,512]{1,0:T(8,128)(2,1)S(1)}, u32[]{:S(2)}, u32[]{:S(2)}) collective-permute-start(bf16[64,512]{1,0:T(8,128)(2,1)S(1)} %add_convert_fusion.refs_0_), channel_id=1, source_target_pairs={{0,2},{1,3},{2,0},{3,1},{4,6},{5,7},{6,4},{7,5},{8,10},{9,11},{10,... | collective-permute-start | bytes 196616 | tf_op jit(solution)/shard_map/ppermute | solution.py:518
  215.6 3.5 %collective-permute-start.19 = (bf16[64,512]{1,0:T(8,128)(2,1)S(1)}, bf16[64,512]{1,0:T(8,128)(2,1)S(1)}, u32[]{:S(2)}, u32[]{:S(2)}) collective-permute-start(bf16[64,512]{1,0:T(8,128)(2,1)S(1)} %add_convert_fusion.refs_0_), channel_id=1, source_target_pairs={{0,3},{1,0},{2,1},{3,2},{4,7},{5,4},{6,5},{7,6},{8,11},{9,8},{10,9... | collective-permute-start | bytes 196616 | tf_op jit(solution)/shard_map/ppermute | solution.py:518
  218.1 1.0 copy-start.7
  221.4 21.9 %collective-permute-start.20 = (bf16[256,512]{1,0:T(8,128)(2,1)}, bf16[256,512]{1,0:T(8,128)(2,1)S(1)}, u32[]{:S(2)}, u32[]{:S(2)}) collective-permute-start(bf16[256,512]{1,0:T(8,128)(2,1)} %put_parts.1.mine_ref), channel_id=1, source_target_pairs={{0,4},{1,5},{2,6},{3,7},{4,0},{5,1},{6,2},{7,3},{8,12},{9,13},{10,... | collective-permute-start | bytes 786440 | tf_op jit(solution)/shard_map/ppermute | solution.py:518
  (4 other events, 2.8 us)

commit v5 on v4

--- a/solution.py
+++ b/solution.py
@@ -593,14 +593,13 @@
     part, terms = lax.optimization_barrier((part, terms))
     sent = part.astype(jnp.bfloat16)
     part = part + sum(shift(sent, "x", s).astype(jnp.float32) for s in (1, 2, 3))
-    terms, so_far, part, low, high, grads = lax.optimization_barrier(
-        (terms, so_far, part, low, high, grads)
-    )
+    terms, so_far, part, grads = lax.optimization_barrier((terms, so_far, part, grads))
 
     came_back = exchange(terms)
     so_far = sum_back(0, cap, send_index, count, so_far, band_sum(grads, band), low, high)
     sent = part.astype(jnp.bfloat16)
     part = part + sum(shift(sent, "y", s).astype(jnp.float32) for s in (1, 2, 3))
+    part, low, high = lax.optimization_barrier((part, low, high))
     sent = part.astype(jnp.bfloat16)
     grad_weight = gather_sum([sent] + [within(sent, 0, s) for s in (1, 2, 3)], core, cell)
     came_back, so_far, grad_weight = lax.optimization_barrier((came_back, so_far, grad_weight))

time: 271 us -> 265 us (0.978)
  waiting for transfers between devices: 121 us -> 114 us
    ppermute x6, waiting for transfers between devices: 21.4 us -> 14.4 us  [shift(): lax.ppermute(v, 'genome', [(i, moved(i, kind, s)) for i in range(32)])]
  transfers between devices with their start and end apart: 24 -> 24, of which waited for: 8 -> 7; matrix products, arithmetic and copies ran while one was open for 3% -> 3% of each run, Pallas kernels for 19% -> 19%
where the time goes in v5:
time: 265 us; the launch traced here: 262 us
  waiting for transfers between devices  114 us (43%)
  Pallas kernels  73.1 us (28%)
  starting transfers between devices  63.2 us (24%)
  local copies, waits for them, and re-layouts  6.05 us (2%)
  matrix products  3.49 us (1%)
    ppermute x2, waiting for transfers between devices, to_neighbours(): lax.ppermute(high, 'genome', forward)  76.9 us
    pallas_call x2, Pallas kernels, band_sum(): pl.pallas_call(band_kernel, grid=(band.shape[0],), in_specs=[pl.BlockSpec...  26.7 us
    all_to_all x3, starting transfers between devices, exchange(): return lax.all_to_all(cut, 'genome', 0, 0, tiled=True).reshape(blocks.shape)  25.4 us
    ppermute x11, starting transfers between devices, within(): return lax.ppermute(v, ('genome', 'cell'), pairs)  17.2 us
    all_to_all x3, waiting for transfers between devices, exchange(): return lax.all_to_all(cut, 'genome', 0, 0, tiled=True).reshape(blocks.shape)  14.7 us
    ppermute x6, waiting for transfers between devices, shift(): lax.ppermute(v, 'genome', [(i, moved(i, kind, s)) for i in range(32)])  14.4 us
    pallas_call x1, Pallas kernels, middle(): pl.pallas_call(functools.partial(middle_kernel, cap), in_specs=[SMEM] + [...  11.7 us
    ppermute x6, starting transfers between devices, shift(): lax.ppermute(v, 'genome', [(i, moved(i, kind, s)) for i in range(32)])  8.91 us
  transfers between devices with their start and end apart: 24, of which 7 were waited for; matrix products, arithmetic and copies ran while one was open for 3% of the time, Pallas kernels for 19%

profile of v5, /device:TPU:1, one launch (start us, length us, event | category | flops | bytes accessed | tf_op | source)
XLA Modules:
  0.0 262.0 jit_solution(10817969831795144754)
XLA Ops:
  0.6 4.8 %gather_blocks.1 = bf16[8192,512]{1,0:T(8,128)(2,1)} custom-call(s32[2,32]{1,0:T(2,128)} %bitcast.46, s32[1,32]{1,0:T(1,128)} %bitcast.43, bf16[2048,512]{1,0:T(8,128)(2,1)} %bitcast.34), custom_call_target="tpu_custom_call" | custom-call | bytes 10485760 | tf_op jit(solution)/shard_map/gather_blocks/pallas_call | solution.py:87
  5.4 8.7 %all-to-all-start = ((bf16[32,256,512]{2,1,0:T(8,128)(2,1)}), bf16[32,256,512]{2,1,0:T(8,128)(2,1)}, u32[]{:S(2)}, u32[]{:S(2)}) async-start(bf16[32,256,512]{2,1,0:T(8,128)(2,1)} %bitcast.32), calls=%async_computation | async-start | bytes 16777216 | tf_op jit(solution)/shard_map/all_to_all | solution.py:498
  14.1 3.8 %rim_terms.2 = (bf16[512,512]{1,0:T(8,128)(2,1)}, bf16[512,512]{1,0:T(8,128)(2,1)}) custom-call(bf16[2048,512]{1,0:T(8,128)(2,1)} %bitcast.35, bf16[16,9,128,128]{3,2,1,0:T(8,128)(2,1)} %bitcast.26, bf16[16,9,128,128]{3,2,1,0:T(8,128)(2,1)} %bitcast.27), custom_call_target="tpu_custom_call" | custom-call | flops 335544320 | bytes 6291456 | tf_op jit(solution)/shard_map/rim_terms/pallas_call | solution.py:176
  17.9 3.5 %collective-permute-start = (bf16[512,512]{1,0:T(8,128)(2,1)}, bf16[512,512]{1,0:T(8,128)(2,1)S(1)}, u32[]{:S(2)}, u32[]{:S(2)}) collective-permute-start(bf16[512,512]{1,0:T(8,128)(2,1)} %get-tuple-element.24), channel_id=1, source_target_pairs={{0,4},{4,8},{8,12},{12,16},{16,20},{20,24},{24,28},{28,32},{32,36}... | collective-permute-start | bytes 1572872 | tf_op jit(solution)/shard_map/ppermute | solution.py:198
  21.4 1.9 collective-permute-start.1
  23.4 13.4 %band_sum.2.band_ref = f32[2048,512]{1,0:T(8,128)} custom-call(bf16[2048,512]{1,0:T(8,128)(2,1)} %bitcast.36, bf16[16,9,128,128]{3,2,1,0:T(8,128)(2,1)} %bitcast.28), custom_call_target="tpu_custom_call" | custom-call | flops 41070624768 | bytes 187170816 | tf_op jit(solution)/shard_map/band_sum/pallas_call | solution.py:135
  37.5 76.8 %collective-permute-done.low_ref = bf16[512,512]{1,0:T(8,128)(2,1)S(1)} collective-permute-done((bf16[512,512]{1,0:T(8,128)(2,1)}, bf16[512,512]{1,0:T(8,128)(2,1)S(1)}, u32[]{:S(2)}, u32[]{:S(2)}) %collective-permute-start) | collective-permute-done | bytes 524320 | tf_op jit(solution)/shard_map/ppermute | solution.py:198
  114.3 4.9 %collective-permute-done.1.high_ref = bf16[512,512]{1,0:T(8,128)(2,1)S(1)} collective-permute-done((bf16[512,512]{1,0:T(8,128)(2,1)}, bf16[512,512]{1,0:T(8,128)(2,1)S(1)}, u32[]{:S(2)}, u32[]{:S(2)}) %collective-permute-start.1) | collective-permute-done | bytes 524320 | tf_op jit(solution)/shard_map/ppermute | solution.py:198
  120.0 11.7 %middle.1 = (bf16[2048,512]{1,0:T(8,128)(2,1)}, bf16[2048,512]{1,0:T(8,128)(2,1)}, bf16[2048,512]{1,0:T(8,128)(2,1)}, bf16[4096,512]{1,0:T(8,128)(2,1)}) custom-call(s32[64]{0:T(128)} %reshape.36.target_ref, bf16[8192,512]{1,0:T(8,128)(2,1)} %bitcast.5.arrived_ref, bf16[64,128,128]{2,1,0:T(8,128)(2,1)} %bitcast.37, f32[2048,512]{1,0:T(8,128)} %band_sum.2.band_ref, ...), custom_call_target="tpu_custom_call" | custom-call | flops 3221225472 | bytes 31457280 | tf_op jit(solution)/shard_map/middle/pallas_call | solution.py:317
  131.7 10.1 %all-to-all-start.1 = ((bf16[32,128,512]{2,1,0:T(8,128)(2,1)}), bf16[32,128,512]{2,1,0:T(8,128)(2,1)}, u32[]{:S(2)}, u32[]{:S(2)}) async-start(bf16[32,128,512]{2,1,0:T(8,128)(2,1)} %bitcast.39), calls=%async_computation.1 | async-start | bytes 8388608 | tf_op jit(solution)/shard_map/all_to_all | solution.py:498
  141.9 3.8 %rim_terms.3 = (bf16[512,512]{1,0:T(8,128)(2,1)}, bf16[512,512]{1,0:T(8,128)(2,1)}) custom-call(bf16[2048,512]{1,0:T(8,128)(2,1)} %get-tuple-element.37.v_ref.grads_ref, bf16[16,9,128,128]{3,2,1,0:T(8,128)(2,1)} %bitcast.29, bf16[16,9,128,128]{3,2,1,0:T(8,128)(2,1)} %bitcast.30), custom_call_target="tpu_custom_call" | custom-call | flops 335544320 | bytes 6291456 | tf_op jit(solution)/shard_map/rim_terms/pallas_call | solution.py:176
  145.7 3.5 %fusion = f32[512,512]{1,0:T(8,128)S(1)} fusion(bf16[2048,512]{1,0:T(8,128)(2,1)} %get-tuple-element.31, bf16[2048,512]{1,0:T(8,128)(2,1)} %get-tuple-element.37.v_ref.grads_ref), kind=kOutput, calls=%fused_computation.10 | convolution fusion | flops 1073741824 | bytes 5242880 | tf_op jit(solution)/shard_map/dot_general | solution.py:32
  151.7 3.3 %collective-permute-start.3 = (f32[64,512]{1,0:T(8,128)S(1)}, f32[64,512]{1,0:T(8,128)S(1)}, u32[]{:S(2)}, u32[]{:S(2)}) collective-permute-start(f32[64,512]{1,0:T(8,128)S(1)} %get-tuple-element.51), channel_id=1, source_target_pairs={{0,2},{1,3},{2,0},{3,1},{4,6},{5,7},{6,4},{7,5},{8,10},{9,11},{10,... | collective-permute-start | bytes 393224 | tf_op jit(solution)/shard_map/ppermute | solution.py:518
  157.5 1.9 collective-permute-start.7
  159.4 1.8 collective-permute-done.3
  162.2 5.4 %back_terms.1 = bf16[4096,512]{1,0:T(8,128)(2,1)} custom-call(s32[64]{0:T(128)} %reshape.36.target_ref, bf16[2048,512]{1,0:T(8,128)(2,1)} %get-tuple-element.37.v_ref.grads_ref, bf16[64,128,128]{2,1,0:T(8,128)(2,1)} %bitcast.38), custom_call_target="tpu_custom_call" | custom-call | flops 536870912 | bytes 8388608 | tf_op jit(solution)/shard_map/back_terms/pallas_call | solution.py:348
  169.0 3.0 %collective-permute-start.10 = (bf16[64,512]{1,0:T(8,128)(2,1)S(1)}, bf16[64,512]{1,0:T(8,128)(2,1)S(1)}, u32[]{:S(2)}, u32[]{:S(2)}) collective-permute-start(bf16[64,512]{1,0:T(8,128)(2,1)S(1)} %convert_element_type.27), channel_id=1, source_target_pairs={{0,16},{4,20},{8,24},{12,28},{16,0},{20,4},{24,8},{28,12},{32,48},... | collective-permute-start | bytes 196616 | tf_op jit(solution)/shard_map/ppermute | solution.py:511
  173.4 4.4 %collective-permute-start.12 = (bf16[512,512]{1,0:T(8,128)(2,1)}, bf16[512,512]{1,0:T(8,128)(2,1)S(1)}, u32[]{:S(2)}, u32[]{:S(2)}) collective-permute-start(bf16[512,512]{1,0:T(8,128)(2,1)} %get-tuple-element.38), channel_id=1, source_target_pairs={{0,4},{4,8},{8,12},{12,16},{16,20},{20,24},{24,28},{28,32},{32,36}... | collective-permute-start | bytes 1572872 | tf_op jit(solution)/shard_map/ppermute | solution.py:198
  177.8 1.9 collective-permute-start.13
  179.7 14.3 %collective-permute-done.10 = bf16[64,512]{1,0:T(8,128)(2,1)S(1)} collective-permute-done((bf16[64,512]{1,0:T(8,128)(2,1)S(1)}, bf16[64,512]{1,0:T(8,128)(2,1)S(1)}, u32[]{:S(2)}, u32[]{:S(2)}) %collective-permute-start.10) | collective-permute-done | bytes 65568 | tf_op jit(solution)/shard_map/ppermute | solution.py:511
  194.2 1.8 collective-permute-start.14
  195.9 2.2 collective-permute-start.15
  198.6 6.6 %all-to-all-start.2 = ((bf16[32,128,512]{2,1,0:T(8,128)(2,1)}), bf16[32,128,512]{2,1,0:T(8,128)(2,1)}, u32[]{:S(2)}, u32[]{:S(2)}) async-start(bf16[32,128,512]{2,1,0:T(8,128)(2,1)} %bitcast.33), calls=%async_computation.2 | async-start | bytes 8388608 | tf_op jit(solution)/shard_map/all_to_all | solution.py:498
  205.3 1.7 collective-permute-start.17
  207.0 3.3 %collective-permute-start.18 = (bf16[64,512]{1,0:T(8,128)(2,1)S(1)}, bf16[64,512]{1,0:T(8,128)(2,1)S(1)}, u32[]{:S(2)}, u32[]{:S(2)}) collective-permute-start(bf16[64,512]{1,0:T(8,128)(2,1)S(1)} %add_add_fusion.refs_0_), channel_id=1, source_target_pairs={{0,2},{1,3},{2,0},{3,1},{4,6},{5,7},{6,4},{7,5},{8,10},{9,11},{10,... | collective-permute-start | bytes 196616 | tf_op jit(solution)/shard_map/ppermute | solution.py:518
  214.5 1.7 put_parts.1.mine_ref
  216.1 1.7 collective-permute-start.20
  217.9 13.4 %band_sum.3.band_ref = f32[2048,512]{1,0:T(8,128)} custom-call(bf16[2048,512]{1,0:T(8,128)(2,1)} %get-tuple-element.37.v_ref.grads_ref, bf16[16,9,128,128]{3,2,1,0:T(8,128)(2,1)} %bitcast.31), custom_call_target="tpu_custom_call" | custom-call | flops 41070624768 | bytes 187170816 | tf_op jit(solution)/shard_map/band_sum/pallas_call | solution.py:135
  231.2 6.8 %sum_back.1.sum_ref = f32[2048,512]{1,0:T(8,128)} custom-call(s32[64]{0:T(128)} %reshape.40.index_ref, s32[32]{0:T(128)} %bitcast.44, bf16[4096,512]{1,0:T(8,128)(2,1)} %bitcast.12.back_ref, f32[2048,512]{1,0:T(8,128)} %band_sum.3.band_ref, bf16[512,512]{1,0:T(8,128)(2,1)} %copy-done.1, bf16[512,512]{1,0:T(8,128)(2,1)} %copy-done.2), custom_call_target="tpu_custom_call" | custom-call | flops 1048576 | bytes 12582912 | tf_op jit(solution)/shard_map/sum_back/pallas_call | solution.py:419
  238.7 2.1 join_halves.1
  240.8 14.7 %all-to-all-done.2 = bf16[32,128,512]{2,1,0:T(8,128)(2,1)} async-done(((bf16[32,128,512]{2,1,0:T(8,128)(2,1)}), bf16[32,128,512]{2,1,0:T(8,128)(2,1)}, u32[]{:S(2)}, u32[]{:S(2)}) %all-to-all-start.2) | async-done | bytes 4194336 | tf_op jit(solution)/shard_map/all_to_all | solution.py:498
  255.5 6.4 %tail.1 = bf16[2048,512]{1,0:T(8,128)(2,1)} custom-call(s32[64]{0:T(128)} %reshape.40.index_ref, s32[32]{0:T(128)} %bitcast.45, bf16[4096,512]{1,0:T(8,128)(2,1)} %bitcast.14.back_ref, f32[2048,512]{1,0:T(8,128)} %sum_back.1.sum_ref, bf16[512,512]{1,0:T(8,128)(2,1)} %bitcast.40), custom_call_target="tpu_custom_call" | custom-call | flops 1073741824 | bytes 10485760 | tf_op jit(solution)/shard_map/tail/pallas_call | solution.py:473
  (65 shorter events, 15.8 us)
Async XLA Ops:
  5.4 113.8 %all-to-all-start = ((bf16[32,256,512]{2,1,0:T(8,128)(2,1)}), bf16[32,256,512]{2,1,0:T(8,128)(2,1)}, u32[]{:S(2)}, u32[]{:S(2)}) async-start(bf16[32,256,512]{2,1,0:T(8,128)(2,1)} %bitcast.32), calls=%async_computation | async-start | bytes 16777216 | tf_op jit(solution)/shard_map/all_to_all | solution.py:498
  17.9 96.5 %collective-permute-start = (bf16[512,512]{1,0:T(8,128)(2,1)}, bf16[512,512]{1,0:T(8,128)(2,1)S(1)}, u32[]{:S(2)}, u32[]{:S(2)}) collective-permute-start(bf16[512,512]{1,0:T(8,128)(2,1)} %get-tuple-element.24), channel_id=1, source_target_pairs={{0,4},{4,8},{8,12},{12,16},{16,20},{20,24},{24,28},{28,32},{32,36}... | collective-permute-start | bytes 1572872 | tf_op jit(solution)/shard_map/ppermute | solution.py:198
  21.4 15.3 %copy-start.12 = (s32[1,1,32,2]{2,3,1,0:T(2,128)S(1)}, s32[1,1,32,2]{2,3,1,0:T(2,128)}, u32[]{:S(2)}) copy-start(s32[1,1,32,2]{2,3,1,0:T(2,128)} %param.11) | copy-start | bytes 772
  21.4 97.8 %collective-permute-start.1 = (bf16[512,512]{1,0:T(8,128)(2,1)}, bf16[512,512]{1,0:T(8,128)(2,1)S(1)}, u32[]{:S(2)}, u32[]{:S(2)}) collective-permute-start(bf16[512,512]{1,0:T(8,128)(2,1)} %get-tuple-element.25), channel_id=1, source_target_pairs={{4,0},{8,4},{12,8},{16,12},{20,16},{24,20},{28,24},{32,28},{36,32}... | collective-permute-start | bytes 1572872 | tf_op jit(solution)/shard_map/ppermute | solution.py:198
  114.3 4.9 %copy-start.3 = (bf16[512,512]{1,0:T(8,128)(2,1)}, bf16[512,512]{1,0:T(8,128)(2,1)S(1)}, u32[]{:S(2)}) copy-start(bf16[512,512]{1,0:T(8,128)(2,1)S(1)} %collective-permute-done.low_ref) | copy-start | bytes 1572868
  131.7 62.4 %all-to-all-start.1 = ((bf16[32,128,512]{2,1,0:T(8,128)(2,1)}), bf16[32,128,512]{2,1,0:T(8,128)(2,1)}, u32[]{:S(2)}, u32[]{:S(2)}) async-start(bf16[32,128,512]{2,1,0:T(8,128)(2,1)} %bitcast.39), calls=%async_computation.1 | async-start | bytes 8388608 | tf_op jit(solution)/shard_map/all_to_all | solution.py:498
  150.0 7.5 %collective-permute-start.2 = (f32[64,512]{1,0:T(8,128)S(1)}, f32[64,512]{1,0:T(8,128)S(1)}, u32[]{:S(2)}, u32[]{:S(2)}) collective-permute-start(f32[64,512]{1,0:T(8,128)S(1)} %get-tuple-element.45), channel_id=1, source_target_pairs={{0,1},{1,2},{2,3},{3,0},{4,5},{5,6},{6,7},{7,4},{8,9},{9,10},{10,1... | collective-permute-start | bytes 393224 | tf_op jit(solution)/shard_map/ppermute | solution.py:518
  151.7 9.5 %collective-permute-start.3 = (f32[64,512]{1,0:T(8,128)S(1)}, f32[64,512]{1,0:T(8,128)S(1)}, u32[]{:S(2)}, u32[]{:S(2)}) collective-permute-start(f32[64,512]{1,0:T(8,128)S(1)} %get-tuple-element.51), channel_id=1, source_target_pairs={{0,2},{1,3},{2,0},{3,1},{4,6},{5,7},{6,4},{7,5},{8,10},{9,11},{10,... | collective-permute-start | bytes 393224 | tf_op jit(solution)/shard_map/ppermute | solution.py:518
  155.0 12.6 %collective-permute-start.4 = (f32[64,512]{1,0:T(8,128)}, f32[64,512]{1,0:T(8,128)}, u32[]{:S(2)}, u32[]{:S(2)}) collective-permute-start(f32[64,512]{1,0:T(8,128)} %get-tuple-element.50), channel_id=1, source_target_pairs={{0,3},{1,0},{2,1},{3,2},{4,7},{5,4},{6,5},{7,6},{8,11},{9,8},{10,9... | collective-permute-start | bytes 393224 | tf_op jit(solution)/shard_map/ppermute | solution.py:518
  155.7 11.9 %collective-permute-start.5 = (f32[64,512]{1,0:T(8,128)}, f32[64,512]{1,0:T(8,128)}, u32[]{:S(2)}, u32[]{:S(2)}) collective-permute-start(f32[64,512]{1,0:T(8,128)} %get-tuple-element.49), channel_id=1, source_target_pairs={{0,4},{1,5},{2,6},{3,7},{4,0},{5,1},{6,2},{7,3},{8,12},{9,13},{10,... | collective-permute-start | bytes 393224 | tf_op jit(solution)/shard_map/ppermute | solution.py:518
  156.9 10.8 %collective-permute-start.6 = (f32[64,512]{1,0:T(8,128)S(1)}, f32[64,512]{1,0:T(8,128)}, u32[]{:S(2)}, u32[]{:S(2)}) collective-permute-start(f32[64,512]{1,0:T(8,128)S(1)} %get-tuple-element.48), channel_id=1, source_target_pairs={{0,5},{1,6},{2,7},{3,4},{4,1},{5,2},{6,3},{7,0},{8,13},{9,14},{10,... | collective-permute-start | bytes 393224 | tf_op jit(solution)/shard_map/ppermute | solution.py:518
  157.5 10.1 %collective-permute-start.7 = (f32[64,512]{1,0:T(8,128)S(1)}, f32[64,512]{1,0:T(8,128)}, u32[]{:S(2)}, u32[]{:S(2)}) collective-permute-start(f32[64,512]{1,0:T(8,128)S(1)} %get-tuple-element.47), channel_id=1, source_target_pairs={{0,6},{1,7},{2,4},{3,5},{4,2},{5,3},{6,0},{7,1},{8,14},{9,15},{10,... | collective-permute-start | bytes 393224 | tf_op jit(solution)/shard_map/ppermute | solution.py:518
  161.9 5.8 %collective-permute-start.8 = (f32[64,512]{1,0:T(8,128)S(1)}, f32[64,512]{1,0:T(8,128)}, u32[]{:S(2)}, u32[]{:S(2)}) collective-permute-start(f32[64,512]{1,0:T(8,128)S(1)} %get-tuple-element.46), channel_id=1, source_target_pairs={{0,7},{1,4},{2,5},{3,6},{4,3},{5,0},{6,1},{7,2},{8,15},{9,12},{10,... | collective-permute-start | bytes 393224 | tf_op jit(solution)/shard_map/ppermute | solution.py:518
  169.0 25.1 %collective-permute-start.10 = (bf16[64,512]{1,0:T(8,128)(2,1)S(1)}, bf16[64,512]{1,0:T(8,128)(2,1)S(1)}, u32[]{:S(2)}, u32[]{:S(2)}) collective-permute-start(bf16[64,512]{1,0:T(8,128)(2,1)S(1)} %convert_element_type.27), channel_id=1, source_target_pairs={{0,16},{4,20},{8,24},{12,28},{16,0},{20,4},{24,8},{28,12},{32,48},... | collective-permute-start | bytes 196616 | tf_op jit(solution)/shard_map/ppermute | solution.py:511
  172.0 22.1 %collective-permute-start.11 = (bf16[64,512]{1,0:T(8,128)(2,1)S(1)}, bf16[64,512]{1,0:T(8,128)(2,1)S(1)}, u32[]{:S(2)}, u32[]{:S(2)}) collective-permute-start(bf16[64,512]{1,0:T(8,128)(2,1)S(1)} %convert_element_type.27), channel_id=1, source_target_pairs={{0,24},{4,28},{8,0},{12,4},{16,8},{20,12},{24,16},{28,20},{32,56},... | collective-permute-start | bytes 196616 | tf_op jit(solution)/shard_map/ppermute | solution.py:511
  172.9 21.2 %collective-permute-start.9 = (bf16[64,512]{1,0:T(8,128)(2,1)S(1)}, bf16[64,512]{1,0:T(8,128)(2,1)S(1)}, u32[]{:S(2)}, u32[]{:S(2)}) collective-permute-start(bf16[64,512]{1,0:T(8,128)(2,1)S(1)} %convert_element_type.27), channel_id=1, source_target_pairs={{0,8},{4,12},{8,16},{12,20},{16,24},{20,28},{24,0},{28,4},{32,40},... | collective-permute-start | bytes 196616 | tf_op jit(solution)/shard_map/ppermute | solution.py:511
  173.4 31.8 %collective-permute-start.12 = (bf16[512,512]{1,0:T(8,128)(2,1)}, bf16[512,512]{1,0:T(8,128)(2,1)S(1)}, u32[]{:S(2)}, u32[]{:S(2)}) collective-permute-start(bf16[512,512]{1,0:T(8,128)(2,1)} %get-tuple-element.38), channel_id=1, source_target_pairs={{0,4},{4,8},{8,12},{12,16},{16,20},{20,24},{24,28},{28,32},{32,36}... | collective-permute-start | bytes 1572872 | tf_op jit(solution)/shard_map/ppermute | solution.py:198
  177.8 27.5 %collective-permute-start.13 = (bf16[512,512]{1,0:T(8,128)(2,1)}, bf16[512,512]{1,0:T(8,128)(2,1)S(1)}, u32[]{:S(2)}, u32[]{:S(2)}) collective-permute-start(bf16[512,512]{1,0:T(8,128)(2,1)} %get-tuple-element.39), channel_id=1, source_target_pairs={{4,0},{8,4},{12,8},{16,12},{20,16},{24,20},{28,24},{32,28},{36,32}... | collective-permute-start | bytes 1572872 | tf_op jit(solution)/shard_map/ppermute | solution.py:198
  194.2 11.0 %collective-permute-start.14 = (bf16[64,512]{1,0:T(8,128)(2,1)S(1)}, bf16[64,512]{1,0:T(8,128)(2,1)S(1)}, u32[]{:S(2)}, u32[]{:S(2)}) collective-permute-start(bf16[64,512]{1,0:T(8,128)(2,1)S(1)} %convert_element_type.31), channel_id=1, source_target_pairs={{0,32},{4,36},{8,40},{12,44},{16,48},{20,52},{24,56},{28,60},{32,6... | collective-permute-start | bytes 196616 | tf_op jit(solution)/shard_map/ppermute | solution.py:511
  195.9 9.3 %collective-permute-start.15 = (bf16[64,512]{1,0:T(8,128)(2,1)S(1)}, bf16[64,512]{1,0:T(8,128)(2,1)S(1)}, u32[]{:S(2)}, u32[]{:S(2)}) collective-permute-start(bf16[64,512]{1,0:T(8,128)(2,1)S(1)} %convert_element_type.31), channel_id=1, source_target_pairs={{0,64},{4,68},{8,72},{12,76},{16,80},{20,84},{24,88},{28,92},{32,9... | collective-permute-start | bytes 196616 | tf_op jit(solution)/shard_map/ppermute | solution.py:511
  198.1 7.1 %collective-permute-start.16 = (bf16[64,512]{1,0:T(8,128)(2,1)S(1)}, bf16[64,512]{1,0:T(8,128)(2,1)S(1)}, u32[]{:S(2)}, u32[]{:S(2)}) collective-permute-start(bf16[64,512]{1,0:T(8,128)(2,1)S(1)} %convert_element_type.31), channel_id=1, source_target_pairs={{0,96},{4,100},{8,104},{12,108},{16,112},{20,116},{24,120},{28,124... | collective-permute-start | bytes 196616 | tf_op jit(solution)/shard_map/ppermute | solution.py:511
  198.6 12.4 %copy-start.11 = (s32[1,1,32,2]{2,3,1,0:T(2,128)S(1)}, s32[1,1,32,2]{2,3,1,0:T(2,128)}, u32[]{:S(2)}) copy-start(s32[1,1,32,2]{2,3,1,0:T(2,128)} %param.12) | copy-start | bytes 772
  198.6 12.5 %copy-start = (bf16[512,512]{1,0:T(8,128)(2,1)S(1)}, bf16[512,512]{1,0:T(8,128)(2,1)}, u32[]{:S(2)}) copy-start(bf16[512,512]{1,0:T(8,128)(2,1)} %weight_ref.1) | copy-start | bytes 1572868
  198.6 56.8 %all-to-all-start.2 = ((bf16[32,128,512]{2,1,0:T(8,128)(2,1)}), bf16[32,128,512]{2,1,0:T(8,128)(2,1)}, u32[]{:S(2)}, u32[]{:S(2)}) async-start(bf16[32,128,512]{2,1,0:T(8,128)(2,1)} %bitcast.33), calls=%async_computation.2 | async-start | bytes 8388608 | tf_op jit(solution)/shard_map/all_to_all | solution.py:498
  205.3 8.6 %copy-start.5 = (bf16[64,512]{1,0:T(8,128)(2,1)}, bf16[64,512]{1,0:T(8,128)(2,1)S(1)}, u32[]{:S(2)}) copy-start(bf16[64,512]{1,0:T(8,128)(2,1)S(1)} %add_add_fusion.refs_0_) | copy-start | bytes 196612
  205.3 25.9 %copy-start.1 = (bf16[512,512]{1,0:T(8,128)(2,1)}, bf16[512,512]{1,0:T(8,128)(2,1)S(1)}, u32[]{:S(2)}) copy-start(bf16[512,512]{1,0:T(8,128)(2,1)S(1)} %collective-permute-done.12.low_ref) | copy-start | bytes 1572868
  205.3 25.9 %copy-start.2 = (bf16[512,512]{1,0:T(8,128)(2,1)}, bf16[512,512]{1,0:T(8,128)(2,1)S(1)}, u32[]{:S(2)}) copy-start(bf16[512,512]{1,0:T(8,128)(2,1)S(1)} %collective-permute-done.13.high_ref) | copy-start | bytes 1572868
  205.3 7.5 %collective-permute-start.17 = (bf16[64,512]{1,0:T(8,128)(2,1)S(1)}, bf16[64,512]{1,0:T(8,128)(2,1)S(1)}, u32[]{:S(2)}, u32[]{:S(2)}) collective-permute-start(bf16[64,512]{1,0:T(8,128)(2,1)S(1)} %add_add_fusion.refs_0_), channel_id=1, source_target_pairs={{0,1},{1,2},{2,3},{3,0},{4,5},{5,6},{6,7},{7,4},{8,9},{9,10},{10,1... | collective-permute-start | bytes 196616 | tf_op jit(solution)/shard_map/ppermute | solution.py:518
  207.0 6.6 %collective-permute-start.18 = (bf16[64,512]{1,0:T(8,128)(2,1)S(1)}, bf16[64,512]{1,0:T(8,128)(2,1)S(1)}, u32[]{:S(2)}, u32[]{:S(2)}) collective-permute-start(bf16[64,512]{1,0:T(8,128)(2,1)S(1)} %add_add_fusion.refs_0_), channel_id=1, source_target_pairs={{0,2},{1,3},{2,0},{3,1},{4,6},{5,7},{6,4},{7,5},{8,10},{9,11},{10,... | collective-permute-start | bytes 196616 | tf_op jit(solution)/shard_map/ppermute | solution.py:518
  210.3 3.5 %collective-permute-start.19 = (bf16[64,512]{1,0:T(8,128)(2,1)S(1)}, bf16[64,512]{1,0:T(8,128)(2,1)S(1)}, u32[]{:S(2)}, u32[]{:S(2)}) collective-permute-start(bf16[64,512]{1,0:T(8,128)(2,1)S(1)} %add_add_fusion.refs_0_), channel_id=1, source_target_pairs={{0,3},{1,0},{2,1},{3,2},{4,7},{5,4},{6,5},{7,6},{8,11},{9,8},{10,9... | collective-permute-start | bytes 196616 | tf_op jit(solution)/shard_map/ppermute | solution.py:518
  212.8 1.1 copy-start.8
  216.1 21.9 %collective-permute-start.20 = (bf16[256,512]{1,0:T(8,128)(2,1)}, bf16[256,512]{1,0:T(8,128)(2,1)S(1)}, u32[]{:S(2)}, u32[]{:S(2)}) collective-permute-start(bf16[256,512]{1,0:T(8,128)(2,1)} %put_parts.1.mine_ref), channel_id=1, source_target_pairs={{0,4},{1,5},{2,6},{3,7},{4,0},{5,1},{6,2},{7,3},{8,12},{9,13},{10,... | collective-permute-start | bytes 786440 | tf_op jit(solution)/shard_map/ppermute | solution.py:518
  (5 other events, 3.4 us)
